TPU v7x, 32 devices: a whole 2x2x4 slice. The times are simulated.
32 devices in a mesh: dp: 8 (over y, x, core), tp: 4 (over z).
Axes of the slice: x: 2, y: 2, z: 4, core: 2. Of those that a mesh axis runs over, the one named last changes fastest.
Arguments:
- patches: bfloat16 [8192, 8192], P('dp', 'tp'), may hold values from -6 to 6
- keep_mask: int32 [8192], P(('dp', 'tp')), may hold values 0 or 1
- segments: int32 [8, 1024], P('dp'), may hold values from 0 to 3, as said below
- embed_weight: bfloat16 [8192, 1024], P('tp'), may hold values from -0.0625 to 0.0625
- first_gain: float32 [1024], replicated, may hold values from 0.1 to 1.9
- mamba_gate: bfloat16 [1024, 2048], P(None, 'tp'), may hold values from -0.1875 to 0.1875
- mamba_input: bfloat16 [1024, 2048], P(None, 'tp'), may hold values from -0.1875 to 0.1875
- state_in: bfloat16 [1024, 512], P(None, 'tp'), may hold values from -0.1875 to 0.1875
- state_out: bfloat16 [1024, 512], P(None, 'tp'), may hold values from -0.1875 to 0.1875
- step_weight: bfloat16 [1024, 32], P(None, 'tp'), may hold values from -0.1875 to 0.1875
- conv_input: float32 [4, 2048], P(None, 'tp'), may hold values from -3 to 3
- conv_statein: float32 [4, 512], P(None, 'tp'), may hold values from -3 to 3
- conv_stateout: float32 [4, 512], P(None, 'tp'), may hold values from -3 to 3
- step_bias: float32 [32], P('tp'), may hold values from -4 to -1
- rate_log: float32 [32], P('tp'), may hold values from -6 to 0
- skip_gain: float32 [32], P('tp'), may hold values from 0.5 to 1.5
- inner_gain: float32 [2048], P('tp'), may hold values from 0.1 to 1.9
- mamba_output: bfloat16 [2048, 1024], P('tp'), may hold values from -0.125 to 0.125
- query_weight: bfloat16 [1024, 1024], P(None, 'tp'), may hold values from -0.1875 to 0.1875
- key_weight: bfloat16 [1024, 1024], P(None, 'tp'), may hold values from -0.1875 to 0.1875
- value_weight: bfloat16 [1024, 1024], P(None, 'tp'), may hold values from -0.1875 to 0.1875
- attn_output: bfloat16 [1024, 1024], P('tp'), may hold values from -0.5 to 0.5
- second_gain: float32 [1024], replicated, may hold values from 0.1 to 1.9
- ffn_gate: bfloat16 [1024, 4096], P(None, 'tp'), may hold values from -0.1875 to 0.1875
- ffn_up: bfloat16 [1024, 4096], P(None, 'tp'), may hold values from -0.1875 to 0.1875
- ffn_down: bfloat16 [4096, 1024], P('tp'), may hold values from -0.09375 to 0.09375
- out_grad: bfloat16 [8192, 1024], P(('dp', 'tp')), may hold values from -6 to 6
Outputs:
- out: bfloat16 [8192, 1024], P(('dp', 'tp'))
- patches_grad: bfloat16 [8192, 8192], P('dp', 'tp')
- embed_weight_grad: float32 [8192, 1024], P('tp', 'dp')
- first_gain_grad: float32 [1024], P(('dp', 'tp'))
- mamba_gate_grad: float32 [1024, 2048], P('dp', 'tp')
- mamba_input_grad: float32 [1024, 2048], P('dp', 'tp')
- state_in_grad: float32 [1024, 512], P('dp', 'tp')
- state_out_grad: float32 [1024, 512], P('dp', 'tp')
- step_weight_grad: float32 [1024, 32], P('dp', 'tp')
- conv_input_grad: float32 [4, 2048], P(None, 'tp')
- conv_statein_grad: float32 [4, 512], P(None, 'tp')
- conv_stateout_grad: float32 [4, 512], P(None, 'tp')
- step_bias_grad: float32 [32], P('tp')
- rate_log_grad: float32 [32], P('tp')
- skip_gain_grad: float32 [32], P('tp')
- inner_gain_grad: float32 [2048], P('tp')
- mamba_output_grad: float32 [2048, 1024], P('tp', 'dp')
- query_weight_grad: float32 [1024, 1024], P('dp', 'tp')
- key_weight_grad: float32 [1024, 1024], P('dp', 'tp')
- value_weight_grad: float32 [1024, 1024], P('dp', 'tp')
- attn_output_grad: float32 [1024, 1024], P('tp', 'dp')
- second_gain_grad: float32 [1024], P(('dp', 'tp'))
- ffn_gate_grad: float32 [1024, 4096], P('dp', 'tp')
- ffn_up_grad: float32 [1024, 4096], P('dp', 'tp')
- ffn_down_grad: float32 [4096, 1024], P('tp', 'dp')
Inputs may be any that keep to these rules, and one draw needn't show every extreme that they name: `segments`: along each row the document numbers never fall and rise by one at a time; each row holds documents 0 to 3.
All inputs are finite; a program needn't handle non-finite values. No bound on the sum of `keep_mask` on one device may be relied on, other than what follows from the above.
Results may differ from a plain program's by a relative error of at most 0.0208.
Values may be sent and summed in bfloat16 or wider, within the bound.
A program may use at most 256 MiB of HBM per device.

v0:
```python
import jax
import jax.numpy as jnp
from jax import lax
from jax.sharding import PartitionSpec as P

NST = 128
AHDIM = 64


eps = 1e-05
exact_mode = lax.Precision.HIGHEST


def rms_scale(signal, gain):
    return signal * lax.rsqrt(jnp.mean(signal * signal, axis=-1, keepdims=True) + eps) * gain


def swiglu(gate_val, up_val):
    return jax.nn.silu(gate_val) * up_val


def shifted_rows(signal, lag_rows, segment):
    length = signal.shape[0]
    shifted = jnp.concatenate(
        [jnp.zeros((lag_rows, signal.shape[1]), signal.dtype), signal[: length - lag_rows]], axis=0
    )
    seg_shift = jnp.concatenate(
        [jnp.full((lag_rows,), -1, jnp.int32), segment[: length - lag_rows]]
    )
    return jnp.where((seg_shift == segment)[:, None], shifted, 0.0)


def causal_conv(signal, kernel, segment):
    output = signal * kernel[0]
    for lag_rows in range(1, kernel.shape[0]):
        output = output + shifted_rows(signal, lag_rows, segment) * kernel[lag_rows]
    return jax.nn.silu(output)


def visible(first_row, block_rows, segment):
    positions = jnp.arange(segment.shape[0], dtype=jnp.int32)
    row_pos = first_row + jnp.arange(block_rows, dtype=jnp.int32)
    row_seg = lax.dynamic_slice_in_dim(segment, first_row, block_rows, 0)
    return (row_pos[:, None] >= positions[None, :]) & (row_seg[:, None] == segment[None, :])


def mixer_core(
    gate_z,
    inner_x,
    state_b,
    state_c,
    step_raw,
    queries,
    key_rows,
    value_rows,
    conv_input,
    conv_statein,
    conv_stateout,
    step_bias,
    rate_log,
    skip_gain,
    inner_gain,
    segment,
):
    length = inner_x.shape[0]
    head_count = step_raw.shape[1]
    head_dim = inner_x.shape[1] // head_count
    groups = state_b.shape[1] // NST
    per_group = head_count // groups
    inner_width = inner_x.shape[1]
    block_rows = min(512, length)
    block_count = length // block_rows
    xconv = causal_conv(inner_x, conv_input, segment)
    bconv = causal_conv(state_b, conv_statein, segment)
    cconv = causal_conv(state_c, conv_stateout, segment)
    step_size = jax.nn.softplus(step_raw + step_bias)
    cum_log = jnp.cumsum(step_size * -jnp.exp(rate_log), axis=0)
    scaled_x = (xconv.reshape(length, head_count, head_dim) * step_size[:, :, None]).transpose(
        1, 0, 2
    )
    bgroup = bconv.reshape(length, groups, NST).transpose(1, 0, 2)
    cgroup = cconv.reshape(length, groups, NST).transpose(1, 0, 2)
    log_heads = cum_log.T

    def ssd_rows(block_index):
        first_row = block_index * block_rows
        rows_c = lax.dynamic_slice_in_dim(cgroup, first_row, block_rows, 1)
        inner_prod = jnp.einsum("gtn,gsn->gts", rows_c, bgroup, precision=exact_mode)
        inner_prod = jnp.repeat(inner_prod, per_group, axis=0)
        allowed = visible(first_row, block_rows, segment)[None]
        rows_log = lax.dynamic_slice_in_dim(log_heads, first_row, block_rows, 1)
        log_gap = rows_log[:, :, None] - log_heads[:, None, :]
        factor = jnp.where(allowed, jnp.exp(jnp.where(allowed, log_gap, 0.0)), 0.0)
        return jnp.einsum("hts,hsp->htp", inner_prod * factor, scaled_x, precision=exact_mode)

    blocks = jnp.arange(block_count, dtype=jnp.int32)
    ssd_out = lax.map(jax.checkpoint(ssd_rows), blocks)
    ssd_out = ssd_out.transpose(1, 0, 2, 3).reshape(head_count, length, head_dim).transpose(1, 0, 2)
    ssd_out = ssd_out + xconv.reshape(length, head_count, head_dim) * skip_gain[:, None]
    gated_out = ssd_out.reshape(length, inner_width) * jax.nn.silu(gate_z)
    grouped = gated_out.reshape(length, groups, inner_width // groups)
    grouped = grouped * lax.rsqrt(jnp.mean(grouped * grouped, axis=-1, keepdims=True) + eps)
    mamba_out = grouped.reshape(length, inner_width) * inner_gain
    att_heads = queries.shape[1] // AHDIM
    query_h = queries.reshape(length, att_heads, AHDIM).transpose(1, 0, 2)
    key_h = key_rows.reshape(length, att_heads, AHDIM).transpose(1, 0, 2)
    value_h = value_rows.reshape(length, att_heads, AHDIM).transpose(1, 0, 2)

    def attend_rows(block_index):
        first_row = block_index * block_rows
        rows_q = lax.dynamic_slice_in_dim(query_h, first_row, block_rows, 1)
        scores = jnp.einsum("hqd,hkd->hqk", rows_q, key_h, precision=exact_mode) * AHDIM ** (-0.5)
        allowed = visible(first_row, block_rows, segment)[None]
        scores = jnp.where(allowed, scores, -1e30)
        peak = jnp.max(scores, axis=-1, keepdims=True)
        weights = jnp.exp(scores - peak)
        weights = weights / jnp.sum(weights, axis=-1, keepdims=True)
        return jnp.einsum("hqk,hkd->hqd", weights, value_h, precision=exact_mode)

    attn_out = lax.map(jax.checkpoint(attend_rows), blocks)
    attn_out = attn_out.transpose(1, 0, 2, 3).reshape(att_heads, length, AHDIM).transpose(1, 0, 2)
    return (mamba_out, attn_out.reshape(length, att_heads * AHDIM))


def split_parts(matrix, widths, axis):
    pieces_out = []
    offset = 0
    for width in widths:
        pieces_out.append(lax.slice_in_dim(matrix, offset, offset + width, axis=axis))
        offset = offset + width
    return pieces_out


def reduce_weights(rows_first, cols_first):
    return (
        lax.psum_scatter(
            rows_first.astype(jnp.bfloat16), "dp", scatter_dimension=0, tiled=True
        ).astype(jnp.float32),
        lax.psum_scatter(
            cols_first.astype(jnp.bfloat16), "dp", scatter_dimension=1, tiled=True
        ).astype(jnp.float32),
    )


def shards(
    patches,
    keep_mask,
    segments,
    embed_weight,
    first_gain,
    mamba_gate,
    mamba_input,
    state_in,
    state_out,
    step_weight,
    conv_input,
    conv_statein,
    conv_stateout,
    step_bias,
    rate_log,
    skip_gain,
    inner_gain,
    mamba_output,
    query_weight,
    key_weight,
    value_weight,
    attn_output,
    second_gain,
    ffn_gate,
    ffn_up,
    ffn_down,
    out_grad,
):
    segment = segments[0]
    keep_col = keep_mask.astype(jnp.float32)[:, None]
    contract_last = (((1,), (1,)), ((), ()))
    row_block = patches
    embedded = lax.psum_scatter(
        jnp.dot(row_block, embed_weight, preferred_element_type=jnp.float32),
        "tp",
        scatter_dimension=0,
        tiled=True,
    )
    resid_one = embedded * keep_col
    normed_one = rms_scale(resid_one, first_gain).astype(jnp.bfloat16)
    full_one = lax.all_gather(normed_one, "tp", axis=0, tiled=True)
    in_list = (
        mamba_gate,
        mamba_input,
        state_in,
        state_out,
        step_weight,
        query_weight,
        key_weight,
        value_weight,
    )
    in_widths = [member.shape[1] for member in in_list]
    in_weights = jnp.concatenate(in_list, axis=1)
    projected = jnp.dot(full_one, in_weights, preferred_element_type=jnp.float32)
    proj_parts = tuple(split_parts(projected, in_widths, 1))
    core_params = (
        conv_input,
        conv_statein,
        conv_stateout,
        step_bias,
        rate_log,
        skip_gain,
        inner_gain,
    )

    def core_apply(proj_tuple, param_tuple):
        return mixer_core(
            proj_tuple[0],
            proj_tuple[1],
            proj_tuple[2],
            proj_tuple[3],
            proj_tuple[4],
            proj_tuple[5],
            proj_tuple[6],
            proj_tuple[7],
            param_tuple[0],
            param_tuple[1],
            param_tuple[2],
            param_tuple[3],
            param_tuple[4],
            param_tuple[5],
            param_tuple[6],
            segment,
        )

    core_result, core_pull = jax.vjp(core_apply, proj_parts, core_params)
    inner_width = mamba_output.shape[0]
    mix_in = jnp.concatenate([core_result[0], core_result[1]], axis=1).astype(jnp.bfloat16)
    out_weights = jnp.concatenate([mamba_output, attn_output], axis=0)
    row_block = mix_in
    mixer_sum = lax.psum_scatter(
        jnp.dot(row_block, out_weights, preferred_element_type=jnp.float32).astype(jnp.bfloat16),
        "tp",
        scatter_dimension=0,
        tiled=True,
    ).astype(jnp.float32)
    resid_two = resid_one + mixer_sum
    normed_two = rms_scale(resid_two, second_gain).astype(jnp.bfloat16)
    full_two = lax.all_gather(normed_two, "tp", axis=0, tiled=True)
    ffn_width = ffn_gate.shape[1]
    ffn_weights = jnp.concatenate([ffn_gate, ffn_up], axis=1)
    gate_up = jnp.dot(full_two, ffn_weights, preferred_element_type=jnp.float32)
    hidden_f, swiglu_pull = jax.vjp(swiglu, gate_up[:, :ffn_width], gate_up[:, ffn_width:])
    hidden = hidden_f.astype(jnp.bfloat16)
    row_block = hidden
    ffn_out = lax.psum_scatter(
        jnp.dot(row_block, ffn_down, preferred_element_type=jnp.float32).astype(jnp.bfloat16),
        "tp",
        scatter_dimension=0,
        tiled=True,
    ).astype(jnp.float32)
    result = (resid_two + ffn_out).astype(jnp.bfloat16)
    grad_full = lax.all_gather(out_grad, "tp", axis=0, tiled=True)
    down_grad = jnp.einsum("sf,sd->fd", hidden, grad_full, preferred_element_type=jnp.float32)
    hidden_grad = lax.dot_general(
        grad_full, ffn_down, contract_last, preferred_element_type=jnp.float32
    )
    gate_grad, up_grad = swiglu_pull(hidden_grad)
    gu_grad = jnp.concatenate([gate_grad, up_grad], axis=1).astype(jnp.bfloat16)
    ffn_in_grad = jnp.einsum("sd,sc->dc", full_two, gu_grad, preferred_element_type=jnp.float32)
    row_block = gu_grad
    normed_two_grad = lax.psum_scatter(
        lax.dot_general(
            row_block, ffn_weights, contract_last, preferred_element_type=jnp.float32
        ).astype(jnp.bfloat16),
        "tp",
        scatter_dimension=0,
        tiled=True,
    ).astype(jnp.float32)
    _, norm_two_pull = jax.vjp(rms_scale, resid_two, second_gain)
    two_part, second_gain_grad = norm_two_pull(normed_two_grad)
    resid_two_grad = out_grad.astype(jnp.float32) + two_part
    mix_grad = resid_two_grad.astype(jnp.bfloat16)
    mix_full = lax.all_gather(mix_grad, "tp", axis=0, tiled=True)
    mixout_grad = jnp.einsum("sc,sd->cd", mix_in, mix_full, preferred_element_type=jnp.float32)
    mixin_grad = lax.dot_general(
        mix_full, out_weights, contract_last, preferred_element_type=jnp.float32
    )
    proj_grads, param_grads = core_pull((mixin_grad[:, :inner_width], mixin_grad[:, inner_width:]))
    proj_grad = jnp.concatenate(proj_grads, axis=1).astype(jnp.bfloat16)
    in_grad = jnp.einsum("sd,sc->dc", full_one, proj_grad, preferred_element_type=jnp.float32)
    row_block = proj_grad
    normed_one_grad = lax.psum_scatter(
        lax.dot_general(
            row_block, in_weights, contract_last, preferred_element_type=jnp.float32
        ).astype(jnp.bfloat16),
        "tp",
        scatter_dimension=0,
        tiled=True,
    ).astype(jnp.float32)
    _, norm_one_pull = jax.vjp(rms_scale, resid_one, first_gain)
    one_part, first_gain_grad = norm_one_pull(normed_one_grad)
    resid_one_grad = resid_two_grad + one_part
    embedded_grad = (resid_one_grad * keep_col).astype(jnp.bfloat16)
    embedded_full = lax.all_gather(embedded_grad, "tp", axis=0, tiled=True)
    patches_grad = lax.dot_general(
        embedded_full, embed_weight, contract_last, preferred_element_type=jnp.float32
    ).astype(jnp.bfloat16)
    embed_grad = jnp.einsum("sp,sd->pd", patches, embedded_full, preferred_element_type=jnp.float32)
    rows_all, cols_all = reduce_weights(
        jnp.concatenate([in_grad, ffn_in_grad], axis=1),
        jnp.concatenate([embed_grad, mixout_grad, down_grad], axis=0),
    )
    head_sums = lax.psum(
        (
            param_grads[0],
            param_grads[1],
            param_grads[2],
            param_grads[3],
            param_grads[4],
            param_grads[5],
            param_grads[6],
        ),
        "dp",
    )
    gain_one_sum, gain_two_sum = (
        lax.psum_scatter(first_gain_grad, ("dp", "tp"), scatter_dimension=0, tiled=True),
        lax.psum_scatter(second_gain_grad, ("dp", "tp"), scatter_dimension=0, tiled=True),
    )
    row_parts = split_parts(rows_all, in_widths + [ffn_width, ffn_width], 1)
    col_parts = split_parts(
        cols_all, [embed_weight.shape[0], inner_width, attn_output.shape[0], ffn_down.shape[0]], 0
    )
    return (
        result,
        patches_grad,
        col_parts[0],
        gain_one_sum,
        row_parts[0],
        row_parts[1],
        row_parts[2],
        row_parts[3],
        row_parts[4],
        head_sums[0],
        head_sums[1],
        head_sums[2],
        head_sums[3],
        head_sums[4],
        head_sums[5],
        head_sums[6],
        col_parts[1],
        row_parts[5],
        row_parts[6],
        row_parts[7],
        col_parts[2],
        gain_two_sum,
        row_parts[8],
        row_parts[9],
        col_parts[3],
    )


def solution(mesh):
    return jax.shard_map(
        shards,
        mesh=mesh,
        in_specs=(
            P("dp", "tp"),
            P(("dp", "tp")),
            P("dp", None),
            P("tp", None),
            P(),
            P(None, "tp"),
            P(None, "tp"),
            P(None, "tp"),
            P(None, "tp"),
            P(None, "tp"),
            P(None, "tp"),
            P(None, "tp"),
            P(None, "tp"),
            P("tp"),
            P("tp"),
            P("tp"),
            P("tp"),
            P("tp", None),
            P(None, "tp"),
            P(None, "tp"),
            P(None, "tp"),
            P("tp", None),
            P(),
            P(None, "tp"),
            P(None, "tp"),
            P("tp", None),
            P(("dp", "tp"), None),
        ),
        out_specs=(
            P(("dp", "tp"), None),
            P("dp", "tp"),
            P("tp", "dp"),
            P(("dp", "tp")),
            P("dp", "tp"),
            P("dp", "tp"),
            P("dp", "tp"),
            P("dp", "tp"),
            P("dp", "tp"),
            P(None, "tp"),
            P(None, "tp"),
            P(None, "tp"),
            P("tp"),
            P("tp"),
            P("tp"),
            P("tp"),
            P("tp", "dp"),
            P("dp", "tp"),
            P("dp", "tp"),
            P("dp", "tp"),
            P("tp", "dp"),
            P(("dp", "tp")),
            P("dp", "tp"),
            P("dp", "tp"),
            P("tp", "dp"),
        ),
        check_vma=False,
    )
```

profile of v0, /device:TPU:0, one launch (start us, length us, event | category | flops | bytes accessed | tf_op | source)
XLA Modules:
  0.0 1234.7 jit_solution(6794374455360761532)
XLA Ops:
  7.3 10.1 fusion.170
  18.0 79.0 %reduce-scatter.10.cloned.1.call-done = f32[256,1024]{1,0:T(8,128)} async-done(((f32[1024,1024]{1,0:T(8,128)}), f32[256,1024]{1,0:T(8,128)}) %reduce-scatter.10.cloned.1.call-update) | async-done | bytes 1048592 | tf_op jit(solution)/shard_map/reduce_scatter | solution.py:178
  101.2 7.5 concatenate.77
  112.3 35.1 %all-gather.6.cloned.1.call-done = bf16[1024,1024]{1,0:T(8,128)(2,1)} async-done(((bf16[256,1024]{1,0:T(8,128)(2,1)}), bf16[1024,1024]{1,0:T(8,128)(2,1)}) %all-gather.6.cloned.1.call-update) | async-done | bytes 2097168 | tf_op jit(solution)/shard_map/all_gather | solution.py:186
  147.4 7.8 fusion.171
  175.9 5.5 fusion.110
  183.4 50.9 %while.65 = (s32[]{:T(128)}, f32[2,8,512,64]{2,3,1,0:T(8,128)}, s32[2]{0:T(128)S(1)}, f32[1,1024,128]{2,1,0:T(8,128)S(1)}, f32[1,1024,128]{2,1,0:T(8,128)S(1)}, ...) while((s32[]{:T(128)}, f32[2,8,512,64]{2,3,1,0:T(8,128)}, ...), condition=%wide.region_5.6_spmd.clone, body=%wide.region_4.5_spmd.clone.sunk | while | flops 4044882432 | bytes 17660152 | solution.py:97
  187.3 21.5 %fusion.258 = f32[2,8,512,64]{2,3,1,0:T(8,128)} fusion(f32[2,8,512,64]{2,3,1,0:T(8,128)} %get-tuple-element.1586, s32[]{:T(128)S(6)} %copy.275, f32[8,1024,64]{1,2,0:T(8,128)S(1)} %copy-done.54, f32[8,1024]{1,0:T(8,128)S(1)} %bitcast.347, f32[8,512]{1,0:T(8,128)S(1)} %constant_dynamic-slice_fusion.10, f32[512,1024]{1,0:T(8,128)S(1)} %fusion.256, ...), kind=kOutput, calls=%fused_computation.18.clone.1 | convolution fusion | flops 3238002688 | bytes 5816324 | tf_op jit(solution)/shard_map/jvp()/while/body/eval_jaxpr/hts,hsp->htp/dot_general | solution.py:94
  212.5 21.5 %fusion.258 = f32[2,8,512,64]{2,3,1,0:T(8,128)} fusion(f32[2,8,512,64]{2,3,1,0:T(8,128)} %get-tuple-element.1586, s32[]{:T(128)S(6)} %copy.275, f32[8,1024,64]{1,2,0:T(8,128)S(1)} %copy-done.54, f32[8,1024]{1,0:T(8,128)S(1)} %bitcast.347, f32[8,512]{1,0:T(8,128)S(1)} %constant_dynamic-slice_fusion.10, f32[512,1024]{1,0:T(8,128)S(1)} %fusion.256, ...), kind=kOutput, calls=%fused_computation.18.clone.1 | convolution fusion | flops 3238002688 | bytes 5816324 | tf_op jit(solution)/shard_map/jvp()/while/body/eval_jaxpr/hts,hsp->htp/dot_general | solution.py:94
  237.3 4.3 multiply_reduce_fusion.9
  244.7 53.3 %while.66 = (s32[]{:T(128)}, bf16[2,4,512,64]{3,2,1,0:T(8,128)(2,1)}, s32[2]{0:T(128)S(1)}, s32[1024]{0:T(1024)S(1)}, s32[1,1024]{1,0:T(1,128)S(1)}, /*index=5*/...) while((s32[]{:T(128)}, ...), condition=%wide.region_10.11_spmd.clone, body=%wide.region_7.10_spmd.clone.sunk | while | flops 1616380416 | bytes 12597447 | solution.py:120
  246.6 10.9 multiply_select_fusion.4
  257.5 11.9 online-softmax
  273.2 10.9 multiply_select_fusion.4
  284.1 11.9 online-softmax
  305.3 4.6 convolution_convert_fusion.6
  310.0 42.7 %reduce-scatter.12.cloned.1.call-done = bf16[256,1024]{1,0:T(8,128)(2,1)} async-done(((bf16[1024,1024]{1,0:T(8,128)(2,1)}), bf16[256,1024]{1,0:T(8,128)(2,1)}) %reduce-scatter.12.cloned.1.call-update) | async-done | bytes 524304 | tf_op jit(solution)/shard_map/reduce_scatter | solution.py:236
  361.9 39.9 %all-gather.8.cloned.1.call-done = bf16[1024,1024]{1,0:T(8,128)(2,1)} async-done(((bf16[256,1024]{1,0:T(8,128)(2,1)}), bf16[1024,1024]{1,0:T(8,128)(2,1)}) %all-gather.8.cloned.1.call-update) | async-done | bytes 2097168 | tf_op jit(solution)/shard_map/all_gather | solution.py:244
  401.8 10.7 fusion.172
  412.4 35.4 %all-gather.10.cloned.1.call-done = bf16[1024,1024]{1,0:T(8,128)(2,1)} async-done(((bf16[256,1024]{1,0:T(8,128)(2,1)}), bf16[1024,1024]{1,0:T(8,128)(2,1)}) %all-gather.10.cloned.1.call-update) | async-done | bytes 2097168 | tf_op jit(solution)/shard_map/all_gather | solution.py:258
  447.9 8.2 fusion.97
  458.1 7.9 fusion.111
  466.1 42.7 %reduce-scatter.16.cloned.1.call-done = bf16[256,1024]{1,0:T(8,128)(2,1)} async-done(((bf16[1024,1024]{1,0:T(8,128)(2,1)}), bf16[256,1024]{1,0:T(8,128)(2,1)}) %reduce-scatter.16.cloned.1.call-update) | async-done | bytes 524304 | tf_op jit(solution)/shard_map/reduce_scatter | solution.py:267
  516.3 42.7 %all-gather.12.cloned.1.call-done = bf16[1024,1024]{1,0:T(8,128)(2,1)} async-done(((bf16[256,1024]{1,0:T(8,128)(2,1)}), bf16[1024,1024]{1,0:T(8,128)(2,1)}) %all-gather.12.cloned.1.call-update) | async-done | bytes 2097168 | tf_op jit(solution)/shard_map/all_gather | solution.py:279
  559.0 4.0 fusion.173
  566.4 5.0 multiply_reduce_fusion.3
  576.2 127.1 %while.67 = (s32[]{:T(128)}, f32[1,1024,128]{1,2,0:T(8,128)}, f32[1,1024,128]{2,1,0:T(8,128)}, f32[8,1024]{1,0:T(8,128)S(1)}, f32[8,1024,64]{1,2,0:T(8,128)}, /*...) while((s32[]{:T(128)}, f32[1,1024,128]{1,2,0:T(8,128)}, ...), condition=%wide.region_21.22_spmd.clone, body=%wide.region_17.21_spmd.clone.sunk | while | flops 8923725824 | bytes 76626464 | solution.py:97
  586.8 22.9 %fusion.274 = (f32[8,512]{1,0:T(8,128)}, f32[8,1024]{1,0:T(8,128)S(1)}, f32[512,1024]{1,0:T(8,128)S(1)}) fusion(f32[512,1024]{1,0:T(8,128)S(1)} %fusion.272, f32[8,1024]{1,0:T(8,128)S(1)} %get-tuple-element.1540, f32[8,512]{1,0:T(8,128)S(1)} %constant_dynamic-slice_fusion.13, pred[512,1024]{1,0:T(8,128)(4,1)S(1)} %fusion.273, ...), kind=kOutput, calls=%fused_computation.40.clone.1 | convolution fusion | flops 3266826240 | bytes 7962624 | tf_op jit(solution)/shard_map/transpose(jvp())/while/body/eval_jaxpr/checkpoint/hts,hsp->htp/dot_general | solution.py:94
  615.4 6.0 fusion.276
  621.4 18.2 %select_add_fusion.5 = f32[8,1024,64]{1,2,0:T(8,128)} fusion(f32[8,1024,64]{1,2,0:T(8,128)} %get-tuple-element.1669, f32[8,512,64]{1,2,0:T(8,128)S(1)} %bitcast.310, f32[512,1024]{1,0:T(8,128)S(1)} %copy-done.11, f32[8,1024]{1,0:T(8,128)S(1)} %get-tuple-element.1540, f32[8,512]{1,0:T(8,128)S(1)} %copy-done.70, pred[512,1024]{1,0:T(8,128)(4,1)} %copy-done.31, ...), kind=kOutput, calls=%fused_computation.47.clone.1 | convolution fusion | flops 3239051264 | bytes 7913473 | tf_op jit(solution)/shard_map/transpose(jvp())/while/body/eval_jaxpr/checkpoint/hts,hsp->htp/dot_general | solution.py:94
  649.9 22.9 %fusion.274 = (f32[8,512]{1,0:T(8,128)}, f32[8,1024]{1,0:T(8,128)S(1)}, f32[512,1024]{1,0:T(8,128)S(1)}) fusion(f32[512,1024]{1,0:T(8,128)S(1)} %fusion.272, f32[8,1024]{1,0:T(8,128)S(1)} %get-tuple-element.1540, f32[8,512]{1,0:T(8,128)S(1)} %constant_dynamic-slice_fusion.13, pred[512,1024]{1,0:T(8,128)(4,1)S(1)} %fusion.273, ...), kind=kOutput, calls=%fused_computation.40.clone.1 | convolution fusion | flops 3266826240 | bytes 7962624 | tf_op jit(solution)/shard_map/transpose(jvp())/while/body/eval_jaxpr/checkpoint/hts,hsp->htp/dot_general | solution.py:94
  678.5 6.0 fusion.276
  684.6 18.5 %select_add_fusion.5 = f32[8,1024,64]{1,2,0:T(8,128)} fusion(f32[8,1024,64]{1,2,0:T(8,128)} %get-tuple-element.1669, f32[8,512,64]{1,2,0:T(8,128)S(1)} %bitcast.310, f32[512,1024]{1,0:T(8,128)S(1)} %copy-done.11, f32[8,1024]{1,0:T(8,128)S(1)} %get-tuple-element.1540, f32[8,512]{1,0:T(8,128)S(1)} %copy-done.70, pred[512,1024]{1,0:T(8,128)(4,1)} %copy-done.31, ...), kind=kOutput, calls=%fused_computation.47.clone.1 | convolution fusion | flops 3239051264 | bytes 7913473 | tf_op jit(solution)/shard_map/transpose(jvp())/while/body/eval_jaxpr/checkpoint/hts,hsp->htp/dot_general | solution.py:94
  707.5 5.6 multiply_reduce_fusion.7
  718.1 4.4 multiply_reduce_fusion.12
  729.7 9.9 reduce-window.16
  743.6 166.1 %while.68 = (s32[]{:T(128)}, f32[4,1024,64]{1,2,0:T(8,128)}, f32[4,1024,64]{1,2,0:T(8,128)}, f32[4,1024,64]{1,2,0:T(8,128)}, s32[2]{0:T(128)S(1)}, /*index=5*/f3...) while((s32[]{:T(128)}, f32[4,1024,64]{1,2,0:T(8,128)}, ...), condition=%wide.region_31.32_spmd.clone, body=%wide.region_25.31_spmd.clone.sunk | while | flops 8129217024 | bytes 241367584 | solution.py:120
  768.4 9.3 fusion.285
  780.1 13.1 %convert_reduce_fusion.2 = (f32[4,512]{1,0:T(4,128)S(1)}, pred[4,512,1024]{2,1,0:T(32,128)(4,1)S(1)}, f32[4,512]{1,0:T(4,128)S(1)}, f32[4,512,1024]{2,1,0:T(8,128)}) fusion(f32[4,512]{1,0:T(4,128)S(1)} %get-tuple-element.1561, f32[4,512,1024]{2,1,0:T(8,128)S(1)} %get-tuple-element.1562, pred[512,1024]{1,0:T(8,128)(4,1)S(1)} %fusion.284, ...), kind=kOutput, calls=%fused_computation.73.clone.1 | convolution fusion | flops 1629483008 | bytes 21004288 | tf_op jit(solution)/shard_map/transpose(jvp())/while/body/eval_jaxpr/checkpoint/hqk,hkd->hqd/dot_general | solution.py:118
  793.2 6.7 fusion.287
  800.0 10.3 fusion.288
  811.3 12.8 %fusion.289 = f32[4,1024,64]{1,2,0:T(8,128)} fusion(f32[4,512,1024]{2,1,0:T(8,128)} %copy-done.3, pred[4,512,1024]{2,1,0:T(32,128)(4,1)} %copy-done.151, f32[4,512]{1,0:T(4,128)S(1)} %negate_divide_fusion.2, pred[512,1024]{1,0:T(8,128)(4,1)S(1)} %fusion.284, f32[4,1024,64]{1,2,0:T(8,128)} %get-tuple-element.1713, pred[]{:T(512)S(6)} %compare.39, ...), kind=kOutput, calls=%fused_computation.96.clone.1 | convolution fusion | flops 1619525632 | bytes 13639685 | tf_op jit(solution)/shard_map/transpose(jvp())/while/body/eval_jaxpr/checkpoint/hqd,hkd->hqk/dot_general | solution.py:112
  824.1 7.9 fusion.290
  836.6 9.3 fusion.285
  848.2 13.1 %convert_reduce_fusion.2 = (f32[4,512]{1,0:T(4,128)S(1)}, pred[4,512,1024]{2,1,0:T(32,128)(4,1)S(1)}, f32[4,512]{1,0:T(4,128)S(1)}, f32[4,512,1024]{2,1,0:T(8,128)}) fusion(f32[4,512]{1,0:T(4,128)S(1)} %get-tuple-element.1561, f32[4,512,1024]{2,1,0:T(8,128)S(1)} %get-tuple-element.1562, pred[512,1024]{1,0:T(8,128)(4,1)S(1)} %fusion.284, ...), kind=kOutput, calls=%fused_computation.73.clone.1 | convolution fusion | flops 1629483008 | bytes 21004288 | tf_op jit(solution)/shard_map/transpose(jvp())/while/body/eval_jaxpr/checkpoint/hqk,hkd->hqd/dot_general | solution.py:118
  861.3 6.7 fusion.287
  868.1 10.3 fusion.288
  879.4 13.1 %fusion.289 = f32[4,1024,64]{1,2,0:T(8,128)} fusion(f32[4,512,1024]{2,1,0:T(8,128)} %copy-done.3, pred[4,512,1024]{2,1,0:T(32,128)(4,1)} %copy-done.151, f32[4,512]{1,0:T(4,128)S(1)} %negate_divide_fusion.2, pred[512,1024]{1,0:T(8,128)(4,1)S(1)} %fusion.284, f32[4,1024,64]{1,2,0:T(8,128)} %get-tuple-element.1713, pred[]{:T(512)S(6)} %compare.39, ...), kind=kOutput, calls=%fused_computation.96.clone.1 | convolution fusion | flops 1619525632 | bytes 13639685 | tf_op jit(solution)/shard_map/transpose(jvp())/while/body/eval_jaxpr/checkpoint/hqd,hkd->hqk/dot_general | solution.py:112
  892.5 7.9 fusion.290
  924.8 8.6 convolution_convert_fusion.4
  933.4 5.2 convolution_convert_fusion.5
  938.8 37.3 %reduce-scatter.18.cloned.1.call-done = bf16[256,1024]{1,0:T(8,128)(2,1)} async-done(((bf16[1024,1024]{1,0:T(8,128)(2,1)}), bf16[256,1024]{1,0:T(8,128)(2,1)}) %reduce-scatter.18.cloned.1.call-update) | async-done | bytes 524304 | tf_op jit(solution)/shard_map/reduce_scatter | solution.py:288
  977.6 44.0 %reduce-scatter.14.cloned.1.call-done = bf16[256,1024]{1,0:T(8,128)(2,1)} async-done(((bf16[1024,1024]{1,0:T(8,128)(2,1)}), bf16[256,1024]{1,0:T(8,128)(2,1)}) %reduce-scatter.14.cloned.1.call-update) | async-done | bytes 524304 | tf_op jit(solution)/shard_map/reduce_scatter | solution.py:251
  1025.2 9.6 convolution_convert_fusion.1
  1034.7 8.5 convolution_convert_fusion
  1043.3 7.8 pad_maximum_fusion
  1051.1 11.4 copy.181
  1062.6 6.1 convolution_convert_fusion.3
  1071.7 7.5 convert_bitcast_fusion
  1079.3 4.1 pad_maximum_fusion.1
  1084.5 24.3 %all-reduce.35 = (f32[4,512]{1,0:T(4,128)}, f32[4,128]{1,0:T(4,128)}, f32[4,128]{1,0:T(4,128)}, f32[8]{0:T(128)}, f32[8]{0:T(128)}, /*index=5*/f32[8]{0:T(128)}, f32[512]{0:T(512)}) all-reduce(f32[4,512]{1,0:T(4,128)S(1)} %pad_add_fusion, f32[4,128]{1,0:T(4,128)S(1)} %pad_add_fusion.2, ...), channel_id=1, replica_groups=mesh['dp'=8,'tp'=4] {'dp'}, use_global_device_ids=true, to_apply=%region_42.43 | all-reduce | flops 3608 | bytes 28864 | tf_op jit(solution)/shard_map/psum | solution.py:309
  1108.8 39.5 %all-reduce.34 = (f32[1024]{0:T(1024)S(1)}, f32[1024]{0:T(1024)S(1)}) all-reduce(f32[1024]{0:T(1024)S(1)} %get-tuple-element.1096, f32[1024]{0:T(1024)S(1)} %copy-done.96), channel_id=8, replica_groups=mesh['dp'=8,'tp'=4] {'dp','tp'}, use_global_device_ids=true, to_apply=%region_36.37.clone | all-reduce | flops 2048 | bytes 16384
  1149.4 9.5 convolution_convert_fusion.2
  1174.0 45.8 %reduce-scatter.20.cloned.1.call-done = bf16[3840,128]{0,1:T(8,128)(2,1)} async-done(((bf16[3840,1024]{0,1:T(8,128)(2,1)}), bf16[3840,128]{0,1:T(8,128)(2,1)}) %reduce-scatter.20.cloned.1.call-update) | async-done | bytes 983056 | tf_op jit(solution)/shard_map/reduce_scatter | solution.py:139
  (585 shorter events, 196.3 us)
Async XLA Ops:
  7.2 440.7 %copy-start = (bf16[1024,1024]{1,0:T(8,128)(2,1)S(1)}, bf16[1024,1024]{1,0:T(8,128)(2,1)}, u32[]{:S(2)}) copy-start(bf16[1024,1024]{1,0:T(8,128)(2,1)} %param.60) | copy-start | bytes 6291460
  7.2 89.8 %reduce-scatter.10.cloned.1.call-start = ((), (), s32[]{:S(2)}) async-start(), calls=%async_computation.7 | async-start | bytes 5242880 | tf_op jit(solution)/shard_map/reduce_scatter | solution.py:178
  17.4 81.1 %copy-start.75 = (f32[1024]{0:T(1024)S(1)}, f32[1024]{0:T(1024)}, u32[]{:S(2)}) copy-start(f32[1024]{0:T(1024)} %param.39) | copy-start | bytes 12292
  17.4 83.6 %copy-start.97 = (bf16[1024,8]{0,1:T(8,128)(2,1)S(1)}, bf16[1024,8]{0,1:T(8,128)(2,1)}, u32[]{:S(2)}) copy-start(bf16[1024,8]{0,1:T(8,128)(2,1)} %param.44) | copy-start | bytes 49156
  17.4 83.8 %copy-start.57 = (bf16[1024,512]{1,0:T(8,128)(2,1)S(1)}, bf16[1024,512]{1,0:T(8,128)(2,1)}, u32[]{:S(2)}) copy-start(bf16[1024,512]{1,0:T(8,128)(2,1)} %param.40) | copy-start | bytes 3145732
  17.4 129.9 %all-gather.6.cloned.1.call-start = ((), (), s32[]{:S(2)}) async-start(), calls=%async_computation.8 | async-start | bytes 2621440 | tf_op jit(solution)/shard_map/all_gather | solution.py:186
  18.0 334.7 %copy-start.77 = (f32[256]{0:T(256)}, f32[256]{0:T(256)S(1)}, u32[]{:S(2)}) copy-start(f32[256]{0:T(256)S(1)} %convert_element_type.71) | copy-start | bytes 3076
  98.5 10.3 copy-start.105
  98.5 10.2 copy-start.98
  100.7 252.0 %reduce-scatter.12.cloned.1.call-start = ((), (), s32[]{:S(2)}) async-start(), calls=%async_computation.9 | async-start | bytes 2621440 | tf_op jit(solution)/shard_map/reduce_scatter | solution.py:236
  111.9 50.9 %copy-start.133 = (f32[8]{0:T(128)}, f32[8]{0:T(128)S(1)}, u32[]{:S(2)}) copy-start(f32[8]{0:T(128)S(1)} %exponential_negate_fusion) | copy-start | bytes 100
  112.0 401.6 %copy-start.79 = (pred[1024]{0:T(1024)(128)(4,1)}, pred[1024]{0:T(1024)(128)(4,1)S(1)}, u32[]{:S(2)}) copy-start(pred[1024]{0:T(1024)(128)(4,1)S(1)} %get-tuple-element.1255) | copy-start | bytes 3076
  112.1 402.2 %copy-start.83 = (pred[1024]{0:T(1024)(128)(4,1)}, pred[1024]{0:T(1024)(128)(4,1)S(1)}, u32[]{:S(2)}) copy-start(pred[1024]{0:T(1024)(128)(4,1)S(1)} %get-tuple-element.1257) | copy-start | bytes 3076
  112.1 402.8 %copy-start.81 = (pred[1024]{0:T(1024)(128)(4,1)}, pred[1024]{0:T(1024)(128)(4,1)S(1)}, u32[]{:S(2)}) copy-start(pred[1024]{0:T(1024)(128)(4,1)S(1)} %get-tuple-element.1256) | copy-start | bytes 3076
  112.1 57.4 %copy-start.115 = (f32[128]{0:T(128)}, f32[128]{0:T(128)S(1)}, u32[]{:S(2)}) copy-start(f32[128]{0:T(128)S(1)} %get-tuple-element.1275) | copy-start | bytes 1540
  112.1 57.4 %copy-start.117 = (f32[128]{0:T(128)}, f32[128]{0:T(128)S(1)}, u32[]{:S(2)}) copy-start(f32[128]{0:T(128)S(1)} %get-tuple-element.1258) | copy-start | bytes 1540
  112.1 57.4 %copy-start.119 = (f32[128]{0:T(128)}, f32[128]{0:T(128)S(1)}, u32[]{:S(2)}) copy-start(f32[128]{0:T(128)S(1)} %get-tuple-element.1260) | copy-start | bytes 1540
  112.1 57.4 %copy-start.121 = (f32[128]{0:T(128)}, f32[128]{0:T(128)S(1)}, u32[]{:S(2)}) copy-start(f32[128]{0:T(128)S(1)} %get-tuple-element.1273) | copy-start | bytes 1540
  112.2 57.4 %copy-start.123 = (f32[128]{0:T(128)}, f32[128]{0:T(128)S(1)}, u32[]{:S(2)}) copy-start(f32[128]{0:T(128)S(1)} %get-tuple-element.1261) | copy-start | bytes 1540
  112.2 57.4 %copy-start.125 = (f32[128]{0:T(128)}, f32[128]{0:T(128)S(1)}, u32[]{:S(2)}) copy-start(f32[128]{0:T(128)S(1)} %get-tuple-element.1272) | copy-start | bytes 1540
  112.2 57.4 %copy-start.127 = (f32[128]{0:T(128)}, f32[128]{0:T(128)S(1)}, u32[]{:S(2)}) copy-start(f32[128]{0:T(128)S(1)} %get-tuple-element.1259) | copy-start | bytes 1540
  112.2 57.4 %copy-start.129 = (f32[128]{0:T(128)}, f32[128]{0:T(128)S(1)}, u32[]{:S(2)}) copy-start(f32[128]{0:T(128)S(1)} %get-tuple-element.1274) | copy-start | bytes 1540
  112.2 63.6 %copy-start.87 = (f32[1,512]{1,0:T(1,128)}, f32[1,512]{1,0:T(1,128)S(1)}, u32[]{:S(2)}) copy-start(f32[1,512]{1,0:T(1,128)S(1)} %get-tuple-element.1251) | copy-start | bytes 6148
  112.2 63.6 %copy-start.89 = (f32[1,512]{1,0:T(1,128)}, f32[1,512]{1,0:T(1,128)S(1)}, u32[]{:S(2)}) copy-start(f32[1,512]{1,0:T(1,128)S(1)} %get-tuple-element.1253) | copy-start | bytes 6148
  112.2 63.6 %copy-start.91 = (f32[1,512]{1,0:T(1,128)}, f32[1,512]{1,0:T(1,128)S(1)}, u32[]{:S(2)}) copy-start(f32[1,512]{1,0:T(1,128)S(1)} %get-tuple-element.1254) | copy-start | bytes 6148
  112.2 63.6 %copy-start.93 = (f32[1,512]{1,0:T(1,128)}, f32[1,512]{1,0:T(1,128)S(1)}, u32[]{:S(2)}) copy-start(f32[1,512]{1,0:T(1,128)S(1)} %get-tuple-element.1252) | copy-start | bytes 6148
  163.0 18.5 %copy-start.62 = (f32[1024,8]{0,1:T(8,128)}, f32[1024,8]{0,1:T(8,128)S(1)}, u32[]{:S(2)}) copy-start(f32[1024,8]{0,1:T(8,128)S(1)} %get-tuple-element.1213) | copy-start | bytes 98308
  309.9 45.5 %copy-start.73 = (f32[1024]{0:T(1024)S(1)}, f32[1024]{0:T(1024)}, u32[]{:S(2)}) copy-start(f32[1024]{0:T(1024)} %param.57) | copy-start | bytes 12292
  310.0 91.8 %all-gather.8.cloned.1.call-start = ((), (), s32[]{:S(2)}) async-start(), calls=%async_computation.10 | async-start | bytes 2621440 | tf_op jit(solution)/shard_map/all_gather | solution.py:244
  354.4 156.7 %copy-start.85 = (f32[256]{0:T(256)}, f32[256]{0:T(256)S(1)}, u32[]{:S(2)}) copy-start(f32[256]{0:T(256)S(1)} %fusion.148) | copy-start | bytes 3076
  356.4 91.5 %all-gather.10.cloned.1.call-start = ((), (), s32[]{:S(2)}) async-start(), calls=%async_computation.12 | async-start | bytes 2621440 | tf_op jit(solution)/shard_map/all_gather | solution.py:258
  356.9 151.8 %reduce-scatter.16.cloned.1.call-start = ((), (), s32[]{:S(2)}) async-start(), calls=%async_computation.13 | async-start | bytes 2621440 | tf_op jit(solution)/shard_map/reduce_scatter | solution.py:267
  466.0 93.0 %all-gather.12.cloned.1.call-start = ((), (), s32[]{:S(2)}) async-start(), calls=%async_computation.14 | async-start | bytes 2621440 | tf_op jit(solution)/shard_map/all_gather | solution.py:279
  513.5 462.6 %reduce-scatter.18.cloned.1.call-start = ((), (), s32[]{:S(2)}) async-start(), calls=%async_computation.15 | async-start | bytes 2621440 | tf_op jit(solution)/shard_map/reduce_scatter | solution.py:288
  576.2 127.1 %copy-start.63 = (f32[1024,8]{0,1:T(8,128)S(1)}, f32[1024,8]{0,1:T(8,128)}, u32[]{:S(2)}) copy-start(f32[1024,8]{0,1:T(8,128)} %copy-done.62) | copy-start | bytes 98308
  586.2 23.6 %copy-start.10 = (f32[512,1024]{1,0:T(8,128)}, f32[512,1024]{1,0:T(8,128)S(1)}, u32[]{:S(2)}) copy-start(f32[512,1024]{1,0:T(8,128)S(1)} %fusion.272) | copy-start | bytes 6291460 | tf_op jit(solution)/shard_map/transpose(jvp())/while
  586.2 23.5 %copy-start.69 = (f32[8,512]{1,0:T(8,128)}, f32[8,512]{1,0:T(8,128)S(1)}, u32[]{:S(2)}) copy-start(f32[8,512]{1,0:T(8,128)S(1)} %constant_dynamic-slice_fusion.13) | copy-start | bytes 49156 | tf_op jit(solution)/shard_map/transpose(jvp())/while
  586.8 22.9 %copy-start.31 = (pred[512,1024]{1,0:T(8,128)(4,1)}, pred[512,1024]{1,0:T(8,128)(4,1)S(1)}, u32[]{:S(2)}) copy-start(pred[512,1024]{1,0:T(8,128)(4,1)S(1)} %fusion.273) | copy-start | bytes 1572868 | tf_op jit(solution)/shard_map/transpose(jvp())/while
  649.2 23.6 %copy-start.10 = (f32[512,1024]{1,0:T(8,128)}, f32[512,1024]{1,0:T(8,128)S(1)}, u32[]{:S(2)}) copy-start(f32[512,1024]{1,0:T(8,128)S(1)} %fusion.272) | copy-start | bytes 6291460 | tf_op jit(solution)/shard_map/transpose(jvp())/while
  649.3 23.5 %copy-start.69 = (f32[8,512]{1,0:T(8,128)}, f32[8,512]{1,0:T(8,128)S(1)}, u32[]{:S(2)}) copy-start(f32[8,512]{1,0:T(8,128)S(1)} %constant_dynamic-slice_fusion.13) | copy-start | bytes 49156 | tf_op jit(solution)/shard_map/transpose(jvp())/while
  649.9 22.9 %copy-start.31 = (pred[512,1024]{1,0:T(8,128)(4,1)}, pred[512,1024]{1,0:T(8,128)(4,1)S(1)}, u32[]{:S(2)}) copy-start(pred[512,1024]{1,0:T(8,128)(4,1)S(1)} %fusion.273) | copy-start | bytes 1572868 | tf_op jit(solution)/shard_map/transpose(jvp())/while
  728.6 12.0 slice-start
  777.7 15.4 %copy-start.1 = (f32[4,512,1024]{2,1,0:T(8,128)}, f32[4,512,1024]{2,1,0:T(8,128)S(1)}, u32[]{:S(2)}) copy-start(f32[4,512,1024]{2,1,0:T(8,128)S(1)} %get-tuple-element.1562) | copy-start | bytes 25165828 | tf_op jit(solution)/shard_map/transpose(jvp())/while
  799.9 10.4 copy-start.3
  811.3 12.8 %copy-start.2 = (f32[4,512,1024]{2,1,0:T(8,128)S(1)}, f32[4,512,1024]{2,1,0:T(8,128)}, u32[]{:S(2)}) copy-start(f32[4,512,1024]{2,1,0:T(8,128)} %copy-done.1) | copy-start | bytes 25165828 | tf_op jit(solution)/shard_map/transpose(jvp())/while
  811.3 12.8 %copy-start.58 = (f32[4,1024,64]{1,2,0:T(8,128)S(1)}, f32[4,1024,64]{1,2,0:T(8,128)}, u32[]{:S(2)}) copy-start(f32[4,1024,64]{1,2,0:T(8,128)} %get-tuple-element.1714) | copy-start | bytes 3145732 | tf_op jit(solution)/shard_map/transpose(jvp())/while
  845.8 15.4 %copy-start.1 = (f32[4,512,1024]{2,1,0:T(8,128)}, f32[4,512,1024]{2,1,0:T(8,128)S(1)}, u32[]{:S(2)}) copy-start(f32[4,512,1024]{2,1,0:T(8,128)S(1)} %get-tuple-element.1562) | copy-start | bytes 25165828 | tf_op jit(solution)/shard_map/transpose(jvp())/while
  868.0 10.4 copy-start.3
  879.4 13.1 %copy-start.2 = (f32[4,512,1024]{2,1,0:T(8,128)S(1)}, f32[4,512,1024]{2,1,0:T(8,128)}, u32[]{:S(2)}) copy-start(f32[4,512,1024]{2,1,0:T(8,128)} %copy-done.1) | copy-start | bytes 25165828 | tf_op jit(solution)/shard_map/transpose(jvp())/while
  879.4 13.1 %copy-start.58 = (f32[4,1024,64]{1,2,0:T(8,128)S(1)}, f32[4,1024,64]{1,2,0:T(8,128)}, u32[]{:S(2)}) copy-start(f32[4,1024,64]{1,2,0:T(8,128)} %get-tuple-element.1714) | copy-start | bytes 3145732 | tf_op jit(solution)/shard_map/transpose(jvp())/while
  912.6 12.1 slice-start.1
  933.4 88.3 %reduce-scatter.14.cloned.1.call-start = ((), (), s32[]{:S(2)}) async-start(), calls=%async_computation.11 | async-start | bytes 2621440 | tf_op jit(solution)/shard_map/reduce_scatter | solution.py:251
  938.7 37.5 %copy-start.15 = (f32[256,1024]{1,0:T(8,128)S(1)}, f32[256,1024]{1,0:T(8,128)}, u32[]{:S(2)}) copy-start(f32[256,1024]{1,0:T(8,128)} %reduce-scatter.10.cloned.1.call-done) | copy-start | bytes 3145732
  938.7 37.5 %copy-start.76 = (f32[1024]{0:T(1024)S(1)}, f32[1024]{0:T(1024)}, u32[]{:S(2)}) copy-start(f32[1024]{0:T(1024)} %param.39) | copy-start | bytes 12292
  938.7 37.5 %copy-start.78 = (f32[256]{0:T(256)S(1)}, f32[256]{0:T(256)}, u32[]{:S(2)}) copy-start(f32[256]{0:T(256)} %copy-done.77) | copy-start | bytes 3076
  938.7 37.5 %copy-start.99 = (f32[256]{0:T(256)S(1)}, f32[256]{0:T(256)}, u32[]{:S(2)}) copy-start(f32[256]{0:T(256)} %copy-done.98) | copy-start | bytes 3076
  938.7 38.9 %copy-start.106 = (f32[256]{0:T(256)S(1)}, f32[256]{0:T(256)}, u32[]{:S(2)}) copy-start(f32[256]{0:T(256)} %copy-done.105) | copy-start | bytes 3076
  938.7 83.0 %copy-start.74 = (f32[1024]{0:T(1024)S(1)}, f32[1024]{0:T(1024)}, u32[]{:S(2)}) copy-start(f32[1024]{0:T(1024)} %param.57) | copy-start | bytes 12292
  938.7 83.0 %copy-start.86 = (f32[256]{0:T(256)S(1)}, f32[256]{0:T(256)}, u32[]{:S(2)}) copy-start(f32[256]{0:T(256)} %copy-done.85) | copy-start | bytes 3076
  938.7 82.9 %copy-start.104 = (f32[256]{0:T(256)S(1)}, f32[256]{0:T(256)}, u32[]{:S(2)}) copy-start(f32[256]{0:T(256)} %copy-done.103) | copy-start | bytes 3076
  938.7 132.9 %all-gather.14.cloned.1.call-start = ((), (), s32[]{:S(2)}) async-start(), calls=%async_computation.16 | async-start | bytes 2621440 | tf_op jit(solution)/shard_map/all_gather | solution.py:300
  1025.1 133.9 %reduce-scatter.22.cloned.1.call-start = ((), (), s32[]{:S(2)}) async-start(), calls=%async_computation.18 | async-start | bytes 9732096
  1062.5 157.3 %reduce-scatter.20.cloned.1.call-start = ((), (), s32[]{:S(2)}) async-start(), calls=%async_computation.17 | async-start | bytes 8847360 | tf_op jit(solution)/shard_map/reduce_scatter | solution.py:139
  1083.5 25.3 %copy-start.96 = (f32[1024]{0:T(1024)S(1)}, f32[1024]{0:T(1024)}, u32[]{:S(2)}) copy-start(f32[1024]{0:T(1024)} %get-tuple-element.1098) | copy-start | bytes 12292
  (126 other events, 437.6 us)
Sparse Core Ops, SparseCore 0:
  17.5 79.4 reduce-scatter.9
  100.9 46.4 all-gather.5
  310.1 42.5 reduce-scatter.11
  356.5 45.2 all-gather.7
  403.2 44.6 all-gather.9
  466.1 42.5 reduce-scatter.15
  513.7 45.2 all-gather.11
  933.5 42.5 reduce-scatter.17
  978.4 43.1 reduce-scatter.13
  1025.2 45.2 all-gather.13
  1074.5 72.4 reduce-scatter.21
  1150.3 69.4 reduce-scatter.19
where the time goes:
time: 1240 us; the launch traced here: 1230 us
  waiting for transfers between devices  445 us (36%)
  matrix products  390 us (31%)
  local copies, waits for them, and re-layouts  136 us (11%)
  other arithmetic  123 us (10%)
  blocking collectives  63.8 us (5%)
  loops' own time  36.7 us (3%)
  Pallas kernels  23.7 us (2%)
  between operations  16.2 us (1%)
    dot_general x6, matrix products, ssd_rows(): jnp.einsum('hts,hsp->htp', inner_prod * factor, scaled_x, precision=exact...  125 us
    dot_general x8, matrix products, attend_rows(): jnp.einsum('hqd,hkd->hqk', rows_q, key_h, precision=exact_mode)  86.9 us
    reduce_scatter x1, waiting for transfers between devices, shards(): lax.psum_scatter(jnp.dot(row_block, embed_weight, preferred_element_type=...  79 us
    unnamed x298, local copies, waits for them, and re-layouts  52.9 us
    reduce_scatter x1, waiting for transfers between devices, reduce_weights(): lax.psum_scatter(cols_first.astype(jnp.bfloat16), 'dp', scatter_dimension...  45.8 us
    reduce_scatter x1, waiting for transfers between devices, shards(): lax.psum_scatter(jnp.dot(row_block, ffn_down, preferred_element_type=jnp....  44 us
    all_gather x1, waiting for transfers between devices, shards(): mix_full = lax.all_gather(mix_grad, 'tp', axis=0, tiled=True)  42.7 us
    reduce_scatter x1, waiting for transfers between devices, shards(): lax.psum_scatter(lax.dot_general(row_block, ffn_weights, contract_last, p...  42.7 us
  transfers between devices with their start and end apart: 12, of which 10 were waited for; matrix products, arithmetic and copies ran while one was open for 10% of the time, Pallas kernels for 0%

commit v1 on v0

v1 whole, which is shorter than its diff:
```python
import functools

import jax
import jax.numpy as jnp
from jax import lax
from jax.experimental import pallas as pl
from jax.experimental.pallas import tpu as pltpu
from jax.sharding import PartitionSpec as P

f32 = jnp.float32
bf16 = jnp.bfloat16
eps = 1e-05
NST = 128
LOG2E = 1.4426950408889634
LOW = -1e30
NN = ((1,), (0,))
NT = ((1,), (1,))
TN = ((0,), (0,))
PROJ = 2048
STEPS = 8


def mm(a, b, dims=NN):
    return lax.dot_general(a, b, (dims, ((), ())), preferred_element_type=f32)


def mmx(a, b, dims=NN):
    return lax.dot_general(
        a, b, (dims, ((), ())), preferred_element_type=f32, precision=lax.Precision.HIGHEST
    )


def iota(shape, axis):
    return lax.broadcasted_iota(jnp.int32, shape, axis)


def expand(v):
    low_half = iota((1, 128), 1) < 64
    return jnp.concatenate(
        [
            jnp.where(low_half, v[:, h : h + 1], v[:, h + 1 : h + 2])
            for h in range(0, v.shape[1], 2)
        ],
        axis=1,
    )


def head_sum(v):
    owner = (iota((512, 8), 0) // 64 == iota((512, 8), 1)).astype(f32)
    return mmx(v, owner)


def softplus(v):
    return jnp.maximum(v, 0.0) + jnp.log1p(jnp.exp(-jnp.abs(v)))


def tile4(v):
    return jnp.concatenate([v, v, v, v], axis=1)


def fill_segments(seg_ref, segcol):
    length = seg_ref.shape[1]
    segcol[0:8, :] = jnp.full((8, 128), -1.0, f32)
    segcol[length + 8 : length + 16, :] = jnp.full((8, 128), -2.0, f32)
    for row in range(0, length, 128):
        piece = jnp.broadcast_to(seg_ref[0:1, row : row + 128], (128, 128))
        segcol[8 + row : 8 + row + 128, :] = piece.T


def taps_of(taps, tile):
    if tile < 4:
        return taps[0][:, tile * 128 : tile * 128 + 128]
    return taps[tile - 3][...]


def conv_masks(rows, segx):
    here = segx[8 : 8 + rows, :]
    return [(segx[8 - lag : 8 - lag + rows, :] == here).astype(f32) for lag in (1, 2, 3)]


def conv_pre(tile, rows, uext, masks, taps):
    lanes = slice(tile * 128, tile * 128 + 128)
    w = taps_of(taps, tile)
    lags = [uext[8 : 8 + rows, lanes]]
    for lag in (1, 2, 3):
        lags.append(uext[8 - lag : 8 - lag + rows, lanes] * masks[lag - 1])
    pre = lags[0] * w[0:1, :]
    for lag in (1, 2, 3):
        pre = pre + lags[lag] * w[lag : lag + 1, :]
    return pre, lags


def load_inputs(first, rows, proj, segcol, uext, segx):
    @pl.when(first == 0)
    def _():
        uext[0:8, :] = jnp.zeros((8, 768), f32)

    @pl.when(first > 0)
    def _():
        uext[0:8, :] = proj[pl.ds(pl.multiple_of(first - 16, 16), 16), 512:1280].astype(f32)[8:16]

    uext[8 : 8 + rows, :] = proj[pl.ds(first, rows), 512:1280].astype(f32)
    segx[...] = segcol[pl.ds(first, rows + 16), :]


def decays(first, rows, step, bias, rate):
    raw = step[pl.ds(first, rows), :] + bias[...]
    size = softplus(raw)
    logs = size * -jnp.exp(rate[...])
    scaled = logs * LOG2E
    lower = (iota((rows, rows), 0) >= iota((rows, rows), 1)).astype(f32)
    cum = mmx(lower, scaled)
    wide = jnp.concatenate([cum, jnp.zeros((rows, 120), f32)], axis=1)
    return raw, size, logs, cum, wide.T[0:8, :]


def half_masks():
    low_half = iota((1, 128), 1) < 64
    return low_half, jnp.logical_not(low_half)


def keep(mask, v):
    return jnp.where(mask, v, jnp.zeros_like(v))


def mixer_fwd_chunk(
    index, rows, proj, step, seg, segcol, taps, bias, rate, skip, gain, uext, segx, state,
    oacc, stats, mix_out, ssd_out, states_out, lse_out,
):
    first = pl.multiple_of(index * rows, rows)
    here = pl.ds(first, rows)
    halves = half_masks()
    load_inputs(first, rows, proj, segcol, uext, segx)
    masks = conv_masks(rows, segx)
    acts = []
    for tile in range(6):
        pre, _ = conv_pre(tile, rows, uext, masks, taps)
        acts.append(pre * jax.nn.sigmoid(pre))
    xc = jnp.concatenate(acts[0:4], axis=1)
    bc, cc = acts[4].astype(bf16), acts[5].astype(bf16)
    _, size, _, cum, cumr = decays(first, rows, step, bias, rate)
    segc = segx[8 : 8 + rows, :]
    before = segx[7:8, :]
    goes_on = (segc == before).astype(f32)
    segr = seg[0:1, here]
    wide_seg = jnp.concatenate([segc] * (rows // 128), axis=1)
    allowed = (iota((rows, rows), 0) >= iota((rows, rows), 1)) & (wide_seg == segr)
    away = jnp.where(allowed, 0.0, LOW)
    cb = mm(cc, bc, NT)
    xs = xc * expand(size)
    xsb = xs.astype(bf16)
    parts = []
    for pair in range(4):
        lhs = []
        for h in (2 * pair, 2 * pair + 1):
            gap = cum[:, h : h + 1] - cumr[h : h + 1, :] + away
            lhs.append((cb * jnp.exp2(gap)).astype(bf16))
        xp = xsb[:, pair * 128 : pair * 128 + 128]
        rhs = jnp.concatenate([keep(halves[0], xp), keep(halves[1], xp)], axis=0)
        parts.append(mm(jnp.concatenate(lhs, axis=1), rhs))
    ssd = jnp.concatenate(parts, axis=1) + xc * expand(skip[...])
    st = state[...]
    stb = st.astype(bf16)
    states_out[index] = stb
    ssd = ssd + mm(cc, stb) * expand(jnp.exp2(cum)) * tile4(goes_on)
    last = cum[rows - 1 : rows, :]
    fits = (segc == segc[rows - 1 : rows, :]).astype(f32)
    weight = expand(jnp.exp2(last - cum)) * tile4(fits)
    added = mm(bc, (xs * weight).astype(bf16), TN)
    passes = (segc[rows - 1 : rows, :] == before).astype(f32)
    state[...] = st * (expand(jnp.exp2(last)) * tile4(passes)) + added
    ssd_out[here, :] = ssd.astype(bf16)
    z = proj[here, 0:512].astype(f32)
    g = ssd * (z * jax.nn.sigmoid(z))
    r = lax.rsqrt(jnp.mean(g * g, axis=1, keepdims=True) + eps)
    mix_out[here, 0:512] = (g * r * gain[...]).astype(bf16)
    own_seg = seg[0:1, here]

    def keys(block, fresh):
        start = pl.multiple_of(block * rows, rows)
        away = attention_away(start, first, rows, own_seg, segcol)
        for pair in range(2):
            lanes = pair * 128
            q = proj[here, 1280 + lanes : 1408 + lanes] * jnp.asarray(0.125, bf16)
            k = proj[pl.ds(start, rows), 1536 + lanes : 1664 + lanes]
            v = proj[pl.ds(start, rows), 1792 + lanes : 1920 + lanes]
            for half in range(2):
                h = 2 * pair + half
                mine = slice(h * 64, h * 64 + 64)
                s = mm(k, keep(halves[half], q), NT) + away
                peak = jnp.max(s, axis=0, keepdims=True)
                if not fresh:
                    old = stats[h : h + 1, :]
                    peak = jnp.maximum(peak, old)
                    fade = jnp.exp(old - peak)
                p = jnp.exp(s - peak)
                total = jnp.sum(p, axis=0, keepdims=True)
                o = mm(v, p.astype(bf16), TN)[half * 64 : half * 64 + 64, :]
                if not fresh:
                    total = total + stats[h + 4 : h + 5, :] * fade
                    o = o + oacc[mine, :] * fade
                stats[h : h + 1, :] = peak
                stats[h + 4 : h + 5, :] = total
                oacc[mine, :] = o

    keys(index, True)

    def earlier(block, _):
        keys(block, False)
        return 0

    lax.fori_loop(0, index, earlier, 0)
    lse_out[0:4, here] = stats[0:4, :] + jnp.log(stats[4:8, :])
    for h in range(4):
        mine = slice(h * 64, h * 64 + 64)
        oacc[mine, :] = oacc[mine, :] * (1.0 / stats[h + 4 : h + 5, :])
    for pair in range(2):
        mine = slice(pair * 128, pair * 128 + 128)
        mix_out[here, 512 + pair * 128 : 640 + pair * 128] = oacc[mine, :].T.astype(bf16)


def attention_away(start, first, rows, own_seg, segcol):
    key_seg = segcol[pl.ds(start + 8, rows), :]
    wide = jnp.concatenate([key_seg] * (rows // 128), axis=1)
    allowed = (wide == own_seg) & (
        iota((rows, rows), 0) + start <= iota((rows, rows), 1) + first
    )
    return jnp.where(allowed, 0.0, LOW)


def mixer_bwd_chunk(
    index, rows, proj, step, seg, segcol, taps, bias, rate, skip, gain, uext, segx, dext,
    dstate, dkv, dqs, mix, ssd_in, states_in, lse_in, dmix, dproj, dstep, dtaps, dheads, dgain, dskip,
):
    first = pl.multiple_of(index * rows, rows)
    here = pl.ds(first, rows)
    halves = half_masks()
    load_inputs(first, rows, proj, segcol, uext, segx)
    masks = conv_masks(rows, segx)
    acts = []
    for tile in range(6):
        pre, _ = conv_pre(tile, rows, uext, masks, taps)
        acts.append(pre * jax.nn.sigmoid(pre))
    xc = jnp.concatenate(acts[0:4], axis=1)
    bc, cc = acts[4].astype(bf16), acts[5].astype(bf16)
    raw, size, logs, cum, cumr = decays(first, rows, step, bias, rate)
    z = proj[here, 0:512].astype(f32)
    ssd = ssd_in[here, :].astype(f32)
    dmo = dmix[here, 0:512].astype(f32)
    sig = jax.nn.sigmoid(z)
    act = z * sig
    g = ssd * act
    r = lax.rsqrt(jnp.mean(g * g, axis=1, keepdims=True) + eps)
    gain_part = jnp.sum(dmo * g * r, axis=0, keepdims=True)
    a = dmo * gain[...]
    dg = r * a - (r * r * r) * g * jnp.mean(a * g, axis=1, keepdims=True)
    dssd = dg * act
    dproj[here, 0:512] = (dg * ssd * (sig * (1.0 + z * (1.0 - sig)))).astype(bf16)
    skip_part = jnp.sum(dssd * xc, axis=0, keepdims=True)
    dxc = dssd * expand(skip[...])
    dyb = dssd.astype(bf16)
    wide_size = expand(size)
    xs = xc * wide_size
    xsb = xs.astype(bf16)
    segc = segx[8 : 8 + rows, :]
    before = segx[7:8, :]
    goes_on = (segc == before).astype(f32)
    segr = seg[0:1, here]
    wide_seg = jnp.concatenate([segc] * (rows // 128), axis=1)
    allowed = (iota((rows, rows), 0) <= iota((rows, rows), 1)) & (wide_seg == segr)
    away = jnp.where(allowed, 0.0, LOW)
    cbt = mm(bc, cc, NT)
    dcbt = jnp.zeros((rows, rows), f32)
    to_rows = []
    from_rows = jnp.zeros((rows, 8), f32)
    parts = []
    for pair in range(4):
        lanes = slice(pair * 128, pair * 128 + 128)
        lhs, rhs = [], []
        for half in range(2):
            h = 2 * pair + half
            lt = jnp.exp2(cumr[h : h + 1, :] - cum[:, h : h + 1] + away)
            mt = cbt * lt
            lhs.append(mt.astype(bf16))
            rhs.append(keep(halves[half], dyb[:, lanes]))
            dl = mm(keep(halves[half], xsb[:, lanes]), dyb[:, lanes], NT)
            dcbt = dcbt + dl * lt
            gt = dl * mt
            to_rows.append(jnp.sum(gt, axis=0, keepdims=True))
            from_rows = jnp.where(
                iota((1, 8), 1) == h, jnp.sum(gt, axis=1, keepdims=True), from_rows
            )
        parts.append(mm(jnp.concatenate(lhs, axis=1), jnp.concatenate(rhs, axis=0)))
    dxs = jnp.concatenate(parts, axis=1)
    dcb = dcbt.astype(bf16)
    db = mm(dcb, cc)
    dc = mm(dcb, bc, TN)
    upper = (iota((rows, rows), 0) <= iota((rows, rows), 1)).astype(f32)
    late = -from_rows
    reach = expand(jnp.exp2(cum)) * tile4(goes_on)
    stb = states_in[index]
    dye = dssd * reach
    dyeb = dye.astype(bf16)
    dc = dc + mm(dyeb, stb, NT)
    late = late + head_sum(dye * mm(cc, stb))
    into_state = mm(cc, dyeb, TN)
    last = cum[rows - 1 : rows, :]
    fits = (segc == segc[rows - 1 : rows, :]).astype(f32)
    weight = expand(jnp.exp2(last - cum)) * tile4(fits)
    dst = dstate[...]
    dsb = dst.astype(bf16)
    dxi = mm(bc, dsb) * weight
    dxs = dxs + dxi
    db = db + mm((xs * weight).astype(bf16), dsb, NT)
    strict = (iota((rows, rows), 0) > iota((rows, rows), 1)).astype(f32)
    dlog = mmx(strict, head_sum(xs * dxi))
    passes = (segc[rows - 1 : rows, :] == before).astype(f32)
    fade = expand(jnp.exp2(last)) * tile4(passes)
    through = jnp.sum(stb.astype(f32) * dst, axis=0, keepdims=True) * fade
    dlog = dlog + head_sum(jnp.broadcast_to(through, (8, 512)))[0:1, :]
    dstate[...] = dst * fade + into_state
    dlog = dlog + mmx(upper, late) + mmx(upper, jnp.concatenate(to_rows, axis=0), NT)
    dsize = head_sum(dxs * xc) - dlog * jnp.exp(rate[...])
    rate_part = jnp.sum(dlog * logs, axis=0, keepdims=True)
    draw = dsize * jax.nn.sigmoid(raw)
    bias_part = jnp.sum(draw, axis=0, keepdims=True)
    dstep[here, :] = draw.astype(dstep.dtype)
    dxc = dxc + dxs * wide_size
    dacts = [dxc[:, t * 128 : t * 128 + 128] for t in range(4)] + [db, dc]
    dext[rows : rows + 8, :] = dext[0:8, :]
    ahead = [(segx[8 + lag : 8 + lag + rows, :] == segc).astype(f32) for lag in (1, 2, 3)]
    for tile in range(6):
        lanes = slice(tile * 128, tile * 128 + 128)
        w = taps_of(taps, tile)
        pre, lags = conv_pre(tile, rows, uext, masks, taps)
        sig = jax.nn.sigmoid(pre)
        dpre = dacts[tile] * (sig * (1.0 + pre * (1.0 - sig)))
        dext[0:rows, lanes] = dpre
        du = dpre * w[0:1, :]
        for lag in (1, 2, 3):
            du = du + dext[lag : lag + rows, lanes] * ahead[lag - 1] * w[lag : lag + 1, :]
        dproj[here, 512 + tile * 128 : 640 + tile * 128] = du.astype(bf16)
        sums = jnp.concatenate(
            [jnp.sum(dpre * shifted, axis=0, keepdims=True) for shifted in lags], axis=0
        )
        dtaps[:, lanes] = dtaps[:, lanes] + sums
    head_parts = jnp.concatenate([bias_part, rate_part], axis=0)
    dheads[...] = dheads[...] + head_parts
    dgain[...] = dgain[...] + gain_part
    dskip[...] = dskip[...] + skip_part
    own_seg = seg[0:1, here]
    dos = [dmix[here, 512 + pair * 128 : 640 + pair * 128] for pair in range(2)]
    owner = (iota((8, 256), 1) // 64 == iota((8, 256), 0)).astype(f32)
    delta = mmx(
        owner,
        jnp.concatenate(dos, axis=1).astype(f32) * mix[here, 512:768].astype(f32),
        NT,
    )
    dqs[...] = jnp.zeros_like(dqs)

    def keys(block, _):
        start = pl.multiple_of(block * rows, rows)
        there = pl.ds(start, rows)
        away = attention_away(start, first, rows, own_seg, segcol)
        for pair in range(2):
            lanes = pair * 128
            q = proj[here, 1280 + lanes : 1408 + lanes] * jnp.asarray(0.125, bf16)
            k = proj[there, 1536 + lanes : 1664 + lanes]
            v = proj[there, 1792 + lanes : 1920 + lanes]
            ps, dss, qms, doms = [], [], [], []
            for half in range(2):
                h = 2 * pair + half
                mine = slice(h * 64, h * 64 + 64)
                qm, dom = keep(halves[half], q), keep(halves[half], dos[pair])
                p = jnp.exp(mm(k, qm, NT) + away - lse_in[h : h + 1, here])
                dp = mm(v, dom, NT)
                ds = (p * (dp - delta[h : h + 1, :])).astype(bf16)
                dqs[mine, :] = dqs[mine, :] + mm(k, ds, TN)[half * 64 : half * 64 + 64, :]
                ps.append(p.astype(bf16))
                dss.append(ds)
                qms.append(qm)
                doms.append(dom)
            kl, vl = slice(lanes, lanes + 128), slice(256 + lanes, 384 + lanes)
            dkv[there, kl] = dkv[there, kl] + mm(
                jnp.concatenate(dss, axis=1), jnp.concatenate(qms, axis=0)
            )
            dkv[there, vl] = dkv[there, vl] + mm(
                jnp.concatenate(ps, axis=1), jnp.concatenate(doms, axis=0)
            )
        return 0

    lax.fori_loop(0, index + 1, keys, 0)
    for pair in range(2):
        mine = slice(pair * 128, pair * 128 + 128)
        dproj[here, 1280 + pair * 128 : 1408 + pair * 128] = (dqs[mine, :] * 0.125).T.astype(bf16)
    dproj[here, 1536:2048] = dkv[here, :].astype(bf16)


def fwd_kernel(count, proj, step, seg, t0, t1, t2, bias, rate, skip, gain,
               mix_out, ssd_out, states_out, lse_out, segcol, uext, segx, state, oacc, stats):
    rows = proj.shape[0] // count
    fill_segments(seg, segcol)
    lse_out[...] = jnp.zeros_like(lse_out)
    state[...] = jnp.zeros_like(state)

    def chunk(index, _):
        mixer_fwd_chunk(index, rows, proj, step, seg, segcol, (t0, t1, t2), bias, rate, skip,
                        gain, uext, segx, state, oacc, stats, mix_out, ssd_out, states_out,
                        lse_out)
        return 0

    lax.fori_loop(0, count, chunk, 0)


def bwd_kernel(count, proj, step, seg, t0, t1, t2, bias, rate, skip, gain, mix, ssd_in,
               states_in, lse_in, dmix, dproj, dstep, dtaps, dheads, dgain, dskip,
               segcol, uext, segx, dext, dstate, dkv, dqs):
    rows = proj.shape[0] // count
    fill_segments(seg, segcol)
    for ref in (dtaps, dheads, dgain, dskip, dstate, dkv):
        ref[...] = jnp.zeros_like(ref)
    dext[0:8, :] = jnp.zeros((8, 768), f32)

    def chunk(turn, _):
        mixer_bwd_chunk(count - 1 - turn, rows, proj, step, seg, segcol, (t0, t1, t2), bias,
                        rate, skip, gain, uext, segx, dext, dstate, dkv, dqs, mix, ssd_in,
                        states_in, lse_in, dmix, dproj, dstep, dtaps, dheads, dgain, dskip)
        return 0

    lax.fori_loop(0, count, chunk, 0)
    dskip8 = head_sum(jnp.broadcast_to(dskip[...], (8, 512)))
    dskip[0:1, 0:8] = dskip8[0:1, :]


def mixer_fwd(count, proj, step, seg, taps, bias, rate, skip, gain):
    length = proj.shape[0]
    rows = length // count
    return pl.pallas_call(
        functools.partial(fwd_kernel, count),
        out_shape=(
            jax.ShapeDtypeStruct((length, 768), bf16),
            jax.ShapeDtypeStruct((length, 512), bf16),
            jax.ShapeDtypeStruct((count, NST, 512), bf16),
            jax.ShapeDtypeStruct((8, length), f32),
        ),
        scratch_shapes=[
            pltpu.VMEM((length + 16, 128), f32),
            pltpu.VMEM((rows + 8, 768), f32),
            pltpu.VMEM((rows + 16, 128), f32),
            pltpu.VMEM((NST, 512), f32),
            pltpu.VMEM((256, rows), f32),
            pltpu.VMEM((8, rows), f32),
        ],
        compiler_params=pltpu.CompilerParams(vmem_limit_bytes=60 * 2**20),
    )(proj, step, seg, *taps, bias, rate, skip, gain)


def mixer_bwd(count, proj, step, seg, taps, bias, rate, skip, gain, mix, ssd, states, lse, dmix):
    length = proj.shape[0]
    rows = length // count
    return pl.pallas_call(
        functools.partial(bwd_kernel, count),
        out_shape=(
            jax.ShapeDtypeStruct((length, 2048), bf16),
            jax.ShapeDtypeStruct((length, 8), bf16),
            jax.ShapeDtypeStruct((4, 768), f32),
            jax.ShapeDtypeStruct((2, 8), f32),
            jax.ShapeDtypeStruct((1, 512), f32),
            jax.ShapeDtypeStruct((1, 512), f32),
        ),
        scratch_shapes=[
            pltpu.VMEM((length + 16, 128), f32),
            pltpu.VMEM((rows + 8, 768), f32),
            pltpu.VMEM((rows + 16, 128), f32),
            pltpu.VMEM((rows + 8, 768), f32),
            pltpu.VMEM((NST, 512), f32),
            pltpu.VMEM((length, 512), f32),
            pltpu.VMEM((256, rows), f32),
        ],
        compiler_params=pltpu.CompilerParams(vmem_limit_bytes=60 * 2**20),
    )(proj, step, seg, *taps, bias, rate, skip, gain, mix, ssd, states, lse, dmix)


MESH = pl.DeviceIdType.MESH


class Line:
    def __init__(self, scratch, size):
        (self.own, self.left, self.right, self.full, self.acc,
         self.ss, self.sr, self.gs, self.gr) = scratch
        self.size = size
        self.steps = self.own.shape[1]
        self.me = lax.axis_index("tp")
        self.last = size - 1

    @staticmethod
    def scratch(size, steps, sub, width):
        return [
            pltpu.VMEM((size, steps, sub, width), f32),
            pltpu.VMEM((size, steps, sub, width), bf16),
            pltpu.VMEM((size, steps, sub, width), bf16),
            pltpu.VMEM((size, steps, sub, width), bf16),
            pltpu.VMEM((sub, width), f32),
            pltpu.SemaphoreType.DMA((2, size, steps)),
            pltpu.SemaphoreType.DMA((2, size, steps)),
            pltpu.SemaphoreType.DMA((2, size, steps)),
            pltpu.SemaphoreType.DMA((2, size, steps)),
        ]

    def sum_copy(self, way, d, j):
        buf = self.left if way == 0 else self.right
        return pltpu.make_async_remote_copy(
            src_ref=buf.at[d, j],
            dst_ref=buf.at[d, j],
            send_sem=self.ss.at[way, d, j],
            recv_sem=self.sr.at[way, d, j],
            device_id={"tp": self.me + 1 if way == 0 else self.me - 1},
            device_id_type=MESH,
        )

    def row_copy(self, way, d, j):
        return pltpu.make_async_remote_copy(
            src_ref=self.full.at[d, j],
            dst_ref=self.full.at[d, j],
            send_sem=self.gs.at[way, d, j],
            recv_sem=self.gr.at[way, d, j],
            device_id={"tp": self.me + 1 if way == 0 else self.me - 1},
            device_id_type=MESH,
        )

    def enter(self):
        barrier = pltpu.get_barrier_semaphore()
        me, last = self.me, self.last

        @pl.when(me > 0)
        def _():
            pl.semaphore_signal(barrier, inc=1, device_id={"tp": me - 1}, device_id_type=MESH)

        @pl.when(me < last)
        def _():
            pl.semaphore_signal(barrier, inc=1, device_id={"tp": me + 1}, device_id_type=MESH)

        peers = jnp.where(me > 0, 1, 0) + jnp.where(me < last, 1, 0)
        pl.semaphore_wait(barrier, peers)

    def relay(self, way, j):
        me, last = self.me, self.last
        buf = self.left if way == 0 else self.right
        first_one = me == 0 if way == 0 else me == last

        def one(d, _):
            @pl.when(first_one)
            def _():
                buf[d, j] = self.own[d, j].astype(bf16)

            @pl.when(jnp.logical_not(first_one))
            def _():
                self.sum_copy(way, d, j).wait_recv()
                buf[d, j] = (buf[d, j].astype(f32) + self.own[d, j]).astype(bf16)

            self.sum_copy(way, d, j).start()
            return 0

        if way == 0:
            lax.fori_loop(me + 1, self.size, one, 0)
        else:
            lax.fori_loop(0, me, one, 0)

    def settle(self, j, finish):
        me, last = self.me, self.last
        self.acc[...] = self.own[me, j]

        @pl.when(me > 0)
        def _():
            self.sum_copy(0, me, j).wait_recv()
            self.acc[...] = self.acc[...] + self.left[me, j].astype(f32)

        @pl.when(me < last)
        def _():
            self.sum_copy(1, me, j).wait_recv()
            self.acc[...] = self.acc[...] + self.right[me, j].astype(f32)

        self.full[me, j] = finish(j, self.acc[...])

        @pl.when(me < last)
        def _():
            self.row_copy(0, me, j).start()

        @pl.when(me > 0)
        def _():
            self.row_copy(1, me, j).start()

    def inside(self, j):
        return jnp.logical_and(j >= 0, j < self.steps)

    def pass_on(self, i):
        me, last = self.me, self.last

        def from_left(d, _):
            j = i - jnp.maximum(d, last - d) - (me - d)

            @pl.when(self.inside(j))
            def _():
                self.row_copy(0, d, j).wait_recv()

                @pl.when(me < last)
                def _():
                    self.row_copy(0, d, j).start()

            return 0

        def from_right(d, _):
            j = i - jnp.maximum(d, last - d) - (d - me)

            @pl.when(self.inside(j))
            def _():
                self.row_copy(1, d, j).wait_recv()

                @pl.when(me > 0)
                def _():
                    self.row_copy(1, d, j).start()

            return 0

        lax.fori_loop(0, me, from_left, 0)
        lax.fori_loop(me + 1, self.size, from_right, 0)

    def move(self, i, finish):
        me, last = self.me, self.last
        right_step = i - me
        left_step = i - (last - me)
        final_step = i - jnp.maximum(me, last - me)

        @pl.when(self.inside(right_step))
        def _():
            self.relay(0, right_step)

        @pl.when(self.inside(left_step))
        def _():
            self.relay(1, left_step)

        @pl.when(self.inside(final_step))
        def _():
            self.settle(final_step, finish)

        self.pass_on(i)

    def ready_step(self, i):
        return i - self.last - jnp.maximum(self.me, self.last - self.me)

    def lag(self):
        return 2 * self.last

    def leave(self):
        me, last = self.me, self.last

        def step(j, _):
            def right_sums(d, _):
                self.sum_copy(0, d, j).wait_send()
                return 0

            def left_sums(d, _):
                self.sum_copy(1, d, j).wait_send()
                return 0

            def right_rows(d, _):
                self.row_copy(0, d, j).wait_send()
                return 0

            def left_rows(d, _):
                self.row_copy(1, d, j).wait_send()
                return 0

            lax.fori_loop(me + 1, self.size, right_sums, 0)
            lax.fori_loop(0, me, left_sums, 0)

            @pl.when(me < last)
            def _():
                lax.fori_loop(0, me + 1, right_rows, 0)

            @pl.when(me > 0)
            def _():
                lax.fori_loop(me, self.size, left_rows, 0)

            return 0

        lax.fori_loop(0, self.steps, step, 0)


def flat(v):
    return v.reshape(v.shape[0] * v.shape[1], v.shape[2])


def normed(v, gain):
    return v * lax.rsqrt(jnp.mean(v * v, axis=1, keepdims=True) + eps) * gain


def normed_back(grad, v, gain):
    r = lax.rsqrt(jnp.mean(v * v, axis=1, keepdims=True) + eps)
    a = grad * gain
    back = r * a - (r * r * r) * v * jnp.mean(a * v, axis=1, keepdims=True)
    return back, jnp.sum(grad * v * r, axis=0, keepdims=True)


def embed_kernel(size, patches, embed, keep_rows, gain, wz, wx, wb, wc, wq, wk, wv, ws,
                 resid_out, full_out, proj_out, step_out, *scratch):
    line = Line(scratch, size)
    steps, sub = line.steps, line.own.shape[2]
    columns = []
    for ref in (wz, wx, wb, wc, wq, wk, wv):
        columns.append((ref, sum(c[0].shape[1] for c in columns)))

    def produce(j):
        line.own[:, j] = mm(flat(patches[:, j]), embed[...]).reshape(size, sub, line.own.shape[3])

    def finish(j, total):
        rows = total * keep_rows[j]
        resid_out[j] = rows
        return normed(rows, gain[...]).astype(bf16)

    def consume(j):
        x = line.full[:, j]
        full_out[:, j] = x
        x = flat(x)
        for ref, start in columns:
            width = ref.shape[1]
            proj_out[:, j, :, start : start + width] = (
                mm(x, ref[...]).astype(bf16).reshape(size, sub, width)
            )
        step_out[:, j] = mm(x, ws[...]).reshape(size, sub, ws.shape[1])

    line.enter()
    produce(0)

    def iteration(i, _):
        line.move(i, finish)

        @pl.when(i + 1 < steps)
        def _():
            produce(i + 1)

        ready = line.ready_step(i)

        @pl.when(line.inside(ready))
        def _():
            consume(ready)

        return 0

    lax.fori_loop(0, steps + line.lag(), iteration, 0)
    line.leave()


def ffn_kernel(size, mix, wmo, wao, resid_one, gain, wg, wu, wd, og_full, og_mine,
               resid_grad, full_out, hidden_out, gg_out, ug_out, ffn_out, resid_out, mixg_out,
               dmix, gain_grad, *scratch):
    half = len(scratch) // 2
    one, two = Line(scratch[:half], size), Line(scratch[half:], size)
    steps, sub, width = one.steps, one.own.shape[2], one.own.shape[3]
    inner = wmo.shape[0]

    def shaped(v):
        return v.reshape(size, sub, v.shape[1])

    def produce(j):
        x = flat(mix[:, j])
        one.own[:, j] = shaped(mm(x[:, 0:inner], wmo[...]) + mm(x[:, inner:], wao[...]))

    def finish_one(j, total):
        rows = resid_one[j] + total
        resid_out[j] = rows
        return normed(rows, gain[...]).astype(bf16)

    def middle(j):
        x = one.full[:, j]
        full_out[:, j] = x
        x = flat(x)
        og = flat(og_full[:, j])
        gate, up = mm(x, wg[...]), mm(x, wu[...])
        hg = mm(og, wd[...], NT)
        sig = jax.nn.sigmoid(gate)
        act = gate * sig
        hidden = (act * up).astype(bf16)
        gg = (hg * up * (sig * (1.0 + gate * (1.0 - sig)))).astype(bf16)
        ug = (hg * act).astype(bf16)
        hidden_out[:, j] = shaped(hidden)
        gg_out[:, j] = shaped(gg)
        ug_out[:, j] = shaped(ug)
        two.own[:, j] = shaped(mm(gg, wg[...], NT) + mm(ug, wu[...], NT))
        ffn_out[:, j] = shaped(mm(hidden, wd[...]).astype(bf16))

    def finish_two(j, total):
        back, part = normed_back(total, resid_out[j], gain[...])
        rows = og_mine[j].astype(f32) + back
        resid_grad[j] = rows
        gain_grad[...] = gain_grad[...] + part
        return rows.astype(bf16)

    def consume(j):
        x = two.full[:, j]
        mixg_out[:, j] = x
        x = flat(x)
        dmix[:, j, :, 0:inner] = shaped(mm(x, wmo[...], NT).astype(bf16))
        dmix[:, j, :, inner:] = shaped(mm(x, wao[...], NT).astype(bf16))

    one.enter()
    gain_grad[...] = jnp.zeros_like(gain_grad)
    produce(0)
    lag = one.lag() + 1

    def iteration(i, _):
        one.move(i, finish_one)
        two.move(i - lag, finish_two)

        @pl.when(i + 1 < steps)
        def _():
            produce(i + 1)

        ready_one = one.ready_step(i)

        @pl.when(one.inside(ready_one))
        def _():
            middle(ready_one)

        ready_two = two.ready_step(i - lag)

        @pl.when(two.inside(ready_two))
        def _():
            consume(ready_two)

        return 0

    lax.fori_loop(0, steps + lag + two.lag(), iteration, 0)
    one.leave()
    two.leave()


def entry_kernel(size, dproj, dstep, wz, wx, wb, wc, wq, wk, wv, ws, resid_one, gain, resid_grad,
                 keep_rows, embed, eg_out, patch_grad, gain_grad, *scratch):
    line = Line(scratch, size)
    steps, sub = line.steps, line.own.shape[2]
    columns = []
    for ref in (wz, wx, wb, wc, wq, wk, wv):
        columns.append((ref, sum(c[0].shape[1] for c in columns)))

    def produce(j):
        total = mm(flat(dstep[:, j]), ws[...], NT)
        for ref, start in columns:
            total = total + mm(flat(dproj[:, j, :, start : start + ref.shape[1]]), ref[...], NT)
        line.own[:, j] = total.reshape(size, sub, total.shape[1])

    def finish(j, total):
        back, part = normed_back(total, resid_one[j], gain[...])
        gain_grad[...] = gain_grad[...] + part
        return ((resid_grad[j] + back) * keep_rows[j]).astype(bf16)

    def consume(j):
        x = line.full[:, j]
        eg_out[:, j] = x
        patch_grad[:, j] = (
            mm(flat(x), embed[...], NT).astype(bf16).reshape(size, sub, embed.shape[0])
        )

    line.enter()
    gain_grad[...] = jnp.zeros_like(gain_grad)
    produce(0)

    def iteration(i, _):
        line.move(i, finish)

        @pl.when(i + 1 < steps)
        def _():
            produce(i + 1)

        ready = line.ready_step(i)

        @pl.when(line.inside(ready))
        def _():
            consume(ready)

        return 0

    lax.fori_loop(0, steps + line.lag(), iteration, 0)
    line.leave()


def comm_call(body, out_shape, scratch, identity, *args):
    return pl.pallas_call(
        body,
        out_shape=out_shape,
        in_specs=[pl.BlockSpec(memory_space=pltpu.VMEM)] * len(args),
        out_specs=tuple(pl.BlockSpec(memory_space=pltpu.VMEM) for _ in out_shape),
        scratch_shapes=scratch,
        compiler_params=pltpu.CompilerParams(
            collective_id=identity, has_side_effects=True, vmem_limit_bytes=62 * 2**20
        ),
    )(*args)


def sds(shape, kind):
    return jax.ShapeDtypeStruct(shape, kind)


def split_parts(matrix, widths, axis):
    pieces_out = []
    offset = 0
    for width in widths:
        pieces_out.append(lax.slice_in_dim(matrix, offset, offset + width, axis=axis))
        offset = offset + width
    return pieces_out


def reduce_weights(rows_first, cols_first):
    return (
        lax.psum_scatter(
            rows_first.astype(jnp.bfloat16), "dp", scatter_dimension=0, tiled=True
        ).astype(jnp.float32),
        lax.psum_scatter(
            cols_first.astype(jnp.bfloat16), "dp", scatter_dimension=1, tiled=True
        ).astype(jnp.float32),
    )


def shards(
    patches,
    keep_mask,
    segments,
    embed_weight,
    first_gain,
    mamba_gate,
    mamba_input,
    state_in,
    state_out,
    step_weight,
    conv_input,
    conv_statein,
    conv_stateout,
    step_bias,
    rate_log,
    skip_gain,
    inner_gain,
    mamba_output,
    query_weight,
    key_weight,
    value_weight,
    attn_output,
    second_gain,
    ffn_gate,
    ffn_up,
    ffn_down,
    out_grad,
):
    size = lax.axis_size("tp")
    segment = segments[0]
    length = patches.shape[0]
    mine = length // size
    sub = mine // STEPS
    shape = (size, STEPS, sub)
    width = embed_weight.shape[1]
    keep_rows = keep_mask.astype(f32).reshape(STEPS, sub, 1)
    seg_row = segment.astype(f32)[None]
    taps = (conv_input, conv_statein, conv_stateout)
    core_params = (step_bias[None], rate_log[None], skip_gain[None], inner_gain[None])
    in_list = (
        mamba_gate,
        mamba_input,
        state_in,
        state_out,
        query_weight,
        key_weight,
        value_weight,
        step_weight,
    )
    one_gain, two_gain = first_gain[None], second_gain[None]
    buffers = Line.scratch(size, STEPS, sub, width)
    og_full = lax.all_gather(out_grad, "tp", axis=0, tiled=True)

    resid_one, full_one, projected, step_raw = comm_call(
        functools.partial(embed_kernel, size),
        (
            sds((STEPS, sub, width), f32),
            sds((*shape, width), bf16),
            sds((*shape, PROJ), bf16),
            sds((*shape, step_weight.shape[1]), f32),
        ),
        buffers,
        1,
        patches.reshape(*shape, patches.shape[1]),
        embed_weight,
        keep_rows,
        one_gain,
        *in_list,
    )
    projected = projected.reshape(length, PROJ)
    step_raw = step_raw.reshape(length, step_weight.shape[1])
    mix_in, ssd, states, lse = mixer_fwd(size, projected, step_raw, seg_row, taps, *core_params)
    inner_width = mamba_output.shape[0]
    hidden_width = ffn_gate.shape[1]
    wide = sds((*shape, hidden_width), bf16)
    rows16 = sds((*shape, width), bf16)
    rows32 = sds((STEPS, sub, width), f32)
    (
        resid_grad, full_two, hidden, gate_grad, up_grad, ffn_part, resid_two, mix_full, dmix,
        second_gain_grad,
    ) = comm_call(
        functools.partial(ffn_kernel, size),
        (
            rows32, rows16, wide, wide, wide, rows16, rows32, rows16,
            sds((*shape, mix_in.shape[1]), bf16), sds((1, width), f32),
        ),
        buffers + buffers,
        2,
        mix_in.reshape(*shape, mix_in.shape[1]),
        mamba_output,
        attn_output,
        resid_one,
        two_gain,
        ffn_gate,
        ffn_up,
        ffn_down,
        og_full.reshape(*shape, width),
        out_grad.reshape(STEPS, sub, width),
    )
    ffn_sum = lax.psum_scatter(
        ffn_part.reshape(length, width), "tp", scatter_dimension=0, tiled=True
    )
    result = (resid_two.reshape(mine, width) + ffn_sum.astype(f32)).astype(bf16)

    def rows_of(v):
        return v.reshape(length, v.shape[-1])

    def outer(a, b):
        return mm(rows_of(a), rows_of(b), TN).astype(bf16)

    down_grad = outer(hidden, og_full)
    ffn_gate_part = outer(full_two, gate_grad)
    ffn_up_part = outer(full_two, up_grad)
    mixout_grad = outer(mix_in, mix_full)
    proj_grad, step_grad, dtaps, dheads, dgain, dskip = mixer_bwd(
        size, projected, step_raw, seg_row, taps, *core_params, mix_in, ssd, states, lse,
        rows_of(dmix),
    )
    in_part = jnp.concatenate([outer(full_one, proj_grad), outer(full_one, step_grad)], axis=1)
    embedded_full, patches_grad, first_gain_grad = comm_call(
        functools.partial(entry_kernel, size),
        (rows16, sds((*shape, patches.shape[1]), bf16), sds((1, width), f32)),
        buffers,
        3,
        proj_grad.reshape(*shape, PROJ),
        step_grad.reshape(*shape, step_grad.shape[1]),
        *in_list,
        resid_one,
        one_gain,
        resid_grad,
        keep_rows,
        embed_weight,
    )
    embed_grad = outer(patches, embedded_full)

    def scatter(v, axis):
        return lax.psum_scatter(v, "dp", scatter_dimension=axis, tiled=True).astype(f32)

    ffn_rows = scatter(jnp.concatenate([ffn_gate_part, ffn_up_part], axis=1), 0)
    mid_cols = scatter(jnp.concatenate([mixout_grad, down_grad], axis=0), 1)
    in_rows = scatter(in_part, 0)
    embed_cols = scatter(embed_grad, 1)
    head_sums = lax.psum(
        (
            dtaps[:, 0:512],
            dtaps[:, 512:640],
            dtaps[:, 640:768],
            dheads[0],
            dheads[1],
            dskip[0, 0:8],
            dgain[0],
        ),
        "dp",
    )
    gain_one_sum = lax.psum_scatter(
        first_gain_grad[0], ("dp", "tp"), scatter_dimension=0, tiled=True
    )
    gain_two_sum = lax.psum_scatter(
        second_gain_grad[0], ("dp", "tp"), scatter_dimension=0, tiled=True
    )
    in_parts = split_parts(in_rows, [member.shape[1] for member in in_list], 1)
    ffn_parts = split_parts(ffn_rows, [hidden_width, hidden_width], 1)
    mid_parts = split_parts(mid_cols, [inner_width, attn_output.shape[0], hidden_width], 0)
    return (
        result,
        patches_grad.reshape(length, patches.shape[1]),
        embed_cols,
        gain_one_sum,
        in_parts[0],
        in_parts[1],
        in_parts[2],
        in_parts[3],
        in_parts[7],
        *head_sums,
        mid_parts[0],
        in_parts[4],
        in_parts[5],
        in_parts[6],
        mid_parts[1],
        gain_two_sum,
        ffn_parts[0],
        ffn_parts[1],
        mid_parts[2],
    )


def solution(mesh):
    return jax.shard_map(
        shards,
        mesh=mesh,
        in_specs=(
            P("dp", "tp"),
            P(("dp", "tp")),
            P("dp", None),
            P("tp", None),
            P(),
            P(None, "tp"),
            P(None, "tp"),
            P(None, "tp"),
            P(None, "tp"),
            P(None, "tp"),
            P(None, "tp"),
            P(None, "tp"),
            P(None, "tp"),
            P("tp"),
            P("tp"),
            P("tp"),
            P("tp"),
            P("tp", None),
            P(None, "tp"),
            P(None, "tp"),
            P(None, "tp"),
            P("tp", None),
            P(),
            P(None, "tp"),
            P(None, "tp"),
            P("tp", None),
            P(("dp", "tp"), None),
        ),
        out_specs=(
            P(("dp", "tp"), None),
            P("dp", "tp"),
            P("tp", "dp"),
            P(("dp", "tp")),
            P("dp", "tp"),
            P("dp", "tp"),
            P("dp", "tp"),
            P("dp", "tp"),
            P("dp", "tp"),
            P(None, "tp"),
            P(None, "tp"),
            P(None, "tp"),
            P("tp"),
            P("tp"),
            P("tp"),
            P("tp"),
            P("tp", "dp"),
            P("dp", "tp"),
            P("dp", "tp"),
            P("dp", "tp"),
            P("tp", "dp"),
            P(("dp", "tp")),
            P("dp", "tp"),
            P("dp", "tp"),
            P("tp", "dp"),
        ),
        check_vma=False,
    )
```

time: 1240 us -> 571 us (0.46)
  waiting for transfers between devices: 445 us -> 18.7 us
  matrix products: 390 us -> 29.5 us
  Pallas kernels: 23.7 us -> 382 us
  other arithmetic: 123 us -> 11.4 us
  local copies, waits for them, and re-layouts: 136 us -> 43.8 us
  loops' own time: 36.7 us -> 0 us
    pallas_call x0 -> x5, Pallas kernels: none -> 382 us  [the longest x3 305 us: comm_call(): pl.pallas_call(body, out_shape=out_shape, in_specs=[pl.BlockSpec(memory_s...]
    dot_general x41 -> x7, matrix products: 390 us -> 29.5 us  [mm(): return lax.dot_general(a, b, (dims, ((), ())), preferred_element_type=f32)]
    reduce_scatter x6 -> x3, waiting for transfers between devices: 291 us -> 18 us  [the longest x2 18 us: scatter(): lax.psum_scatter(v, 'dp', scatter_dimension=axis, tiled=True).astype(f32)]
    all_gather x5 -> x1, waiting for transfers between devices: 153 us -> 0.01 us  [shards(): og_full = lax.all_gather(out_grad, 'tp', axis=0, tiled=True)]
    reduce_sum x16 -> x0, other arithmetic: 50.8 us -> none  [the longest x2 13.4 us: attend_rows(): weights = jnp.exp(scores - peak)]
    another operation x4 -> x0, loops' own time: 36.7 us -> none  [the longest x2 32.5 us: mixer_core(): attn_out = lax.map(jax.checkpoint(attend_rows), blocks)]
    unnamed x2 -> x0, Pallas kernels: 23.7 us -> none
    unnamed x298 -> x40, local copies, waits for them, and re-layouts: 52.9 us -> 33.6 us
  transfers between devices with their start and end apart: 12 -> 6, of which waited for: 10 -> 1; matrix products, arithmetic and copies ran while one was open for 10% -> 12% of each run, Pallas kernels for 0% -> 46%
where the time goes in v1:
time: 571 us; the launch traced here: 564 us
  Pallas kernels  382 us (67%)
  blocking collectives  63.1 us (11%)
  local copies, waits for them, and re-layouts  43.8 us (8%)
  matrix products  29.5 us (5%)
  waiting for transfers between devices  18.7 us (3%)
  between operations  14.5 us (3%)
  other arithmetic  11.4 us (2%)
    pallas_call x3, Pallas kernels, comm_call(): pl.pallas_call(body, out_shape=out_shape, in_specs=[pl.BlockSpec(memory_s...  305 us
    pallas_call x1, Pallas kernels, mixer_bwd(): pl.pallas_call(functools.partial(bwd_kernel, count), out_shape=(jax.Shape...  51.6 us
    unnamed x1, blocking collectives  39.4 us
    unnamed x40, local copies, waits for them, and re-layouts  33.6 us
    dot_general x7, matrix products, mm(): return lax.dot_general(a, b, (dims, ((), ())), preferred_element_type=f32)  29.5 us
    pallas_call x1, Pallas kernels, mixer_fwd(): pl.pallas_call(functools.partial(fwd_kernel, count), out_shape=(jax.Shape...  25.3 us
    psum x1, blocking collectives, shards(): lax.psum((dtaps[:, 0:512], dtaps[:, 512:640], dtaps[:, 640:768], dheads[0...  23.7 us
    reduce_scatter x2, waiting for transfers between devices, scatter(): lax.psum_scatter(v, 'dp', scatter_dimension=axis, tiled=True).astype(f32)  18 us
  transfers between devices with their start and end apart: 6, of which 1 were waited for; matrix products, arithmetic and copies ran while one was open for 12% of the time, Pallas kernels for 46%

profile of v1, /device:TPU:0, one launch (start us, length us, event | category | flops | bytes accessed | tf_op | source)
XLA Modules:
  0.0 564.0 jit_solution(18222000224451520935)
XLA Ops:
  7.2 0.0 all-gather.2.cloned.1.call-start
  7.2 0.7 all-gather.2.cloned.1.call-update
  7.9 0.0 reduce-scatter.10.cloned.1.call-start
  8.0 0.7 convert_element_type.49
  8.7 0.9 reshape.129.keep_rows
  9.5 1.6 copy.78.ws
  11.1 1.3 convert_element_type.50.seg
  12.4 108.3 %shard_map.450 = (f32[8,32,1024]{2,1,0:T(8,128)}, bf16[4,8,32,1024]{3,2,1,0:T(8,128)(2,1)}, bf16[4,8,32,2048]{3,2,1,0:T(8,128)(2,1)}, f32[4,8,32,8]{3,2,1,0:T(8,128)}) custom-call(bf16[4,8,32,2048]{3,2,1,0:T(8,128)(2,1)} %bitcast.65, bf16[2048,1024]{1,0:T(8,128)(2,1)} %embed.3, f32[8,32,1]{2,1,0:T(8,128)} %reshape.129.keep_rows, f32[1,1024]{1,0:T(1,128)} %bitcast.80, ...), custom_call_target="tpu_custom_call" | custom-call | tf_op jit(solution)/shard_map/pallas_call | solution.py:888
  120.7 25.3 %shard_map.451 = (bf16[1024,768]{1,0:T(8,128)(2,1)}, bf16[1024,512]{1,0:T(8,128)(2,1)}, bf16[4,128,512]{2,1,0:T(8,128)(2,1)}, f32[8,1024]{1,0:T(8,128)}) custom-call(bf16[1024,2048]{1,0:T(8,128)(2,1)} %bitcast.61, f32[1024,8]{1,0:T(8,128)} %bitcast.68, f32[1,1024]{1,0:T(1,128)} %convert_element_type.50.seg, f32[4,512]{1,0:T(4,128)} %t0.3, f32[4,128]{1,0:T(4,128)} %t1.3, ...), custom_call_target="tpu_custom_call" | custom-call | tf_op jit(solution)/shard_map/pallas_call | solution.py:438
  146.0 124.9 %shard_map.452 = (f32[8,32,1024]{2,1,0:T(8,128)}, bf16[4,8,32,1024]{3,2,1,0:T(8,128)(2,1)}, bf16[4,8,32,1024]{3,2,1,0:T(8,128)(2,1)}, bf16[4,8,32,1024]{3,2,1,0:...) custom-call(bf16[4,8,32,768]{3,2,1,0:T(8,128)(2,1)} %bitcast.64, ...), custom_call_target="tpu_custom_call" | custom-call | tf_op jit(solution)/shard_map/pallas_call | solution.py:888
  270.9 0.0 reduce-scatter.10.cloned.1.call-update
  270.9 0.0 reduce-scatter.16.cloned.1.call-start
  270.9 1.3 copy-done
  272.3 3.6 convolution_convert_fusion.2
  275.9 2.4 convolution_convert_fusion.1
  278.3 2.2 pad_maximum_fusion.2
  280.5 6.0 %copy.88 = bf16[1792,1024]{0,1:T(8,128)(2,1)} copy(bf16[1792,1024]{1,0:T(8,128)(2,1)} %pad_maximum_fusion.2) | data formatting | bytes 7340032
  286.6 0.0 reduce-scatter.16.cloned.1.call-update
  286.6 0.3 reduce-scatter.18.cloned.1.call-start
  286.9 1.3 copy-done.10
  288.2 4.2 bitcast_convert_fusion
  292.3 2.4 bitcast_convert_fusion.1
  294.8 2.5 pad_maximum_fusion.1
  297.2 6.5 %copy.90 = bf16[1024,2048]{1,0:T(8,128)(2,1)} copy(bf16[1024,2048]{0,1:T(8,128)(2,1)} %pad_maximum_fusion.1) | data formatting | bytes 8388608
  303.7 0.0 reduce-scatter.18.cloned.1.call-update
  303.8 0.5 reduce-scatter.12.cloned.1.call-start
  304.3 51.6 %shard_map.453 = (bf16[1024,2048]{1,0:T(8,128)(2,1)}, bf16[1024,8]{1,0:T(8,128)(2,1)}, f32[4,768]{1,0:T(4,128)}, f32[2,8]{1,0:T(2,128)}, f32[1,512]{1,0:T(1,128)}, /*index=5*/f32[1,512]{1,0:T(1,128)}) custom-call(bf16[1024,2048]{1,0:T(8,128)(2,1)} %bitcast.62, f32[1024,8]{1,0:T(8,128)} %bitcast.69, f32[1,1024]{1,0:T(1,128)} %convert_element_type.50.seg, ...), custom_call_target="tpu_custom_call" | custom-call | tf_op jit(solution)/shard_map/pallas_call | solution.py:461
  355.8 72.0 %shard_map.454 = (bf16[4,8,32,1024]{3,2,1,0:T(8,128)(2,1)}, bf16[4,8,32,2048]{3,2,1,0:T(8,128)(2,1)}, f32[1,1024]{1,0:T(1,128)}) custom-call(bf16[4,8,32,2048]{3,2,1,0:T(8,128)(2,1)} %bitcast.67, bf16[4,8,32,8]{3,2,1,0:T(8,128)(2,1)} %bitcast.79, bf16[1024,512]{1,0:T(8,128)(2,1)} %wz.3, bf16[1024,512]{1,0:T(8,128)(2,1)} %wx.3, bf16[1024,128]{1,0:T(8,128)(2,1)} %wb.3, ...), custom_call_target="tpu_custom_call" | custom-call | tf_op jit(solution)/shard_map/pallas_call | solution.py:888
  427.9 9.4 %convert_bitcast_fusion = bf16[2048,1024]{0,1:T(8,128)(2,1)} fusion(bf16[1024,1024]{1,0:T(8,128)(2,1)} %bitcast.96, bf16[1024,2048]{1,0:T(8,128)(2,1)} %param.27), kind=kOutput, calls=%fused_computation.4 | convolution fusion | flops 4297064448 | bytes 10485760 | tf_op jit(solution)/shard_map/dot_general | solution.py:24
  437.3 0.0 reduce-scatter.12.cloned.1.call-update
  437.3 0.0 reduce-scatter.14.cloned.1.call-start
  437.4 1.5 copy-done.1
  438.9 0.0 copy-done.3
  438.9 0.4 convolution_convert_fusion.3
  439.3 0.2 copy.81
  439.5 7.0 %convolution_convert_fusion = bf16[1024,2048]{1,0:T(8,128)(2,1)S(1)} fusion(bf16[1024,1024]{1,0:T(8,128)(2,1)S(1)} %bitcast.72, bf16[1024,2048]{1,0:T(8,128)(2,1)} %get-tuple-element.62), kind=kOutput, calls=%fused_computation.5 | convolution fusion | flops 4297064448 | bytes 10485760 | tf_op jit(solution)/shard_map/dot_general | solution.py:24
  446.5 2.6 pad_maximum_fusion
  449.1 0.0 copy-start.8
  449.1 0.0 reduce-scatter.14.cloned.1.call-update
  449.2 0.6 copy-done.5
  449.8 39.4 %all-reduce.2 = (f32[1024]{0:T(1024)S(1)}, f32[1024]{0:T(1024)S(1)}) all-reduce(f32[1024]{0:T(1024)S(1)} %bitcast.86, f32[1024]{0:T(1024)S(1)} %bitcast.85), channel_id=4, replica_groups=mesh['dp'=8,'tp'=4] {'dp','tp'}, use_global_device_ids=true, to_apply=%region_2.0.clone | all-reduce | flops 2048 | bytes 16384
  489.3 0.6 dynamic-slice
  489.9 0.6 dynamic-slice.1
  490.4 0.7 slice_bitcast_fusion.1
  491.1 23.7 %all-reduce.3 = (f32[4,512]{1,0:T(4,128)}, f32[4,128]{1,0:T(4,128)}, f32[4,128]{1,0:T(4,128)}, f32[8]{0:T(128)}, f32[8]{0:T(128)}, /*index=5*/f32[8]{0:T(128)}, f32[512]{0:T(512)}) all-reduce(f32[4,512]{1,0:T(4,128)S(1)} %slice.62, f32[4,128]{1,0:T(4,128)S(1)} %get-tuple-element.198, ...), channel_id=1, replica_groups=mesh['dp'=8,'tp'=4] {'dp'}, use_global_device_ids=true, to_apply=%region_4.0 | all-reduce | flops 3608 | bytes 28864 | tf_op jit(solution)/shard_map/psum | solution.py:1067
  514.8 2.2 fusion
  516.9 0.9 slice.81
  517.9 0.9 slice.85
  518.7 1.0 slice.88
  519.7 0.8 copy.92
  520.6 0.8 copy.93
  521.3 1.0 copy.94
  522.3 1.3 copy.91
  523.6 0.1 fusion.4
  523.7 1.0 copy.84
  524.7 1.0 copy.85
  525.7 2.2 copy.82
  527.9 18.0 %reduce-scatter.14.cloned.1.call-done = bf16[128,2056]{1,0:T(8,128)(2,1)} async-done(((bf16[1024,2056]{1,0:T(8,128)(2,1)}), bf16[128,2056]{1,0:T(8,128)(2,1)}) %reduce-scatter.14.cloned.1.call-update) | async-done | bytes 526352 | tf_op jit(solution)/shard_map/reduce_scatter | solution.py:1061
  545.9 0.8 slice.80
  546.7 0.7 copy.83
  547.3 1.8 fusion.3
  549.1 1.4 fusion.2
  550.6 1.7 fusion.1
  552.2 4.8 copy.96
  (27 shorter events, 0.0 us)
Async XLA Ops:
  7.2 138.8 %all-gather.2.cloned.1.call-start = ((), (), s32[]{:S(2)}) async-start(), calls=%async_computation.5 | async-start | bytes 2621440 | tf_op jit(solution)/shard_map/all_gather | solution.py:976
  7.9 506.8 %reduce-scatter.10.cloned.1.call-start = ((), (), s32[]{:S(2)}) async-start(), calls=%async_computation.6 | async-start | bytes 2621440 | tf_op jit(solution)/shard_map/reduce_scatter | solution.py:1024
  270.9 1.4 copy-start
  270.9 246.0 %reduce-scatter.16.cloned.1.call-start = ((), (), s32[]{:S(2)}) async-start(), calls=%async_computation.9 | async-start | bytes 4128768
  272.3 3.6 copy-start.2
  272.3 3.6 copy-start.12
  286.6 1.6 copy-start.10
  286.6 235.7 %reduce-scatter.18.cloned.1.call-start = ((), (), s32[]{:S(2)}) async-start(), calls=%async_computation.10 | async-start | bytes 4718592
  288.2 4.2 copy-start.11
  303.8 221.9 %reduce-scatter.12.cloned.1.call-start = ((), (), s32[]{:S(2)}) async-start(), calls=%async_computation.7 | async-start | bytes 4718592 | tf_op jit(solution)/shard_map/reduce_scatter | solution.py:1061
  437.3 1.6 copy-start.1
  437.3 1.6 copy-start.3
  437.3 108.5 %reduce-scatter.14.cloned.1.call-start = ((), (), s32[]{:S(2)}) async-start(), calls=%async_computation.8 | async-start | bytes 5013504 | tf_op jit(solution)/shard_map/reduce_scatter | solution.py:1061
  449.1 0.7 copy-start.5
  449.1 0.7 copy-start.6
  449.1 0.7 copy-start.7
  449.1 41.3 %copy-start.9 = (f32[2,8]{1,0:T(2,128)S(1)}, f32[2,8]{1,0:T(2,128)}, u32[]{:S(2)}) copy-start(f32[2,8]{1,0:T(2,128)} %get-tuple-element.70) | copy-start | bytes 196
  449.1 42.0 %copy-start.8 = (f32[1,512]{1,0:T(1,128)S(1)}, f32[1,512]{1,0:T(1,128)}, u32[]{:S(2)}) copy-start(f32[1,512]{1,0:T(1,128)} %get-tuple-element.72) | copy-start | bytes 6148
  449.1 65.6 %copy-start.4 = (f32[8,32,1024]{2,1,0:T(8,128)S(1)}, f32[8,32,1024]{2,1,0:T(8,128)}, u32[]{:S(2)}) copy-start(f32[8,32,1024]{2,1,0:T(8,128)} %get-tuple-element.56) | copy-start | bytes 3145732
Sparse Core Ops, SparseCore 0:
  9.6 78.0 all-gather.1
  271.0 46.2 reduce-scatter.9
  321.2 47.9 reduce-scatter.15
  372.4 51.3 reduce-scatter.17
  437.5 52.3 reduce-scatter.11
  493.2 52.6 reduce-scatter.13

commit v2 on v1

--- a/solution.py
+++ b/solution.py
@@ -485,7 +485,8 @@
 
 
 class Line:
-    def __init__(self, scratch, size):
+    def __init__(self, scratch, size, hop=1):
+        self.hop = hop
         (self.own, self.left, self.right, self.full, self.acc,
          self.ss, self.sr, self.gs, self.gr) = scratch
         self.size = size
@@ -597,7 +598,7 @@
         me, last = self.me, self.last
 
         def from_left(d, _):
-            j = i - jnp.maximum(d, last - d) - (me - d)
+            j = i - self.hop * (jnp.maximum(d, last - d) + me - d)
 
             @pl.when(self.inside(j))
             def _():
@@ -610,7 +611,7 @@
             return 0
 
         def from_right(d, _):
-            j = i - jnp.maximum(d, last - d) - (d - me)
+            j = i - self.hop * (jnp.maximum(d, last - d) + d - me)
 
             @pl.when(self.inside(j))
             def _():
@@ -627,9 +628,9 @@
 
     def move(self, i, finish):
         me, last = self.me, self.last
-        right_step = i - me
-        left_step = i - (last - me)
-        final_step = i - jnp.maximum(me, last - me)
+        right_step = i - self.hop * me
+        left_step = i - self.hop * (last - me)
+        final_step = i - self.hop * jnp.maximum(me, last - me)
 
         @pl.when(self.inside(right_step))
         def _():
@@ -646,10 +647,10 @@
         self.pass_on(i)
 
     def ready_step(self, i):
-        return i - self.last - jnp.maximum(self.me, self.last - self.me)
+        return i - self.hop * (self.last + jnp.maximum(self.me, self.last - self.me))
 
     def lag(self):
-        return 2 * self.last
+        return 2 * self.hop * self.last
 
     def leave(self):
         me, last = self.me, self.last
@@ -751,16 +752,22 @@
     line.leave()
 
 
-def ffn_kernel(size, mix, wmo, wao, resid_one, gain, wg, wu, wd, og_full, og_mine,
-               resid_grad, full_out, hidden_out, gg_out, ug_out, ffn_out, resid_out, mixg_out,
-               dmix, gain_grad, *scratch):
+def ffn_kernel(size, mix, wmo, wao, resid_one, gain, wg, wu, wd, og_low, og_high, og_mine,
+               resid_grad, ffn_out, resid_out, dmix, grads, gain_grad, hidden_all, gg_all, ug_all,
+               *scratch):
     half = len(scratch) // 2
     one, two = Line(scratch[:half], size), Line(scratch[half:], size)
     steps, sub, width = one.steps, one.own.shape[2], one.own.shape[3]
-    inner = wmo.shape[0]
+    length = size * steps * sub
+    inner, mixed, units = wmo.shape[0], mix.shape[3], wg.shape[1]
+    group = 256
+    groups = width // group
 
     def shaped(v):
         return v.reshape(size, sub, v.shape[1])
+
+    def all_rows(v):
+        return v.reshape(length, v.shape[3])
 
     def produce(j):
         x = flat(mix[:, j])
@@ -771,11 +778,8 @@
         resid_out[j] = rows
         return normed(rows, gain[...]).astype(bf16)
 
-    def middle(j):
-        x = one.full[:, j]
-        full_out[:, j] = x
-        x = flat(x)
-        og = flat(og_full[:, j])
+    def middle(j, og):
+        x = flat(one.full[:, j])
         gate, up = mm(x, wg[...]), mm(x, wu[...])
         hg = mm(og, wd[...], NT)
         sig = jax.nn.sigmoid(gate)
@@ -783,9 +787,9 @@
         hidden = (act * up).astype(bf16)
         gg = (hg * up * (sig * (1.0 + gate * (1.0 - sig)))).astype(bf16)
         ug = (hg * act).astype(bf16)
-        hidden_out[:, j] = shaped(hidden)
-        gg_out[:, j] = shaped(gg)
-        ug_out[:, j] = shaped(ug)
+        hidden_all[:, j] = shaped(hidden)
+        gg_all[:, j] = shaped(gg)
+        ug_all[:, j] = shaped(ug)
         two.own[:, j] = shaped(mm(gg, wg[...], NT) + mm(ug, wu[...], NT))
         ffn_out[:, j] = shaped(mm(hidden, wd[...]).astype(bf16))
 
@@ -797,11 +801,35 @@
         return rows.astype(bf16)
 
     def consume(j):
-        x = two.full[:, j]
-        mixg_out[:, j] = x
-        x = flat(x)
+        x = flat(two.full[:, j])
         dmix[:, j, :, 0:inner] = shaped(mm(x, wmo[...], NT).astype(bf16))
         dmix[:, j, :, inner:] = shaped(mm(x, wao[...], NT).astype(bf16))
+
+    def columns(ref, g):
+        return all_rows(ref[:, :, :, pl.ds(pl.multiple_of(g * group, group), group)])
+
+    def ffn_grads(g):
+        here = pl.ds(pl.multiple_of(g * group, group), group)
+        x = columns(one.full, g)
+        grads[here, 0:units] = mm(x, all_rows(gg_all[...]), TN).astype(bf16)
+        grads[here, units : 2 * units] = mm(x, all_rows(ug_all[...]), TN).astype(bf16)
+        half_steps = steps // 2
+        hidden = hidden_all[...]
+        total = None
+        for part, og in enumerate((og_low, og_high)):
+            cols = og[:, :, :, pl.ds(pl.multiple_of(g * group, group), group)]
+            cols = cols.reshape(length // 2, group)
+            rows = hidden[:, part * half_steps : (part + 1) * half_steps]
+            term = mm(cols, rows.reshape(length // 2, units), TN)
+            total = term if total is None else total + term
+        grads[here, 2 * units + mixed :] = total.astype(bf16)
+
+    def mix_grads(g, _):
+        here = pl.ds(pl.multiple_of(g * group, group), group)
+        grads[here, 2 * units : 2 * units + mixed] = mm(
+            columns(two.full, g), all_rows(mix[...]), TN
+        ).astype(bf16)
+        return 0
 
     one.enter()
     gain_grad[...] = jnp.zeros_like(gain_grad)
@@ -818,9 +846,13 @@
 
         ready_one = one.ready_step(i)
 
-        @pl.when(one.inside(ready_one))
-        def _():
-            middle(ready_one)
+        @pl.when(jnp.logical_and(ready_one >= 0, ready_one < steps // 2))
+        def _():
+            middle(ready_one, flat(og_low[:, ready_one]))
+
+        @pl.when(jnp.logical_and(ready_one >= steps // 2, ready_one < steps))
+        def _():
+            middle(ready_one, flat(og_high[:, ready_one - steps // 2]))
 
         ready_two = two.ready_step(i - lag)
 
@@ -828,60 +860,18 @@
         def _():
             consume(ready_two)
 
+        turn = i - (steps + lag)
+
+        @pl.when(jnp.logical_and(turn >= 0, turn < groups))
+        def _():
+            ffn_grads(turn)
+
         return 0
 
     lax.fori_loop(0, steps + lag + two.lag(), iteration, 0)
+    lax.fori_loop(0, groups, mix_grads, 0)
     one.leave()
     two.leave()
-
-
-def entry_kernel(size, dproj, dstep, wz, wx, wb, wc, wq, wk, wv, ws, resid_one, gain, resid_grad,
-                 keep_rows, embed, eg_out, patch_grad, gain_grad, *scratch):
-    line = Line(scratch, size)
-    steps, sub = line.steps, line.own.shape[2]
-    columns = []
-    for ref in (wz, wx, wb, wc, wq, wk, wv):
-        columns.append((ref, sum(c[0].shape[1] for c in columns)))
-
-    def produce(j):
-        total = mm(flat(dstep[:, j]), ws[...], NT)
-        for ref, start in columns:
-            total = total + mm(flat(dproj[:, j, :, start : start + ref.shape[1]]), ref[...], NT)
-        line.own[:, j] = total.reshape(size, sub, total.shape[1])
-
-    def finish(j, total):
-        back, part = normed_back(total, resid_one[j], gain[...])
-        gain_grad[...] = gain_grad[...] + part
-        return ((resid_grad[j] + back) * keep_rows[j]).astype(bf16)
-
-    def consume(j):
-        x = line.full[:, j]
-        eg_out[:, j] = x
-        patch_grad[:, j] = (
-            mm(flat(x), embed[...], NT).astype(bf16).reshape(size, sub, embed.shape[0])
-        )
-
-    line.enter()
-    gain_grad[...] = jnp.zeros_like(gain_grad)
-    produce(0)
-
-    def iteration(i, _):
-        line.move(i, finish)
-
-        @pl.when(i + 1 < steps)
-        def _():
-            produce(i + 1)
-
-        ready = line.ready_step(i)
-
-        @pl.when(line.inside(ready))
-        def _():
-            consume(ready)
-
-        return 0
-
-    lax.fori_loop(0, steps + line.lag(), iteration, 0)
-    line.leave()
 
 
 def comm_call(body, out_shape, scratch, identity, *args):
@@ -901,24 +891,294 @@
     return jax.ShapeDtypeStruct(shape, kind)
 
 
-def split_parts(matrix, widths, axis):
-    pieces_out = []
-    offset = 0
-    for width in widths:
-        pieces_out.append(lax.slice_in_dim(matrix, offset, offset + width, axis=axis))
-        offset = offset + width
-    return pieces_out
-
-
-def reduce_weights(rows_first, cols_first):
-    return (
-        lax.psum_scatter(
-            rows_first.astype(jnp.bfloat16), "dp", scatter_dimension=0, tiled=True
-        ).astype(jnp.float32),
-        lax.psum_scatter(
-            cols_first.astype(jnp.bfloat16), "dp", scatter_dimension=1, tiled=True
-        ).astype(jnp.float32),
-    )
+class Halving:
+    def __init__(self, data, got, ss, sr):
+        self.data, self.got, self.ss, self.sr = data, got, ss, sr
+        self.count, self.rows = data.shape[0], data.shape[1]
+        self.bits = self.count.bit_length() - 1
+        self.me = lax.axis_index("dp")
+        plain = list(range(self.bits))
+        other = plain if self.bits < 3 else [0, 2, 1] + plain[3:]
+        self.orders = (plain, other)
+
+    @staticmethod
+    def scratch(count, rows, columns):
+        spare = max(count - 1, 1)
+        return [
+            pltpu.VMEM((count, rows, columns), bf16),
+            pltpu.VMEM((spare, rows, columns), bf16),
+            pltpu.SemaphoreType.DMA((2, spare)),
+            pltpu.SemaphoreType.DMA((2, spare)),
+        ]
+
+    def bit(self, b):
+        return lax.rem(self.me // 2**b, 2)
+
+    def block(self, half, stage, e, theirs):
+        order = self.orders[half]
+        place = 0
+        for b in order[:stage]:
+            place = place + self.bit(b) * 2**b
+        b = order[stage]
+        place = place + (1 - self.bit(b) if theirs else self.bit(b)) * 2**b
+        for t, b in enumerate(sorted(order[stage + 1 :])):
+            place = place + lax.rem(e // 2**t, 2) * 2**b
+        return place
+
+    def open(self, stage):
+        return 2 ** (self.bits - 1 - stage)
+
+    def slot(self, stage, e):
+        return sum(self.open(s) for s in range(stage)) + e
+
+    def part(self, half):
+        rows = self.rows // 2
+        return pl.ds(half * rows, rows)
+
+    def copy(self, half, stage, e):
+        b = self.orders[half][stage]
+        slot = self.slot(stage, e)
+        return pltpu.make_async_remote_copy(
+            src_ref=self.data.at[self.block(half, stage, e, True), self.part(half)],
+            dst_ref=self.got.at[slot, self.part(half)],
+            send_sem=self.ss.at[half, slot],
+            recv_sem=self.sr.at[half, slot],
+            device_id={"dp": self.me + (1 - 2 * self.bit(b)) * 2**b},
+            device_id_type=MESH,
+        )
+
+    def start(self, stage, low=0, high=None):
+        def one(e, _):
+            self.copy(0, stage, e).start()
+            self.copy(1, stage, e).start()
+            return 0
+
+        lax.fori_loop(low, self.open(stage) if high is None else high, one, 0)
+
+    def finish(self, stage):
+        def one(e, _):
+            for half in range(2):
+                self.copy(half, stage, e).wait_recv()
+                place, part = self.block(half, stage, e, False), self.part(half)
+                got = self.got[self.slot(stage, e), part]
+                self.data[place, part] = (self.data[place, part].astype(f32) + got.astype(f32)).astype(bf16)
+            return 0
+
+        lax.fori_loop(0, self.open(stage), one, 0)
+
+    def leave(self):
+        for stage in range(self.bits):
+
+            def one(e, _, stage=stage):
+                self.copy(0, stage, e).wait_send()
+                self.copy(1, stage, e).wait_send()
+                return 0
+
+            lax.fori_loop(0, self.open(stage), one, 0)
+
+
+class Doubling:
+    def __init__(self, parts, got, ss, sr, dp, tp):
+        self.parts, self.got, self.ss, self.sr = parts, got, ss, sr
+        self.hops = [("dp", b) for b in range(dp.bit_length() - 1)]
+        self.hops += [("tp", b) for b in range(tp.bit_length() - 1)]
+
+    @staticmethod
+    def scratch(dp, tp, rows, columns):
+        hops = dp.bit_length() + tp.bit_length() - 2
+        return [
+            pltpu.VMEM((hops + 1, rows, columns), f32),
+            pltpu.VMEM((hops, rows, columns), f32),
+            pltpu.SemaphoreType.DMA((hops,)),
+            pltpu.SemaphoreType.DMA((hops,)),
+        ]
+
+    def copy(self, hop):
+        axis, b = self.hops[hop]
+        me = lax.axis_index(axis)
+        flip = (1 - 2 * lax.rem(me // 2**b, 2)) * 2**b
+        return pltpu.make_async_remote_copy(
+            src_ref=self.parts.at[hop],
+            dst_ref=self.got.at[hop],
+            send_sem=self.ss.at[hop],
+            recv_sem=self.sr.at[hop],
+            device_id={axis: me + flip},
+            device_id_type=MESH,
+        )
+
+    def start(self, hop):
+        self.copy(hop).start()
+
+    def finish(self, hop):
+        self.copy(hop).wait_recv()
+        self.parts[hop + 1] = self.parts[hop] + self.got[hop]
+
+    def leave(self):
+        for hop in range(len(self.hops)):
+            self.copy(hop).wait_send()
+
+
+def enter_both(dp, tp):
+    barrier = pltpu.get_barrier_semaphore()
+    me_t, me_d = lax.axis_index("tp"), lax.axis_index("dp")
+    for away in range(1, tp):
+        pl.semaphore_signal(
+            barrier, inc=1, device_id={"tp": lax.rem(me_t + away, tp)}, device_id_type=MESH
+        )
+    bits = dp.bit_length() - 1
+    for b in range(bits):
+        flip = (1 - 2 * lax.rem(me_d // 2**b, 2)) * 2**b
+        pl.semaphore_signal(barrier, inc=1, device_id={"dp": me_d + flip}, device_id_type=MESH)
+    pl.semaphore_wait(barrier, tp - 1 + bits)
+
+
+def entry_kernel(size, dp, dproj, dstep, wz, wx, wb, wc, wq, wk, wv, ws, resid_one, gain, resid_grad,
+                 keep_rows, embed, full_one, patches, dtaps, dheads, dgain, dskip, two_gain_grad,
+                 patch_grad, embed_out, in_out, small_out, *scratch):
+    line = Line(scratch[0:9], size)
+    ins = Halving(*scratch[9:13])
+    emb = Halving(*scratch[13:17])
+    small = Doubling(*scratch[17:21], dp, size)
+    steps, sub, width = line.steps, line.own.shape[2], line.own.shape[3]
+    length = size * steps * sub
+    weights = (wz, wx, wb, wc, wq, wk, wv)
+    columns = []
+    for ref in weights:
+        columns.append((ref, sum(c[0].shape[1] for c in columns)))
+    group = 256
+    groups = width // group
+    in_group = group // ins.rows
+
+    def all_rows(v):
+        return v.reshape(length, v.shape[3])
+
+    def produce(j):
+        total = mm(flat(dstep[:, j]), ws[...], NT)
+        for ref, start in columns:
+            total = total + mm(flat(dproj[:, j, :, start : start + ref.shape[1]]), ref[...], NT)
+        line.own[:, j] = total.reshape(size, sub, width)
+
+    def finish(j, total):
+        back, part = normed_back(total, resid_one[j], gain[...])
+        small.parts[0, 9:10] = small.parts[0, 9:10] + part
+        return ((resid_grad[j] + back) * keep_rows[j]).astype(bf16)
+
+    def consume(d, _):
+        x = flat(line.full[d])
+        patch_grad[d] = mm(x, embed[...], NT).astype(bf16).reshape(steps, sub, embed.shape[0])
+        return 0
+
+    def weight_group(g):
+        x = all_rows(full_one[:, :, :, pl.ds(pl.multiple_of(g * group, group), group)])
+        here = pl.ds(g * in_group, in_group)
+        grad = mm(x, all_rows(dproj[...]), TN).astype(bf16)
+        ins.data[here, :, 0:PROJ] = grad.reshape(in_group, ins.rows, PROJ)
+        grad = mm(x, all_rows(dstep[...]), TN).astype(bf16)
+        grad = jnp.concatenate([grad, jnp.zeros((group, 120), bf16)], axis=1)
+        ins.data[here, :, PROJ:] = grad.reshape(in_group, ins.rows, 128)
+        if ins.bits:
+            ins.start(0, g * in_group // 2, (g + 1) * in_group // 2)
+
+    def embed_group(g):
+        x = all_rows(line.full[:, :, :, pl.ds(pl.multiple_of(g * group, group), group)])
+        grad = mm(x, all_rows(patches[...]), TN).astype(bf16)
+        emb.data[pl.ds(g * in_group, in_group)] = grad.reshape(
+            in_group, emb.rows, grad.shape[1]
+        )
+        if emb.bits:
+            emb.start(0, g * in_group // 2, (g + 1) * in_group // 2)
+
+    enter_both(dp, size)
+    first = jnp.zeros((16, width), f32)
+    small.parts[0] = first
+    small.parts[0, 0:4, 0:768] = dtaps[...]
+    small.parts[0, 4:5, 0:512] = dgain[...]
+    small.parts[0, 5:6, 0:512] = dskip[...]
+    small.parts[0, 6:8, 0:8] = dheads[...]
+    small.parts[0, 8:9] = two_gain_grad[...]
+    produce(0)
+
+    def iteration(i, _):
+        line.move(i, finish)
+
+        @pl.when(i + 1 < steps)
+        def _():
+            produce(i + 1)
+
+        @pl.when(i < groups)
+        def _():
+            weight_group(i)
+
+        for stage in range(ins.bits):
+
+            @pl.when(i == groups + (8 * stage) // max(ins.bits - 1, 1))
+            def _(stage=stage):
+                ins.finish(stage)
+                if stage + 1 < ins.bits:
+                    ins.start(stage + 1)
+
+        return 0
+
+    lax.fori_loop(0, steps + line.lag(), iteration, 0)
+    small.start(0)
+
+    def each_group(g, _):
+        embed_group(g)
+        return 0
+
+    lax.fori_loop(0, groups, each_group, 0)
+    lax.fori_loop(0, size, consume, 0)
+    in_out[...] = ins.data[ins.me]
+    hops = len(small.hops)
+    for turn in range(max(hops, emb.bits)):
+        if turn < hops:
+            small.finish(turn)
+            if turn + 1 < hops:
+                small.start(turn + 1)
+        if turn < emb.bits:
+            emb.finish(turn)
+            if turn + 1 < emb.bits:
+                emb.start(turn + 1)
+    small_out[0:8] = small.parts[dp.bit_length() - 1, 0:8]
+    small_out[8:16] = small.parts[hops, 8:16]
+    embed_out[...] = emb.data[emb.me]
+    line.leave()
+    ins.leave()
+    emb.leave()
+    small.leave()
+
+
+def last_kernel(patch_in, embed_in, ins, mids, small, resid, ffn, place, patch_out, result,
+                embed_out, gz, gx, gb, gc, gq, gk, gv, gs, t0, t1, t2, hb, hr, hs, inner_gain,
+                gmo, gao, ggate, gup, gdown, gain_one, gain_two, sem):
+    move = pltpu.make_async_copy(patch_in, patch_out, sem)
+    move.start()
+    result[...] = (resid[...] + ffn[...].astype(f32)).astype(bf16)
+    start = 0
+    for out in (gz, gx, gb, gc, gq, gk, gv, gs):
+        out[...] = ins[:, start : start + out.shape[1]].astype(f32)
+        start = start + out.shape[1]
+    units, inner = ggate.shape[1], t0.shape[1]
+    ggate[...] = mids[:, 0:units].astype(f32)
+    gup[...] = mids[:, units : 2 * units].astype(f32)
+    flipped = mids[:, 2 * units :].astype(f32)
+    outs = ((gmo, flipped[:, 0:inner]), (gao, flipped[:, inner : flipped.shape[1] - units]),
+            (gdown, flipped[:, flipped.shape[1] - units :]), (embed_out, embed_in[...].astype(f32)))
+    for out, value in outs:
+        out[...] = value.T if out.shape != value.shape else value
+    t0[...] = small[0:4, 0 : t0.shape[1]]
+    t1[...] = small[0:4, t0.shape[1] : t0.shape[1] + t1.shape[1]]
+    t2[...] = small[0:4, t0.shape[1] + t1.shape[1] : t0.shape[1] + 2 * t1.shape[1]]
+    hb[...] = small[6:7, 0 : hb.shape[1]]
+    hr[...] = small[7:8, 0 : hr.shape[1]]
+    hs[...] = small[5:6, 0 : hs.shape[1]]
+    inner_gain[...] = small[4:5, 0 : inner_gain.shape[1]]
+    width, share = small.shape[1], gain_one.shape[1]
+    chosen = (iota((width, share), 0) == iota((width, share), 1) + place[0] * share).astype(f32)
+    gains = mmx(small[8:16, :], chosen)
+    gain_two[...] = gains[0:1, :]
+    gain_one[...] = gains[1:2, :]
+    move.wait()
 
 
 def shards(
@@ -973,7 +1233,8 @@
     )
     one_gain, two_gain = first_gain[None], second_gain[None]
     buffers = Line.scratch(size, STEPS, sub, width)
-    og_full = lax.all_gather(out_grad, "tp", axis=0, tiled=True)
+    og_low, og_high = out_grad[: mine // 2], out_grad[mine // 2 :]
+    og_low = lax.all_gather(og_low, "tp", axis=0)
 
     resid_one, full_one, projected, step_raw = comm_call(
         functools.partial(embed_kernel, size),
@@ -991,26 +1252,26 @@
         one_gain,
         *in_list,
     )
+    og_low, og_high, projected = lax.optimization_barrier((og_low, og_high, projected))
+    og_high = lax.all_gather(og_high, "tp", axis=0)
     projected = projected.reshape(length, PROJ)
     step_raw = step_raw.reshape(length, step_weight.shape[1])
     mix_in, ssd, states, lse = mixer_fwd(size, projected, step_raw, seg_row, taps, *core_params)
     inner_width = mamba_output.shape[0]
     hidden_width = ffn_gate.shape[1]
-    wide = sds((*shape, hidden_width), bf16)
     rows16 = sds((*shape, width), bf16)
     rows32 = sds((STEPS, sub, width), f32)
-    (
-        resid_grad, full_two, hidden, gate_grad, up_grad, ffn_part, resid_two, mix_full, dmix,
-        second_gain_grad,
-    ) = comm_call(
+    mixed = mix_in.shape[1]
+    half_shape = (size, STEPS // 2, sub, width)
+    resid_grad, ffn_part, resid_two, dmix, grads, second_gain_grad = comm_call(
         functools.partial(ffn_kernel, size),
         (
-            rows32, rows16, wide, wide, wide, rows16, rows32, rows16,
-            sds((*shape, mix_in.shape[1]), bf16), sds((1, width), f32),
+            rows32, rows16, rows32, sds((*shape, mixed), bf16),
+            sds((width, 3 * hidden_width + mixed), bf16), sds((1, width), f32),
         ),
-        buffers + buffers,
+        [pltpu.VMEM((*shape, hidden_width), bf16)] * 3 + buffers + buffers,
         2,
-        mix_in.reshape(*shape, mix_in.shape[1]),
+        mix_in.reshape(*shape, mixed),
         mamba_output,
         attn_output,
         resid_one,
@@ -1018,33 +1279,33 @@
         ffn_gate,
         ffn_up,
         ffn_down,
-        og_full.reshape(*shape, width),
+        og_low.reshape(half_shape),
+        og_high.reshape(half_shape),
         out_grad.reshape(STEPS, sub, width),
     )
     ffn_sum = lax.psum_scatter(
         ffn_part.reshape(length, width), "tp", scatter_dimension=0, tiled=True
     )
-    result = (resid_two.reshape(mine, width) + ffn_sum.astype(f32)).astype(bf16)
-
-    def rows_of(v):
-        return v.reshape(length, v.shape[-1])
-
-    def outer(a, b):
-        return mm(rows_of(a), rows_of(b), TN).astype(bf16)
-
-    down_grad = outer(hidden, og_full)
-    ffn_gate_part = outer(full_two, gate_grad)
-    ffn_up_part = outer(full_two, up_grad)
-    mixout_grad = outer(mix_in, mix_full)
+    mid_sum = lax.psum_scatter(grads, "dp", scatter_dimension=0, tiled=True)
     proj_grad, step_grad, dtaps, dheads, dgain, dskip = mixer_bwd(
         size, projected, step_raw, seg_row, taps, *core_params, mix_in, ssd, states, lse,
-        rows_of(dmix),
+        dmix.reshape(length, mixed),
     )
-    in_part = jnp.concatenate([outer(full_one, proj_grad), outer(full_one, step_grad)], axis=1)
-    embedded_full, patches_grad, first_gain_grad = comm_call(
-        functools.partial(entry_kernel, size),
-        (rows16, sds((*shape, patches.shape[1]), bf16), sds((1, width), f32)),
-        buffers,
+    dp = lax.axis_size("dp")
+    block = width // dp
+    features = patches.shape[1]
+    patches_grad, embed_sum, in_sum, small = comm_call(
+        functools.partial(entry_kernel, size, dp),
+        (
+            sds((*shape, features), bf16),
+            sds((block, features), bf16),
+            sds((block, PROJ + 128), bf16),
+            sds((16, width), f32),
+        ),
+        buffers
+        + Halving.scratch(dp, block, PROJ + 128)
+        + Halving.scratch(dp, block, features)
+        + Doubling.scratch(dp, size, 16, width),
         3,
         proj_grad.reshape(*shape, PROJ),
         step_grad.reshape(*shape, step_grad.shape[1]),
@@ -1054,57 +1315,89 @@
         resid_grad,
         keep_rows,
         embed_weight,
+        full_one,
+        patches.reshape(*shape, features),
+        dtaps,
+        dheads,
+        dgain,
+        dskip,
+        second_gain_grad,
     )
-    embed_grad = outer(patches, embedded_full)
-
-    def scatter(v, axis):
-        return lax.psum_scatter(v, "dp", scatter_dimension=axis, tiled=True).astype(f32)
-
-    ffn_rows = scatter(jnp.concatenate([ffn_gate_part, ffn_up_part], axis=1), 0)
-    mid_cols = scatter(jnp.concatenate([mixout_grad, down_grad], axis=0), 1)
-    in_rows = scatter(in_part, 0)
-    embed_cols = scatter(embed_grad, 1)
-    head_sums = lax.psum(
-        (
-            dtaps[:, 0:512],
-            dtaps[:, 512:640],
-            dtaps[:, 640:768],
-            dheads[0],
-            dheads[1],
-            dskip[0, 0:8],
-            dgain[0],
+    place = (lax.axis_index("dp") * size + lax.axis_index("tp"))[None]
+    flip = block % 128 == 0
+
+    def turned(rows):
+        return sds((rows, block) if flip else (block, rows), f32)
+
+    outs = pl.pallas_call(
+        last_kernel,
+        out_shape=(
+            sds((length, features), bf16),
+            sds((mine, width), bf16),
+            turned(features),
+            *[sds((block, member.shape[1]), f32) for member in in_list],
+            *[sds(member.shape, f32) for member in taps],
+            *[sds((1, step_bias.shape[0]), f32)] * 3,
+            sds((1, inner_width), f32),
+            turned(inner_width),
+            turned(attn_output.shape[0]),
+            sds((block, hidden_width), f32),
+            sds((block, hidden_width), f32),
+            turned(hidden_width),
+            sds((1, block // size), f32),
+            sds((1, block // size), f32),
         ),
-        "dp",
+        in_specs=[pl.BlockSpec(memory_space=pl.ANY)]
+        + [pl.BlockSpec(memory_space=pltpu.VMEM)] * 6
+        + [pl.BlockSpec(memory_space=pltpu.SMEM)],
+        out_specs=(
+            pl.BlockSpec(memory_space=pl.ANY),
+            *[pl.BlockSpec(memory_space=pltpu.VMEM)] * 24,
+        ),
+        scratch_shapes=[pltpu.SemaphoreType.DMA],
+        compiler_params=pltpu.CompilerParams(vmem_limit_bytes=40 * 2**20),
+    )(
+        patches_grad.reshape(length, features),
+        embed_sum,
+        in_sum,
+        mid_sum,
+        small,
+        resid_two.reshape(mine, width),
+        ffn_sum,
+        place,
     )
-    gain_one_sum = lax.psum_scatter(
-        first_gain_grad[0], ("dp", "tp"), scatter_dimension=0, tiled=True
-    )
-    gain_two_sum = lax.psum_scatter(
-        second_gain_grad[0], ("dp", "tp"), scatter_dimension=0, tiled=True
-    )
-    in_parts = split_parts(in_rows, [member.shape[1] for member in in_list], 1)
-    ffn_parts = split_parts(ffn_rows, [hidden_width, hidden_width], 1)
-    mid_parts = split_parts(mid_cols, [inner_width, attn_output.shape[0], hidden_width], 0)
+    (
+        patches_grad, result, embed_cols, gz, gx, gb, gc, gq, gk, gv, gs, t0, t1, t2, hb, hr, hs,
+        inner_grad, gmo, gao, ggate, gup, gdown, gain_one, gain_two,
+    ) = outs
+    if not flip:
+        embed_cols, gmo, gao, gdown = embed_cols.T, gmo.T, gao.T, gdown.T
     return (
         result,
-        patches_grad.reshape(length, patches.shape[1]),
+        patches_grad,
         embed_cols,
-        gain_one_sum,
-        in_parts[0],
-        in_parts[1],
-        in_parts[2],
-        in_parts[3],
-        in_parts[7],
-        *head_sums,
-        mid_parts[0],
-        in_parts[4],
-        in_parts[5],
-        in_parts[6],
-        mid_parts[1],
-        gain_two_sum,
-        ffn_parts[0],
-        ffn_parts[1],
-        mid_parts[2],
+        gain_one[0],
+        gz,
+        gx,
+        gb,
+        gc,
+        gs,
+        t0,
+        t1,
+        t2,
+        hb[0],
+        hr[0],
+        hs[0],
+        inner_grad[0],
+        gmo,
+        gq,
+        gk,
+        gv,
+        gao,
+        gain_two[0],
+        ggate,
+        gup,
+        gdown,
     )
 
 

time: 571 us -> 448 us (0.78); the launches traced: 564 us -> 447 us
  blocking collectives: 63.1 us -> 0 us
  Pallas kernels: 382 us -> 416 us
  local copies, waits for them, and re-layouts: 43.8 us -> 12.3 us
  matrix products: 29.5 us -> 0 us
  waiting for transfers between devices: 18.7 us -> 3.22 us
  other arithmetic: 11.4 us -> 1.28 us
    unnamed x1 -> x0, blocking collectives: 39.4 us -> none
    pallas_call x3, Pallas kernels: 305 us -> 335 us  [comm_call(): pl.pallas_call(body, out_shape=out_shape, in_specs=[pl.BlockSpec(memory_s...]
    dot_general x7 -> x0, matrix products: 29.5 us -> none  [mm(): return lax.dot_general(a, b, (dims, ((), ())), preferred_element_type=f32)]
    unnamed x40 -> x18, local copies, waits for them, and re-layouts: 33.6 us -> 9.59 us
    psum x1 -> x0, blocking collectives: 23.7 us -> none  [shards(): lax.psum((dtaps[:, 0:512], dtaps[:, 512:640], dtaps[:, 640:768], dheads[0...]
    reduce_scatter x2 -> x1, waiting for transfers between devices: 18 us -> 0.02 us  [shards(): mid_sum = lax.psum_scatter(grads, 'dp', scatter_dimension=0, tiled=True)]
    concatenate x3 -> x0, other arithmetic: 7.25 us -> none  [the longest x1 2.59 us: shards(): jnp.concatenate([outer(full_one, proj_grad), outer(full_one, step_grad)],...]
    slice x10 -> x1, local copies, waits for them, and re-layouts: 8.5 us -> 1.85 us  [shards(): og_low, og_high = (out_grad[:mine // 2], out_grad[mine // 2:])]
  transfers between devices with their start and end apart: 6 -> 4, of which waited for: 1 -> 1; matrix products, arithmetic and copies ran while one was open for 12% -> 1% of each run, Pallas kernels for 46% -> 63%
where the time goes in v2:
time: 448 us; the launch traced here: 447 us
  Pallas kernels  416 us (93%)
  between operations  13.9 us (3%)
  local copies, waits for them, and re-layouts  12.3 us (3%)
    pallas_call x3, Pallas kernels, comm_call(): pl.pallas_call(body, out_shape=out_shape, in_specs=[pl.BlockSpec(memory_s...  335 us
    pallas_call x1, Pallas kernels, mixer_bwd(): pl.pallas_call(functools.partial(bwd_kernel, count), out_shape=(jax.Shape...  51.6 us
    pallas_call x1, Pallas kernels, mixer_fwd(): pl.pallas_call(functools.partial(fwd_kernel, count), out_shape=(jax.Shape...  25.2 us
    unnamed x18, local copies, waits for them, and re-layouts  9.59 us
  transfers between devices with their start and end apart: 4, of which 1 were waited for; matrix products, arithmetic and copies ran while one was open for 1% of the time, Pallas kernels for 63%

profile of v2, /device:TPU:0, one launch (start us, length us, event | category | flops | bytes accessed | tf_op | source)
XLA Modules:
  0.0 447.5 jit_solution(14858897340779822711)
XLA Ops:
  7.2 0.0 all-gather.5.cloned.1.call-start
  7.2 1.9 fusion
  9.1 0.0 all-gather.5.cloned.1.call-update
  9.1 0.0 all-gather.7.cloned.1.call-start
  9.2 1.6 copy.56.ws
  10.7 0.7 convert_element_type.7
  11.4 0.9 reshape.110.keep_rows
  12.3 0.0 copy-start.7
  12.3 91.7 %shard_map.450 = (f32[8,32,1024]{2,1,0:T(8,128)}, bf16[4,8,32,1024]{3,2,1,0:T(8,128)(2,1)}, bf16[4,8,32,2048]{3,2,1,0:T(8,128)(2,1)}, f32[4,8,32,8]{3,2,1,0:T(8,128)}) custom-call(bf16[4,8,32,2048]{3,2,1,0:T(8,128)(2,1)} %bitcast.31, bf16[2048,1024]{1,0:T(8,128)(2,1)} %embed.3, f32[8,32,1]{2,1,0:T(8,128)} %reshape.110.keep_rows, f32[1,1024]{1,0:T(1,128)} %bitcast.43, ...), custom_call_target="tpu_custom_call" | custom-call | tf_op jit(solution)/shard_map/pallas_call | solution.py:878
  104.0 0.0 all-gather.5.cloned.1.call-done
  104.0 0.0 all-gather.7.cloned.1.call-update
  104.0 0.0 reduce-scatter.5.cloned.1.call-start
  104.1 0.0 copy-done.7
  104.1 0.6 convert_element_type.8.seg
  104.7 25.2 %shard_map.451 = (bf16[1024,768]{1,0:T(8,128)(2,1)}, bf16[1024,512]{1,0:T(8,128)(2,1)}, bf16[4,128,512]{2,1,0:T(8,128)(2,1)}, f32[8,1024]{1,0:T(8,128)}) custom-call(bf16[1024,2048]{1,0:T(8,128)(2,1)} %bitcast.29, f32[1024,8]{1,0:T(8,128)} %bitcast.35, f32[1,1024]{1,0:T(1,128)} %convert_element_type.8.seg, f32[4,512]{1,0:T(4,128)} %t0.3, f32[4,128]{1,0:T(4,128)} %t1.3, ...), custom_call_target="tpu_custom_call" | custom-call | tf_op jit(solution)/shard_map/pallas_call | solution.py:438
  129.9 2.8 all-gather.7.cloned.1.call-done
  132.7 129.4 %shard_map.452 = (f32[8,32,1024]{2,1,0:T(8,128)}, bf16[4,8,32,1024]{3,2,1,0:T(8,128)(2,1)}, f32[8,32,1024]{2,1,0:T(8,128)}, bf16[4,8,32,768]{3,2,1,0:T(8,128)(2,...) custom-call(bf16[4,8,32,768]{3,2,1,0:T(8,128)(2,1)} %bitcast.33, bf16[512,1024]{1,0:T(8,128)(2,1)} %wmo.1, ...), custom_call_target="tpu_custom_call" | custom-call | tf_op jit(solution)/shard_map/pallas_call | solution.py:878
  262.1 0.0 reduce-scatter.5.cloned.1.call-update
  262.1 0.3 reduce-scatter.3.cloned.1.call-start
  262.4 0.3 reduce-scatter.3.cloned.1.call-update
  262.7 51.6 %shard_map.453 = (bf16[1024,2048]{1,0:T(8,128)(2,1)}, bf16[1024,8]{1,0:T(8,128)(2,1)}, f32[4,768]{1,0:T(4,128)}, f32[2,8]{1,0:T(2,128)}, f32[1,512]{1,0:T(1,128)}, /*index=5*/f32[1,512]{1,0:T(1,128)}) custom-call(bf16[1024,2048]{1,0:T(8,128)(2,1)} %bitcast.30, f32[1024,8]{1,0:T(8,128)} %bitcast.36, f32[1,1024]{1,0:T(1,128)} %convert_element_type.8.seg, ...), custom_call_target="tpu_custom_call" | custom-call | tf_op jit(solution)/shard_map/pallas_call | solution.py:461
  314.3 0.0 copy-start.1
  314.3 113.7 %shard_map.454 = (bf16[4,8,32,2048]{3,2,1,0:T(8,128)(2,1)}, bf16[128,2048]{1,0:T(8,128)(2,1)}, bf16[128,2176]{1,0:T(8,128)(2,1)}, f32[16,1024]{1,0:T(8,128)}) custom-call(bf16[4,8,32,2048]{3,2,1,0:T(8,128)(2,1)} %bitcast.34, bf16[4,8,32,8]{3,2,1,0:T(8,128)(2,1)} %bitcast.42, bf16[1024,512]{1,0:T(8,128)(2,1)} %wz.3, bf16[1024,512]{1,0:T(8,128)(2,1)} %wx.3, ...), custom_call_target="tpu_custom_call" | custom-call | tf_op jit(solution)/shard_map/pallas_call | solution.py:878
  428.0 0.0 reduce-scatter.5.cloned.1.call-done.ffn
  428.0 0.0 reduce-scatter.3.cloned.1.call-done.mids
  428.0 0.0 copy-done.1
  428.0 0.0 copy-start
  428.0 2.2 copy-done
  430.2 0.0 copy-start.2
  430.2 1.2 copy-done.2
  431.4 0.0 copy-start.3
  431.4 1.1 copy-done.3
  432.5 0.0 copy-start.4
  432.5 1.0 copy-done.4
  433.5 0.0 copy-start.5
  433.5 1.0 copy-done.5
  434.6 0.0 copy-start.6
  434.6 0.8 copy-done.6
  435.4 4.8 %shard_map.455 = (bf16[1024,2048]{1,0:T(8,128)(2,1)}, bf16[256,1024]{1,0:T(8,128)(2,1)}, f32[2048,128]{1,0:T(8,128)}, f32[128,512]{1,0:T(8,128)}, f32[128,512]{1...) custom-call(bf16[1024,2048]{1,0:T(8,128)(2,1)S(1)} %bitcast.27, ...), custom_call_target="tpu_custom_call" | custom-call | tf_op jit(solution)/shard_map/pallas_call | solution.py:1332
  440.3 0.7 copy.59
Async XLA Ops:
  7.2 96.8 %all-gather.5.cloned.1.call-start = ((), (), s32[]{:S(2)}) async-start(), calls=%async_computation.4 | async-start | bytes 1310720 | tf_op jit(solution)/shard_map/all_gather | solution.py:1237
  9.1 123.6 %all-gather.7.cloned.1.call-start = ((), (), s32[]{:S(2)}) async-start(), calls=%async_computation.5 | async-start | bytes 1310720 | tf_op jit(solution)/shard_map/all_gather | solution.py:1256
  12.3 91.8 %copy-start.7 = (s32[1,1024]{1,0:T(1,128)S(1)}, s32[1,1024]{1,0:T(1,128)}, u32[]{:S(2)}) copy-start(s32[1,1024]{1,0:T(1,128)} %param.29) | copy-start | bytes 12292
  104.0 324.0 %reduce-scatter.5.cloned.1.call-start = ((), (), s32[]{:S(2)}) async-start(), calls=%async_computation.3 | async-start | bytes 2621440 | tf_op jit(solution)/shard_map/reduce_scatter | solution.py:1286
  262.1 165.9 %reduce-scatter.3.cloned.1.call-start = ((), (), s32[]{:S(2)}) async-start(), calls=%async_computation.2 | async-start | bytes 8847360 | tf_op jit(solution)/shard_map/reduce_scatter | solution.py:1289
  314.3 113.8 %copy-start.1 = (f32[8,32,1024]{2,1,0:T(8,128)S(1)}, f32[8,32,1024]{2,1,0:T(8,128)}, u32[]{:S(2)}) copy-start(f32[8,32,1024]{2,1,0:T(8,128)} %get-tuple-element.102) | copy-start | bytes 3145732
  428.0 2.2 copy-start
  430.2 1.2 copy-start.2
  431.4 1.1 copy-start.3
  432.5 1.0 copy-start.4
  433.5 1.0 copy-start.5
  434.6 0.8 copy-start.6
Sparse Core Ops, SparseCore 0:
  10.2 44.4 all-gather.4
  104.1 28.5 all-gather.6
  262.2 43.9 reduce-scatter.4
  309.9 78.5 reduce-scatter.2

commit v3 on v2

--- a/solution.py
+++ b/solution.py
@@ -24,10 +24,21 @@
     return lax.dot_general(a, b, (dims, ((), ())), preferred_element_type=f32)
 
 
-def mmx(a, b, dims=NN):
-    return lax.dot_general(
-        a, b, (dims, ((), ())), preferred_element_type=f32, precision=lax.Precision.HIGHEST
-    )
+def parts_of(v, count):
+    terms = []
+    for _ in range(count):
+        term = v.astype(bf16)
+        terms.append(term)
+        v = v - term.astype(f32)
+    return terms
+
+
+def pick(chosen, v, dims=NN, count=3):
+    total = None
+    for term in parts_of(v, count):
+        product = mm(chosen, term, dims)
+        total = product if total is None else total + product
+    return total
 
 
 def iota(shape, axis):
@@ -46,8 +57,9 @@
 
 
 def head_sum(v):
-    owner = (iota((512, 8), 0) // 64 == iota((512, 8), 1)).astype(f32)
-    return mmx(v, owner)
+    owner = (iota((512, 8), 0) // 64 == iota((512, 8), 1)).astype(bf16)
+    high, low = parts_of(v, 2)
+    return mm(high, owner) + mm(low, owner)
 
 
 def softplus(v):
@@ -81,13 +93,11 @@
 def conv_pre(tile, rows, uext, masks, taps):
     lanes = slice(tile * 128, tile * 128 + 128)
     w = taps_of(taps, tile)
-    lags = [uext[8 : 8 + rows, lanes]]
+    pre = uext[8 : 8 + rows, lanes] * w[0:1, :]
     for lag in (1, 2, 3):
-        lags.append(uext[8 - lag : 8 - lag + rows, lanes] * masks[lag - 1])
-    pre = lags[0] * w[0:1, :]
-    for lag in (1, 2, 3):
-        pre = pre + lags[lag] * w[lag : lag + 1, :]
-    return pre, lags
+        shifted = uext[8 - lag : 8 - lag + rows, lanes] * masks[lag - 1]
+        pre = pre + shifted * w[lag : lag + 1, :]
+    return pre
 
 
 def load_inputs(first, rows, proj, segcol, uext, segx):
@@ -108,8 +118,8 @@
     size = softplus(raw)
     logs = size * -jnp.exp(rate[...])
     scaled = logs * LOG2E
-    lower = (iota((rows, rows), 0) >= iota((rows, rows), 1)).astype(f32)
-    cum = mmx(lower, scaled)
+    lower = (iota((rows, rows), 0) >= iota((rows, rows), 1)).astype(bf16)
+    cum = pick(lower, scaled)
     wide = jnp.concatenate([cum, jnp.zeros((rows, 120), f32)], axis=1)
     return raw, size, logs, cum, wide.T[0:8, :]
 
@@ -134,7 +144,7 @@
     masks = conv_masks(rows, segx)
     acts = []
     for tile in range(6):
-        pre, _ = conv_pre(tile, rows, uext, masks, taps)
+        pre = conv_pre(tile, rows, uext, masks, taps)
         acts.append(pre * jax.nn.sigmoid(pre))
     xc = jnp.concatenate(acts[0:4], axis=1)
     bc, cc = acts[4].astype(bf16), acts[5].astype(bf16)
@@ -229,7 +239,7 @@
 
 
 def mixer_bwd_chunk(
-    index, rows, proj, step, seg, segcol, taps, bias, rate, skip, gain, uext, segx, dext,
+    index, rows, proj, step, seg, segcol, taps, bias, rate, skip, gain, uext, segx, slopes, dext,
     dstate, dkv, dqs, mix, ssd_in, states_in, lse_in, dmix, dproj, dstep, dtaps, dheads, dgain, dskip,
 ):
     first = pl.multiple_of(index * rows, rows)
@@ -239,8 +249,10 @@
     masks = conv_masks(rows, segx)
     acts = []
     for tile in range(6):
-        pre, _ = conv_pre(tile, rows, uext, masks, taps)
-        acts.append(pre * jax.nn.sigmoid(pre))
+        pre = conv_pre(tile, rows, uext, masks, taps)
+        sig = jax.nn.sigmoid(pre)
+        acts.append(pre * sig)
+        slopes[:, tile * 128 : tile * 128 + 128] = sig * (1.0 + pre * (1.0 - sig))
     xc = jnp.concatenate(acts[0:4], axis=1)
     bc, cc = acts[4].astype(bf16), acts[5].astype(bf16)
     raw, size, logs, cum, cumr = decays(first, rows, step, bias, rate)
@@ -295,7 +307,7 @@
     dcb = dcbt.astype(bf16)
     db = mm(dcb, cc)
     dc = mm(dcb, bc, TN)
-    upper = (iota((rows, rows), 0) <= iota((rows, rows), 1)).astype(f32)
+    upper = (iota((rows, rows), 0) <= iota((rows, rows), 1)).astype(bf16)
     late = -from_rows
     reach = expand(jnp.exp2(cum)) * tile4(goes_on)
     stb = states_in[index]
@@ -312,14 +324,14 @@
     dxi = mm(bc, dsb) * weight
     dxs = dxs + dxi
     db = db + mm((xs * weight).astype(bf16), dsb, NT)
-    strict = (iota((rows, rows), 0) > iota((rows, rows), 1)).astype(f32)
-    dlog = mmx(strict, head_sum(xs * dxi))
+    strict = (iota((rows, rows), 0) > iota((rows, rows), 1)).astype(bf16)
+    dlog = pick(strict, head_sum(xs * dxi))
     passes = (segc[rows - 1 : rows, :] == before).astype(f32)
     fade = expand(jnp.exp2(last)) * tile4(passes)
     through = jnp.sum(stb.astype(f32) * dst, axis=0, keepdims=True) * fade
     dlog = dlog + head_sum(jnp.broadcast_to(through, (8, 512)))[0:1, :]
     dstate[...] = dst * fade + into_state
-    dlog = dlog + mmx(upper, late) + mmx(upper, jnp.concatenate(to_rows, axis=0), NT)
+    dlog = dlog + pick(upper, late) + pick(upper, jnp.concatenate(to_rows, axis=0), NT)
     dsize = head_sum(dxs * xc) - dlog * jnp.exp(rate[...])
     rate_part = jnp.sum(dlog * logs, axis=0, keepdims=True)
     draw = dsize * jax.nn.sigmoid(raw)
@@ -332,17 +344,17 @@
     for tile in range(6):
         lanes = slice(tile * 128, tile * 128 + 128)
         w = taps_of(taps, tile)
-        pre, lags = conv_pre(tile, rows, uext, masks, taps)
-        sig = jax.nn.sigmoid(pre)
-        dpre = dacts[tile] * (sig * (1.0 + pre * (1.0 - sig)))
+        dpre = dacts[tile] * slopes[:, lanes]
         dext[0:rows, lanes] = dpre
+        u = uext[8 : 8 + rows, lanes]
         du = dpre * w[0:1, :]
+        sums = [jnp.sum(dpre * u, axis=0, keepdims=True)]
         for lag in (1, 2, 3):
-            du = du + dext[lag : lag + rows, lanes] * ahead[lag - 1] * w[lag : lag + 1, :]
+            later = dext[lag : lag + rows, lanes] * ahead[lag - 1]
+            du = du + later * w[lag : lag + 1, :]
+            sums.append(jnp.sum(later * u, axis=0, keepdims=True))
         dproj[here, 512 + tile * 128 : 640 + tile * 128] = du.astype(bf16)
-        sums = jnp.concatenate(
-            [jnp.sum(dpre * shifted, axis=0, keepdims=True) for shifted in lags], axis=0
-        )
+        sums = jnp.concatenate(sums, axis=0)
         dtaps[:, lanes] = dtaps[:, lanes] + sums
     head_parts = jnp.concatenate([bias_part, rate_part], axis=0)
     dheads[...] = dheads[...] + head_parts
@@ -350,11 +362,12 @@
     dskip[...] = dskip[...] + skip_part
     own_seg = seg[0:1, here]
     dos = [dmix[here, 512 + pair * 128 : 640 + pair * 128] for pair in range(2)]
-    owner = (iota((8, 256), 1) // 64 == iota((8, 256), 0)).astype(f32)
-    delta = mmx(
+    owner = (iota((8, 256), 1) // 64 == iota((8, 256), 0)).astype(bf16)
+    delta = pick(
         owner,
         jnp.concatenate(dos, axis=1).astype(f32) * mix[here, 512:768].astype(f32),
         NT,
+        2,
     )
     dqs[...] = jnp.zeros_like(dqs)
 
@@ -414,7 +427,7 @@
 
 def bwd_kernel(count, proj, step, seg, t0, t1, t2, bias, rate, skip, gain, mix, ssd_in,
                states_in, lse_in, dmix, dproj, dstep, dtaps, dheads, dgain, dskip,
-               segcol, uext, segx, dext, dstate, dkv, dqs):
+               segcol, uext, segx, slopes, dext, dstate, dkv, dqs):
     rows = proj.shape[0] // count
     fill_segments(seg, segcol)
     for ref in (dtaps, dheads, dgain, dskip, dstate, dkv):
@@ -423,7 +436,7 @@
 
     def chunk(turn, _):
         mixer_bwd_chunk(count - 1 - turn, rows, proj, step, seg, segcol, (t0, t1, t2), bias,
-                        rate, skip, gain, uext, segx, dext, dstate, dkv, dqs, mix, ssd_in,
+                        rate, skip, gain, uext, segx, slopes, dext, dstate, dkv, dqs, mix, ssd_in,
                         states_in, lse_in, dmix, dproj, dstep, dtaps, dheads, dgain, dskip)
         return 0
 
@@ -472,6 +485,7 @@
             pltpu.VMEM((length + 16, 128), f32),
             pltpu.VMEM((rows + 8, 768), f32),
             pltpu.VMEM((rows + 16, 128), f32),
+            pltpu.VMEM((rows, 768), f32),
             pltpu.VMEM((rows + 8, 768), f32),
             pltpu.VMEM((NST, 512), f32),
             pltpu.VMEM((length, 512), f32),
@@ -703,9 +717,28 @@
     return back, jnp.sum(grad * v * r, axis=0, keepdims=True)
 
 
-def embed_kernel(size, patches, embed, keep_rows, gain, wz, wx, wb, wc, wq, wk, wv, ws,
-                 resid_out, full_out, proj_out, step_out, *scratch):
-    line = Line(scratch, size)
+class Fetch:
+    def __init__(self, sources, places, sems, first=0):
+        self.copies = [
+            pltpu.make_async_copy(source, place, sems.at[first + n])
+            for n, (source, place) in enumerate(zip(sources, places))
+        ]
+
+    def start(self):
+        for copy in self.copies:
+            copy.start()
+
+    def wait(self):
+        for copy in self.copies:
+            copy.wait()
+
+
+def embed_kernel(size, patches, embed, keep_rows, gain, *refs):
+    weights_in, ws = refs[0:7], refs[7]
+    resid_out, full_out, proj_out, step_out = refs[8:12]
+    wz, wx, wb, wc, wq, wk, wv = weights = refs[12:19]
+    fetch = Fetch(weights_in, weights, refs[19])
+    line = Line(refs[20:], size)
     steps, sub = line.steps, line.own.shape[2]
     columns = []
     for ref in (wz, wx, wb, wc, wq, wk, wv):
@@ -728,8 +761,9 @@
             proj_out[:, j, :, start : start + width] = (
                 mm(x, ref[...]).astype(bf16).reshape(size, sub, width)
             )
-        step_out[:, j] = mm(x, ws[...]).reshape(size, sub, ws.shape[1])
-
+        step_out[:, j] = mm(x, ws[...], NT).reshape(size, sub, ws.shape[0])
+
+    fetch.start()
     line.enter()
     produce(0)
 
@@ -742,6 +776,10 @@
 
         ready = line.ready_step(i)
 
+        @pl.when(ready == 0)
+        def _():
+            fetch.wait()
+
         @pl.when(line.inside(ready))
         def _():
             consume(ready)
@@ -752,9 +790,10 @@
     line.leave()
 
 
-def ffn_kernel(size, mix, wmo, wao, resid_one, gain, wg, wu, wd, og_low, og_high, og_mine,
-               resid_grad, ffn_out, resid_out, dmix, grads, gain_grad, hidden_all, gg_all, ug_all,
-               *scratch):
+def ffn_kernel(size, mix, wmo, wao, resid_one, gain, wg_in, wu_in, wd_in, low_in, high_in, og_mine,
+               resid_grad, ffn_out, resid_out, dmix, grads_out, gain_grad, hidden_all, gg_all, ug_all,
+               wg, wu, wd, og_low, og_high, grads, load, *scratch):
+    fetch = Fetch((wg_in, wu_in, wd_in, low_in, high_in), (wg, wu, wd, og_low, og_high), load)
     half = len(scratch) // 2
     one, two = Line(scratch[:half], size), Line(scratch[half:], size)
     steps, sub, width = one.steps, one.own.shape[2], one.own.shape[3]
@@ -822,15 +861,27 @@
             rows = hidden[:, part * half_steps : (part + 1) * half_steps]
             term = mm(cols, rows.reshape(length // 2, units), TN)
             total = term if total is None else total + term
-        grads[here, 2 * units + mixed :] = total.astype(bf16)
+        grads[here, 2 * units : 3 * units] = total.astype(bf16)
+        give(g).start()
+
+    def give(g):
+        here = pl.ds(pl.multiple_of(g * group, group), group)
+        return pltpu.make_async_copy(
+            grads.at[here, 0 : 3 * units], grads_out.at[here, 0 : 3 * units], load.at[5 + g]
+        )
+
+    def given(g, _):
+        give(g).wait()
+        return 0
 
     def mix_grads(g, _):
         here = pl.ds(pl.multiple_of(g * group, group), group)
-        grads[here, 2 * units : 2 * units + mixed] = mm(
+        grads[here, 3 * units :] = mm(
             columns(two.full, g), all_rows(mix[...]), TN
         ).astype(bf16)
         return 0
 
+    fetch.start()
     one.enter()
     gain_grad[...] = jnp.zeros_like(gain_grad)
     produce(0)
@@ -846,6 +897,10 @@
 
         ready_one = one.ready_step(i)
 
+        @pl.when(ready_one == 0)
+        def _():
+            fetch.wait()
+
         @pl.when(jnp.logical_and(ready_one >= 0, ready_one < steps // 2))
         def _():
             middle(ready_one, flat(og_low[:, ready_one]))
@@ -870,16 +925,28 @@
 
     lax.fori_loop(0, steps + lag + two.lag(), iteration, 0)
     lax.fori_loop(0, groups, mix_grads, 0)
+    last = pltpu.make_async_copy(
+        grads.at[:, 3 * units :], grads_out.at[:, 3 * units :], load.at[5 + groups]
+    )
+    last.start()
+    lax.fori_loop(0, groups, given, 0)
+    last.wait()
     one.leave()
     two.leave()
 
 
-def comm_call(body, out_shape, scratch, identity, *args):
+def comm_call(body, out_shape, scratch, identity, *args, kept=(), given=()):
     return pl.pallas_call(
         body,
         out_shape=out_shape,
-        in_specs=[pl.BlockSpec(memory_space=pltpu.VMEM)] * len(args),
-        out_specs=tuple(pl.BlockSpec(memory_space=pltpu.VMEM) for _ in out_shape),
+        in_specs=[
+            pl.BlockSpec(memory_space=pl.ANY if place in kept else pltpu.VMEM)
+            for place in range(len(args))
+        ],
+        out_specs=tuple(
+            pl.BlockSpec(memory_space=pl.ANY if place in given else pltpu.VMEM)
+            for place in range(len(out_shape))
+        ),
         scratch_shapes=scratch,
         compiler_params=pltpu.CompilerParams(
             collective_id=identity, has_side_effects=True, vmem_limit_bytes=62 * 2**20
@@ -1033,8 +1100,10 @@
 
 
 def entry_kernel(size, dp, dproj, dstep, wz, wx, wb, wc, wq, wk, wv, ws, resid_one, gain, resid_grad,
-                 keep_rows, embed, full_one, patches, dtaps, dheads, dgain, dskip, two_gain_grad,
-                 patch_grad, embed_out, in_out, small_out, *scratch):
+                 keep_rows, embed_in, full_in, patches_in, dtaps, dheads, dgain, dskip, two_gain_grad,
+                 patch_out, embed_out, in_out, small_out, full_one, embed, patches, patch_grad, load,
+                 *scratch):
+    fetch = Fetch((full_in, embed_in, patches_in), (full_one, embed, patches), load)
     line = Line(scratch[0:9], size)
     ins = Halving(*scratch[9:13])
     emb = Halving(*scratch[13:17])
@@ -1053,7 +1122,7 @@
         return v.reshape(length, v.shape[3])
 
     def produce(j):
-        total = mm(flat(dstep[:, j]), ws[...], NT)
+        total = mm(flat(dstep[:, j]), ws[...])
         for ref, start in columns:
             total = total + mm(flat(dproj[:, j, :, start : start + ref.shape[1]]), ref[...], NT)
         line.own[:, j] = total.reshape(size, sub, width)
@@ -1066,10 +1135,18 @@
     def consume(d, _):
         x = flat(line.full[d])
         patch_grad[d] = mm(x, embed[...], NT).astype(bf16).reshape(steps, sub, embed.shape[0])
+        give(d).start()
         return 0
 
+    def give(d):
+        return pltpu.make_async_copy(patch_grad.at[d], patch_out.at[d], load.at[3 + d])
+
+    def given(d, _):
+        give(d).wait()
+        return 0
+
     def weight_group(g):
-        x = all_rows(full_one[:, :, :, pl.ds(pl.multiple_of(g * group, group), group)])
+        x = full_one[:, pl.ds(pl.multiple_of(g * group, group), group)]
         here = pl.ds(g * in_group, in_group)
         grad = mm(x, all_rows(dproj[...]), TN).astype(bf16)
         ins.data[here, :, 0:PROJ] = grad.reshape(in_group, ins.rows, PROJ)
@@ -1088,6 +1165,7 @@
         if emb.bits:
             emb.start(0, g * in_group // 2, (g + 1) * in_group // 2)
 
+    fetch.start()
     enter_both(dp, size)
     first = jnp.zeros((16, width), f32)
     small.parts[0] = first
@@ -1097,6 +1175,7 @@
     small.parts[0, 6:8, 0:8] = dheads[...]
     small.parts[0, 8:9] = two_gain_grad[...]
     produce(0)
+    fetch.copies[0].wait()
 
     def iteration(i, _):
         line.move(i, finish)
@@ -1121,6 +1200,8 @@
 
     lax.fori_loop(0, steps + line.lag(), iteration, 0)
     small.start(0)
+    fetch.copies[1].wait()
+    fetch.copies[2].wait()
 
     def each_group(g, _):
         embed_group(g)
@@ -1142,6 +1223,7 @@
     small_out[0:8] = small.parts[dp.bit_length() - 1, 0:8]
     small_out[8:16] = small.parts[hops, 8:16]
     embed_out[...] = emb.data[emb.me]
+    lax.fori_loop(0, size, given, 0)
     line.leave()
     ins.leave()
     emb.leave()
@@ -1150,20 +1232,29 @@
 
 def last_kernel(patch_in, embed_in, ins, mids, small, resid, ffn, place, patch_out, result,
                 embed_out, gz, gx, gb, gc, gq, gk, gv, gs, t0, t1, t2, hb, hr, hs, inner_gain,
-                gmo, gao, ggate, gup, gdown, gain_one, gain_two, sem):
-    move = pltpu.make_async_copy(patch_in, patch_out, sem)
-    move.start()
+                gmo, gao, ggate, gup, gdown, gain_one, gain_two, held, sem):
+    rows = patch_in.shape[0] // 4
+    pieces = [pl.ds(n * rows, rows) for n in range(4)]
+    takes = [pltpu.make_async_copy(patch_in.at[p], held.at[p], sem.at[n]) for n, p in enumerate(pieces)]
+    gives = [pltpu.make_async_copy(held.at[p], patch_out.at[p], sem.at[4 + n]) for n, p in enumerate(pieces)]
+    for take in takes:
+        take.start()
     result[...] = (resid[...] + ffn[...].astype(f32)).astype(bf16)
     start = 0
-    for out in (gz, gx, gb, gc, gq, gk, gv, gs):
+    for out in (gz, gx, gb, gc, gq, gk, gv):
         out[...] = ins[:, start : start + out.shape[1]].astype(f32)
         start = start + out.shape[1]
+    steps_part = ins[:, start:].astype(f32)
+    gs[...] = steps_part.T[0 : gs.shape[0], :] if gs.shape[1] % 128 == 0 else steps_part[:, 0 : gs.shape[1]]
     units, inner = ggate.shape[1], t0.shape[1]
     ggate[...] = mids[:, 0:units].astype(f32)
     gup[...] = mids[:, units : 2 * units].astype(f32)
+    for take, give in zip(takes, gives):
+        take.wait()
+        give.start()
     flipped = mids[:, 2 * units :].astype(f32)
-    outs = ((gmo, flipped[:, 0:inner]), (gao, flipped[:, inner : flipped.shape[1] - units]),
-            (gdown, flipped[:, flipped.shape[1] - units :]), (embed_out, embed_in[...].astype(f32)))
+    outs = ((gdown, flipped[:, 0:units]), (gmo, flipped[:, units : units + inner]),
+            (gao, flipped[:, units + inner :]), (embed_out, embed_in[...].astype(f32)))
     for out, value in outs:
         out[...] = value.T if out.shape != value.shape else value
     t0[...] = small[0:4, 0 : t0.shape[1]]
@@ -1174,11 +1265,12 @@
     hs[...] = small[5:6, 0 : hs.shape[1]]
     inner_gain[...] = small[4:5, 0 : inner_gain.shape[1]]
     width, share = small.shape[1], gain_one.shape[1]
-    chosen = (iota((width, share), 0) == iota((width, share), 1) + place[0] * share).astype(f32)
-    gains = mmx(small[8:16, :], chosen)
+    chosen = (iota((width, share), 0) == iota((width, share), 1) + place[0] * share).astype(bf16)
+    gains = sum(mm(term, chosen) for term in parts_of(small[8:16, :], 3))
     gain_two[...] = gains[0:1, :]
     gain_one[...] = gains[1:2, :]
-    move.wait()
+    for give in gives:
+        give.wait()
 
 
 def shards(
@@ -1229,7 +1321,7 @@
         query_weight,
         key_weight,
         value_weight,
-        step_weight,
+        step_weight.T,
     )
     one_gain, two_gain = first_gain[None], second_gain[None]
     buffers = Line.scratch(size, STEPS, sub, width)
@@ -1244,13 +1336,16 @@
             sds((*shape, PROJ), bf16),
             sds((*shape, step_weight.shape[1]), f32),
         ),
-        buffers,
+        [pltpu.VMEM(member.shape, bf16) for member in in_list[:7]]
+        + [pltpu.SemaphoreType.DMA((7,))]
+        + buffers,
         1,
         patches.reshape(*shape, patches.shape[1]),
         embed_weight,
         keep_rows,
         one_gain,
         *in_list,
+        kept=(4, 5, 6, 7, 8, 9, 10),
     )
     og_low, og_high, projected = lax.optimization_barrier((og_low, og_high, projected))
     og_high = lax.all_gather(og_high, "tp", axis=0)
@@ -1269,7 +1364,18 @@
             rows32, rows16, rows32, sds((*shape, mixed), bf16),
             sds((width, 3 * hidden_width + mixed), bf16), sds((1, width), f32),
         ),
-        [pltpu.VMEM((*shape, hidden_width), bf16)] * 3 + buffers + buffers,
+        [pltpu.VMEM((*shape, hidden_width), bf16)] * 3
+        + [
+            pltpu.VMEM(ffn_gate.shape, bf16),
+            pltpu.VMEM(ffn_up.shape, bf16),
+            pltpu.VMEM(ffn_down.shape, bf16),
+            pltpu.VMEM(half_shape, bf16),
+            pltpu.VMEM(half_shape, bf16),
+            pltpu.VMEM((width, 3 * hidden_width + mixed), bf16),
+            pltpu.SemaphoreType.DMA((6 + width // 256,)),
+        ]
+        + buffers
+        + buffers,
         2,
         mix_in.reshape(*shape, mixed),
         mamba_output,
@@ -1282,6 +1388,8 @@
         og_low.reshape(half_shape),
         og_high.reshape(half_shape),
         out_grad.reshape(STEPS, sub, width),
+        kept=(5, 6, 7, 8, 9),
+        given=(4,),
     )
     ffn_sum = lax.psum_scatter(
         ffn_part.reshape(length, width), "tp", scatter_dimension=0, tiled=True
@@ -1302,7 +1410,14 @@
             sds((block, PROJ + 128), bf16),
             sds((16, width), f32),
         ),
-        buffers
+        [
+            pltpu.VMEM((length, width), bf16),
+            pltpu.VMEM(embed_weight.shape, bf16),
+            pltpu.VMEM((*shape, features), bf16),
+            pltpu.VMEM((*shape, features), bf16),
+            pltpu.SemaphoreType.DMA((3 + size,)),
+        ]
+        + buffers
         + Halving.scratch(dp, block, PROJ + 128)
         + Halving.scratch(dp, block, features)
         + Doubling.scratch(dp, size, 16, width),
@@ -1315,13 +1430,15 @@
         resid_grad,
         keep_rows,
         embed_weight,
-        full_one,
+        full_one.reshape(length, width),
         patches.reshape(*shape, features),
         dtaps,
         dheads,
         dgain,
         dskip,
         second_gain_grad,
+        kept=(14, 15, 16),
+        given=(0,),
     )
     place = (lax.axis_index("dp") * size + lax.axis_index("tp"))[None]
     flip = block % 128 == 0
@@ -1335,7 +1452,8 @@
             sds((length, features), bf16),
             sds((mine, width), bf16),
             turned(features),
-            *[sds((block, member.shape[1]), f32) for member in in_list],
+            *[sds((block, member.shape[1]), f32) for member in in_list[:7]],
+            turned(step_weight.shape[1]),
             *[sds(member.shape, f32) for member in taps],
             *[sds((1, step_bias.shape[0]), f32)] * 3,
             sds((1, inner_width), f32),
@@ -1354,8 +1472,8 @@
             pl.BlockSpec(memory_space=pl.ANY),
             *[pl.BlockSpec(memory_space=pltpu.VMEM)] * 24,
         ),
-        scratch_shapes=[pltpu.SemaphoreType.DMA],
-        compiler_params=pltpu.CompilerParams(vmem_limit_bytes=40 * 2**20),
+        scratch_shapes=[pltpu.VMEM((length, features), bf16), pltpu.SemaphoreType.DMA((8,))],
+        compiler_params=pltpu.CompilerParams(vmem_limit_bytes=60 * 2**20),
     )(
         patches_grad.reshape(length, features),
         embed_sum,
@@ -1370,7 +1488,9 @@
         patches_grad, result, embed_cols, gz, gx, gb, gc, gq, gk, gv, gs, t0, t1, t2, hb, hr, hs,
         inner_grad, gmo, gao, ggate, gup, gdown, gain_one, gain_two,
     ) = outs
-    if not flip:
+    if flip:
+        gs = gs.T
+    else:
         embed_cols, gmo, gao, gdown = embed_cols.T, gmo.T, gao.T, gdown.T
     return (
         result,

time: 448 us -> 434 us (0.969)
  local copies, waits for them, and re-layouts: 12.3 us -> 2.72 us
  Pallas kernels: 416 us -> 410 us
    unnamed x18 -> x2, local copies, waits for them, and re-layouts: 9.59 us -> 0.01 us
    pallas_call x1, Pallas kernels: 51.6 us -> 43.8 us  [mixer_bwd(): pl.pallas_call(functools.partial(bwd_kernel, count), out_shape=(jax.Shape...]
  transfers between devices with their start and end apart: 4 -> 4, of which waited for: 1 -> 1; matrix products, arithmetic and copies ran while one was open for 1% -> 0% of each run, Pallas kernels for 63% -> 64%
where the time goes in v3:
time: 434 us; the launch traced here: 433 us
  Pallas kernels  410 us (94%)
  between operations  13.9 us (3%)
  waiting for transfers between devices  4.81 us (1%)
    pallas_call x3, Pallas kernels, comm_call(): pl.pallas_call(body, out_shape=out_shape, in_specs=[pl.BlockSpec(memory_s...  335 us
    pallas_call x1, Pallas kernels, mixer_bwd(): pl.pallas_call(functools.partial(bwd_kernel, count), out_shape=(jax.Shape...  43.8 us
    pallas_call x1, Pallas kernels, mixer_fwd(): pl.pallas_call(functools.partial(fwd_kernel, count), out_shape=(jax.Shape...  24.4 us
  transfers between devices with their start and end apart: 4, of which 1 were waited for; matrix products, arithmetic and copies ran while one was open for 0% of the time, Pallas kernels for 64%

profile of v3, /device:TPU:0, one launch (start us, length us, event | category | flops | bytes accessed | tf_op | source)
XLA Modules:
  0.0 433.4 jit_solution(16334300938383891474)
XLA Ops:
  7.2 0.0 all-gather.5.cloned.1.call-start
  7.2 1.9 fusion
  9.1 0.0 all-gather.5.cloned.1.call-update
  9.1 0.0 all-gather.7.cloned.1.call-start
  9.2 0.7 convert_element_type.7
  9.9 0.9 reshape.114.keep_rows
  10.7 0.0 copy-start
  10.7 90.6 %shard_map.450 = (f32[8,32,1024]{2,1,0:T(8,128)}, bf16[4,8,32,1024]{3,2,1,0:T(8,128)(2,1)}, bf16[4,8,32,2048]{3,2,1,0:T(8,128)(2,1)}, f32[4,8,32,8]{3,2,1,0:T(8,128)}) custom-call(bf16[4,8,32,2048]{3,2,1,0:T(8,128)(2,1)} %bitcast.30, bf16[2048,1024]{1,0:T(8,128)(2,1)} %embed_in.1, f32[8,32,1]{2,1,0:T(8,128)} %reshape.114.keep_rows, f32[1,1024]{1,0:T(1,128)} %bitcast.49, ...), custom_call_target="tpu_custom_call" | custom-call | tf_op jit(solution)/shard_map/pallas_call | solution.py:939
  101.4 0.0 all-gather.5.cloned.1.call-done
  101.4 0.0 all-gather.7.cloned.1.call-update
  101.4 0.0 reduce-scatter.5.cloned.1.call-start
  101.5 0.0 copy-done
  101.5 0.6 convert_element_type.8.seg
  102.1 24.4 %shard_map.451 = (bf16[1024,768]{1,0:T(8,128)(2,1)}, bf16[1024,512]{1,0:T(8,128)(2,1)}, bf16[4,128,512]{2,1,0:T(8,128)(2,1)}, f32[8,1024]{1,0:T(8,128)}) custom-call(bf16[1024,2048]{1,0:T(8,128)(2,1)} %bitcast.32, f32[1024,8]{1,0:T(8,128)} %bitcast.38, f32[1,1024]{1,0:T(1,128)} %convert_element_type.8.seg, f32[4,512]{1,0:T(4,128)} %t0.3, f32[4,128]{1,0:T(4,128)} %t1.3, ...), custom_call_target="tpu_custom_call" | custom-call | tf_op jit(solution)/shard_map/pallas_call | solution.py:451
  126.5 4.4 %all-gather.7.cloned.1.call-done = bf16[512,1024]{1,0:T(8,128)(2,1)} async-done(((bf16[128,1024]{1,0:T(8,128)(2,1)}), bf16[512,1024]{1,0:T(8,128)(2,1)}) %all-gather.7.cloned.1.call-update) | async-done | bytes 1048592 | tf_op jit(solution)/shard_map/all_gather | solution.py:1351
  130.9 125.8 %shard_map.452 = (f32[8,32,1024]{2,1,0:T(8,128)}, bf16[4,8,32,1024]{3,2,1,0:T(8,128)(2,1)}, f32[8,32,1024]{2,1,0:T(8,128)}, bf16[4,8,32,768]{3,2,1,0:T(8,128)(2,...) custom-call(bf16[4,8,32,768]{3,2,1,0:T(8,128)(2,1)} %bitcast.34, bf16[512,1024]{1,0:T(8,128)(2,1)} %wmo.1, ...), custom_call_target="tpu_custom_call" | custom-call | tf_op jit(solution)/shard_map/pallas_call | solution.py:939
  256.7 0.0 reduce-scatter.5.cloned.1.call-update
  256.7 0.3 reduce-scatter.3.cloned.1.call-start
  257.0 0.3 reduce-scatter.3.cloned.1.call-update
  257.3 43.8 %shard_map.453 = (bf16[1024,2048]{1,0:T(8,128)(2,1)}, bf16[1024,8]{1,0:T(8,128)(2,1)}, f32[4,768]{1,0:T(4,128)}, f32[2,8]{1,0:T(2,128)}, f32[1,512]{1,0:T(1,128)}, /*index=5*/f32[1,512]{1,0:T(1,128)}) custom-call(bf16[1024,2048]{1,0:T(8,128)(2,1)} %bitcast.33, f32[1024,8]{1,0:T(8,128)} %bitcast.39, f32[1,1024]{1,0:T(1,128)} %convert_element_type.8.seg, ...), custom_call_target="tpu_custom_call" | custom-call | tf_op jit(solution)/shard_map/pallas_call | solution.py:474
  301.1 118.1 %shard_map.454 = (bf16[4,8,32,2048]{3,2,1,0:T(8,128)(2,1)}, bf16[128,2048]{1,0:T(8,128)(2,1)}, bf16[128,2176]{1,0:T(8,128)(2,1)}, f32[16,1024]{1,0:T(8,128)}) custom-call(bf16[4,8,32,2048]{3,2,1,0:T(8,128)(2,1)} %bitcast.35, bf16[4,8,32,8]{3,2,1,0:T(8,128)(2,1)} %bitcast.46, bf16[1024,512]{1,0:T(8,128)(2,1)} %wz.1, bf16[1024,512]{1,0:T(8,128)(2,1)} %wx.1, ...), custom_call_target="tpu_custom_call" | custom-call | tf_op jit(solution)/shard_map/pallas_call | solution.py:939
  419.2 0.0 reduce-scatter.5.cloned.1.call-done.ffn
  419.3 0.0 reduce-scatter.3.cloned.1.call-done.mids
  419.3 7.5 %shard_map.455 = (bf16[1024,2048]{1,0:T(8,128)(2,1)}, bf16[256,1024]{1,0:T(8,128)(2,1)}, f32[2048,128]{1,0:T(8,128)}, f32[128,512]{1,0:T(8,128)}, f32[128,512]{1...) custom-call(bf16[1024,2048]{1,0:T(8,128)(2,1)} %bitcast.36, ...), custom_call_target="tpu_custom_call" | custom-call | tf_op jit(solution)/shard_map/pallas_call | solution.py:1449
Async XLA Ops:
  7.2 94.2 %all-gather.5.cloned.1.call-start = ((), (), s32[]{:S(2)}) async-start(), calls=%async_computation.4 | async-start | bytes 1310720 | tf_op jit(solution)/shard_map/all_gather | solution.py:1329
  9.1 121.7 %all-gather.7.cloned.1.call-start = ((), (), s32[]{:S(2)}) async-start(), calls=%async_computation.5 | async-start | bytes 1310720 | tf_op jit(solution)/shard_map/all_gather | solution.py:1351
  10.7 90.7 %copy-start = (s32[1,1024]{1,0:T(1,128)S(1)}, s32[1,1024]{1,0:T(1,128)}, u32[]{:S(2)}) copy-start(s32[1,1024]{1,0:T(1,128)} %param.29) | copy-start | bytes 12292
  101.4 317.8 %reduce-scatter.5.cloned.1.call-start = ((), (), s32[]{:S(2)}) async-start(), calls=%async_computation.3 | async-start | bytes 2621440 | tf_op jit(solution)/shard_map/reduce_scatter | solution.py:1394
  256.7 162.5 %reduce-scatter.3.cloned.1.call-start = ((), (), s32[]{:S(2)}) async-start(), calls=%async_computation.2 | async-start | bytes 8847360 | tf_op jit(solution)/shard_map/reduce_scatter | solution.py:1397
Sparse Core Ops, SparseCore 0:
  10.2 44.6 all-gather.4
  101.5 29.2 all-gather.6
  256.9 43.9 reduce-scatter.4
  304.5 92.8 reduce-scatter.2

commit v4 on v3

--- a/solution.py
+++ b/solution.py
@@ -135,7 +135,7 @@
 
 def mixer_fwd_chunk(
     index, rows, proj, step, seg, segcol, taps, bias, rate, skip, gain, uext, segx, state,
-    oacc, stats, mix_out, ssd_out, states_out, lse_out,
+    oacc, stats, mix_out, ssd_out, states_out, lse_out, hook,
 ):
     first = pl.multiple_of(index * rows, rows)
     here = pl.ds(first, rows)
@@ -156,6 +156,7 @@
     wide_seg = jnp.concatenate([segc] * (rows // 128), axis=1)
     allowed = (iota((rows, rows), 0) >= iota((rows, rows), 1)) & (wide_seg == segr)
     away = jnp.where(allowed, 0.0, LOW)
+    hook(0)
     cb = mm(cc, bc, NT)
     xs = xc * expand(size)
     xsb = xs.astype(bf16)
@@ -168,6 +169,8 @@
         xp = xsb[:, pair * 128 : pair * 128 + 128]
         rhs = jnp.concatenate([keep(halves[0], xp), keep(halves[1], xp)], axis=0)
         parts.append(mm(jnp.concatenate(lhs, axis=1), rhs))
+        if pair == 1:
+            hook(1)
     ssd = jnp.concatenate(parts, axis=1) + xc * expand(skip[...])
     st = state[...]
     stb = st.astype(bf16)
@@ -179,11 +182,13 @@
     added = mm(bc, (xs * weight).astype(bf16), TN)
     passes = (segc[rows - 1 : rows, :] == before).astype(f32)
     state[...] = st * (expand(jnp.exp2(last)) * tile4(passes)) + added
+    hook(2)
     ssd_out[here, :] = ssd.astype(bf16)
     z = proj[here, 0:512].astype(f32)
     g = ssd * (z * jax.nn.sigmoid(z))
     r = lax.rsqrt(jnp.mean(g * g, axis=1, keepdims=True) + eps)
     mix_out[here, 0:512] = (g * r * gain[...]).astype(bf16)
+    hook(3)
     own_seg = seg[0:1, here]
 
     def keys(block, fresh):
@@ -241,6 +246,7 @@
 def mixer_bwd_chunk(
     index, rows, proj, step, seg, segcol, taps, bias, rate, skip, gain, uext, segx, slopes, dext,
     dstate, dkv, dqs, mix, ssd_in, states_in, lse_in, dmix, dproj, dstep, dtaps, dheads, dgain, dskip,
+    begin,
 ):
     first = pl.multiple_of(index * rows, rows)
     here = pl.ds(first, rows)
@@ -255,6 +261,7 @@
         slopes[:, tile * 128 : tile * 128 + 128] = sig * (1.0 + pre * (1.0 - sig))
     xc = jnp.concatenate(acts[0:4], axis=1)
     bc, cc = acts[4].astype(bf16), acts[5].astype(bf16)
+    begin()
     raw, size, logs, cum, cumr = decays(first, rows, step, bias, rate)
     z = proj[here, 0:512].astype(f32)
     ssd = ssd_in[here, :].astype(f32)
@@ -409,70 +416,54 @@
     dproj[here, 1536:2048] = dkv[here, :].astype(bf16)
 
 
-def fwd_kernel(count, proj, step, seg, t0, t1, t2, bias, rate, skip, gain,
-               mix_out, ssd_out, states_out, lse_out, segcol, uext, segx, state, oacc, stats):
+def bwd_kernel(count, dp, proj, step, seg, t0, t1, t2, bias, rate, skip, gain, mix, ssd_in,
+               states_in, lse_in, dmix, grads_in, dproj, dstep, dtaps, dheads, dgain, dskip,
+               grads_out, segcol, uext, segx, slopes, dext, dstate, dkv, dqs, load, *scratch):
     rows = proj.shape[0] // count
-    fill_segments(seg, segcol)
-    lse_out[...] = jnp.zeros_like(lse_out)
-    state[...] = jnp.zeros_like(state)
-
-    def chunk(index, _):
-        mixer_fwd_chunk(index, rows, proj, step, seg, segcol, (t0, t1, t2), bias, rate, skip,
-                        gain, uext, segx, state, oacc, stats, mix_out, ssd_out, states_out,
-                        lse_out)
-        return 0
-
-    lax.fori_loop(0, count, chunk, 0)
-
-
-def bwd_kernel(count, proj, step, seg, t0, t1, t2, bias, rate, skip, gain, mix, ssd_in,
-               states_in, lse_in, dmix, dproj, dstep, dtaps, dheads, dgain, dskip,
-               segcol, uext, segx, slopes, dext, dstate, dkv, dqs):
-    rows = proj.shape[0] // count
+    sums = Halving(*scratch)
+    take = pltpu.make_async_copy(grads_in, sums.data, load)
+    take.start()
+    enter_pairs(dp)
     fill_segments(seg, segcol)
     for ref in (dtaps, dheads, dgain, dskip, dstate, dkv):
         ref[...] = jnp.zeros_like(ref)
     dext[0:8, :] = jnp.zeros((8, 768), f32)
 
     def chunk(turn, _):
+        def begin():
+            @pl.when(turn == 0)
+            def _():
+                take.wait()
+                if sums.bits:
+                    sums.start(0)
+
         mixer_bwd_chunk(count - 1 - turn, rows, proj, step, seg, segcol, (t0, t1, t2), bias,
                         rate, skip, gain, uext, segx, slopes, dext, dstate, dkv, dqs, mix, ssd_in,
-                        states_in, lse_in, dmix, dproj, dstep, dtaps, dheads, dgain, dskip)
+                        states_in, lse_in, dmix, dproj, dstep, dtaps, dheads, dgain, dskip,
+                        begin)
+        for stage in range(sums.bits):
+
+            @pl.when(turn == -(-stage * (count - 1) // max(sums.bits - 1, 1)))
+            def _(stage=stage):
+                sums.finish(stage)
+                if stage + 1 < sums.bits:
+                    sums.start(stage + 1)
+
         return 0
 
     lax.fori_loop(0, count, chunk, 0)
+    grads_out[...] = sums.data[sums.me]
+    sums.leave()
     dskip8 = head_sum(jnp.broadcast_to(dskip[...], (8, 512)))
     dskip[0:1, 0:8] = dskip8[0:1, :]
 
 
-def mixer_fwd(count, proj, step, seg, taps, bias, rate, skip, gain):
+def mixer_bwd(count, proj, step, seg, taps, bias, rate, skip, gain, mix, ssd, states, lse, dmix, grads):
     length = proj.shape[0]
     rows = length // count
+    dp, block, columns = grads.shape
     return pl.pallas_call(
-        functools.partial(fwd_kernel, count),
-        out_shape=(
-            jax.ShapeDtypeStruct((length, 768), bf16),
-            jax.ShapeDtypeStruct((length, 512), bf16),
-            jax.ShapeDtypeStruct((count, NST, 512), bf16),
-            jax.ShapeDtypeStruct((8, length), f32),
-        ),
-        scratch_shapes=[
-            pltpu.VMEM((length + 16, 128), f32),
-            pltpu.VMEM((rows + 8, 768), f32),
-            pltpu.VMEM((rows + 16, 128), f32),
-            pltpu.VMEM((NST, 512), f32),
-            pltpu.VMEM((256, rows), f32),
-            pltpu.VMEM((8, rows), f32),
-        ],
-        compiler_params=pltpu.CompilerParams(vmem_limit_bytes=60 * 2**20),
-    )(proj, step, seg, *taps, bias, rate, skip, gain)
-
-
-def mixer_bwd(count, proj, step, seg, taps, bias, rate, skip, gain, mix, ssd, states, lse, dmix):
-    length = proj.shape[0]
-    rows = length // count
-    return pl.pallas_call(
-        functools.partial(bwd_kernel, count),
+        functools.partial(bwd_kernel, count, dp),
         out_shape=(
             jax.ShapeDtypeStruct((length, 2048), bf16),
             jax.ShapeDtypeStruct((length, 8), bf16),
@@ -480,7 +471,10 @@
             jax.ShapeDtypeStruct((2, 8), f32),
             jax.ShapeDtypeStruct((1, 512), f32),
             jax.ShapeDtypeStruct((1, 512), f32),
+            jax.ShapeDtypeStruct((block, columns), bf16),
         ),
+        in_specs=[pl.BlockSpec(memory_space=pltpu.VMEM)] * 15
+        + [pl.BlockSpec(memory_space=pl.ANY)],
         scratch_shapes=[
             pltpu.VMEM((length + 16, 128), f32),
             pltpu.VMEM((rows + 8, 768), f32),
@@ -490,9 +484,13 @@
             pltpu.VMEM((NST, 512), f32),
             pltpu.VMEM((length, 512), f32),
             pltpu.VMEM((256, rows), f32),
-        ],
-        compiler_params=pltpu.CompilerParams(vmem_limit_bytes=60 * 2**20),
-    )(proj, step, seg, *taps, bias, rate, skip, gain, mix, ssd, states, lse, dmix)
+            pltpu.SemaphoreType.DMA,
+        ]
+        + Halving.scratch(dp, block, columns),
+        compiler_params=pltpu.CompilerParams(
+            collective_id=5, has_side_effects=True, vmem_limit_bytes=60 * 2**20
+        ),
+    )(proj, step, seg, *taps, bias, rate, skip, gain, mix, ssd, states, lse, dmix, grads)
 
 
 MESH = pl.DeviceIdType.MESH
@@ -702,6 +700,98 @@
         lax.fori_loop(0, self.steps, step, 0)
 
 
+HOOKS = 4
+
+
+def fwd_kernel(count, proj, step, seg, t0, t1, t2, bias, rate, skip, gain, rows_in,
+               mix_out, ssd_out, states_out, lse_out, rows_out, segcol, uext, segx, state, oacc, stats,
+               gathered, ss, sr, load):
+    rows = proj.shape[0] // count
+    ring = Gather(gathered, ss, sr)
+    mine = pltpu.make_async_copy(rows_in, gathered.at[ring.me], load.at[0])
+    mine.start()
+    ring.enter()
+    mine.wait()
+    ring.send_own()
+    fill_segments(seg, segcol)
+    lse_out[...] = jnp.zeros_like(lse_out)
+    state[...] = jnp.zeros_like(state)
+
+    hooks = count * (HOOKS + 1)
+    assert hooks >= ring.turns
+
+    def chunk(index, _):
+        def hook(k):
+            place = index * (HOOKS + 1) + k
+            turn = place * ring.turns // hooks
+
+            @pl.when((place + 1) * ring.turns // hooks > turn)
+            def _():
+                ring.move(turn)
+
+        mixer_fwd_chunk(index, rows, proj, step, seg, segcol, (t0, t1, t2), bias, rate, skip,
+                        gain, uext, segx, state, oacc, stats, mix_out, ssd_out, states_out,
+                        lse_out, hook)
+        hook(HOOKS)
+        return 0
+
+    lax.fori_loop(0, count, chunk, 0)
+
+    give = pltpu.make_async_copy(gathered, rows_out, load.at[1])
+    give.start()
+    ring.leave()
+    give.wait()
+
+
+def mixer_fwd(count, proj, step, seg, taps, bias, rate, skip, gain, own_rows):
+    length = proj.shape[0]
+    rows = length // count
+    width = own_rows.shape[2]
+    pieces = own_rows.shape[0]
+    shape = (count, *own_rows.shape)
+    return pl.pallas_call(
+        functools.partial(fwd_kernel, count),
+        out_shape=(
+            jax.ShapeDtypeStruct((length, 768), bf16),
+            jax.ShapeDtypeStruct((length, 512), bf16),
+            jax.ShapeDtypeStruct((count, NST, 512), bf16),
+            jax.ShapeDtypeStruct((8, length), f32),
+            jax.ShapeDtypeStruct(shape, bf16),
+        ),
+        in_specs=[pl.BlockSpec(memory_space=pltpu.VMEM)] * 10
+        + [pl.BlockSpec(memory_space=pl.ANY)],
+        out_specs=(
+            *[pl.BlockSpec(memory_space=pltpu.VMEM)] * 4,
+            pl.BlockSpec(memory_space=pl.ANY),
+        ),
+        scratch_shapes=[
+            pltpu.VMEM((length + 16, 128), f32),
+            pltpu.VMEM((rows + 8, 768), f32),
+            pltpu.VMEM((rows + 16, 128), f32),
+            pltpu.VMEM((NST, 512), f32),
+            pltpu.VMEM((256, rows), f32),
+            pltpu.VMEM((8, rows), f32),
+            pltpu.VMEM(shape, bf16),
+            pltpu.SemaphoreType.DMA((2, count, pieces)),
+            pltpu.SemaphoreType.DMA((2, count, pieces)),
+            pltpu.SemaphoreType.DMA((2,)),
+        ],
+        compiler_params=pltpu.CompilerParams(
+            collective_id=4, has_side_effects=True, vmem_limit_bytes=60 * 2**20
+        ),
+    )(proj, step, seg, *taps, bias, rate, skip, gain, own_rows)
+
+
+def enter_pairs(dp):
+    barrier = pltpu.get_barrier_semaphore()
+    me = lax.axis_index("dp")
+    bits = dp.bit_length() - 1
+    for b in range(bits):
+        flip = (1 - 2 * lax.rem(me // 2**b, 2)) * 2**b
+        pl.semaphore_signal(barrier, inc=1, device_id={"dp": me + flip}, device_id_type=MESH)
+    pl.semaphore_wait(barrier, bits)
+
+
 def flat(v):
     return v.reshape(v.shape[0] * v.shape[1], v.shape[2])
 
@@ -715,6 +805,85 @@
     a = grad * gain
     back = r * a - (r * r * r) * v * jnp.mean(a * v, axis=1, keepdims=True)
     return back, jnp.sum(grad * v * r, axis=0, keepdims=True)
+
+
+class Gather:
+    def __init__(self, full, ss, sr):
+        self.full, self.ss, self.sr = full, ss, sr
+        self.size, self.pieces = full.shape[0], full.shape[1]
+        self.me = lax.axis_index("tp")
+        self.last = self.size - 1
+        self.turns = self.pieces + 2 * self.last
+
+    enter = Line.enter
+
+    def copy(self, way, d, j):
+        return pltpu.make_async_remote_copy(
+            src_ref=self.full.at[d, j],
+            dst_ref=self.full.at[d, j],
+            send_sem=self.ss.at[way, d, j],
+            recv_sem=self.sr.at[way, d, j],
+            device_id={"tp": self.me + 1 if way == 0 else self.me - 1},
+            device_id_type=MESH,
+        )
+
+    def sends(self, way):
+        return self.me < self.last if way == 0 else self.me > 0
+
+    def send_own(self):
+        def piece(j, _):
+            for way in range(2):
+
+                @pl.when(self.sends(way))
+                def _(way=way):
+                    self.copy(way, self.me, j).start()
+
+            return 0
+
+        lax.fori_loop(0, self.pieces, piece, 0)
+
+    def arrived(self, way, d, j):
+        @pl.when(jnp.logical_and(j >= 0, j < self.pieces))
+        def _():
+            self.copy(way, d, j).wait_recv()
+
+            @pl.when(self.sends(way))
+            def _():
+                self.copy(way, d, j).start()
+
+    def move(self, turn):
+        def from_left(d, _):
+            self.arrived(0, d, turn - 2 * (self.me - d) + 1)
+            return 0
+
+        def from_right(d, _):
+            self.arrived(1, d, turn - 2 * (d - self.me) + 1)
+            return 0
+
+        lax.fori_loop(0, self.me, from_left, 0)
+        lax.fori_loop(self.me + 1, self.size, from_right, 0)
+
+    def leave(self):
+        def piece(j, _):
+            def right(d, _):
+                self.copy(0, d, j).wait_send()
+                return 0
+
+            def left(d, _):
+                self.copy(1, d, j).wait_send()
+                return 0
+
+            @pl.when(self.me < self.last)
+            def _():
+                lax.fori_loop(0, self.me + 1, right, 0)
+
+            @pl.when(self.me > 0)
+            def _():
+                lax.fori_loop(self.me, self.size, left, 0)
+
+            return 0
+
+        lax.fori_loop(0, self.pieces, piece, 0)
 
 
 class Fetch:
@@ -790,10 +959,10 @@
     line.leave()
 
 
-def ffn_kernel(size, mix, wmo, wao, resid_one, gain, wg_in, wu_in, wd_in, low_in, high_in, og_mine,
+def ffn_kernel(size, mix, wmo, wao, resid_one, gain, wg_in, wu_in, wd_in, og_in, og_mine,
                resid_grad, ffn_out, resid_out, dmix, grads_out, gain_grad, hidden_all, gg_all, ug_all,
-               wg, wu, wd, og_low, og_high, grads, load, *scratch):
-    fetch = Fetch((wg_in, wu_in, wd_in, low_in, high_in), (wg, wu, wd, og_low, og_high), load)
+               wg, wu, wd, og_full, grads, load, *scratch):
+    fetch = Fetch((wg_in, wu_in, wd_in, og_in), (wg, wu, wd, og_full), load)
     half = len(scratch) // 2
     one, two = Line(scratch[:half], size), Line(scratch[half:], size)
     steps, sub, width = one.steps, one.own.shape[2], one.own.shape[3]
@@ -817,8 +986,9 @@
         resid_out[j] = rows
         return normed(rows, gain[...]).astype(bf16)
 
-    def middle(j, og):
+    def middle(j):
         x = flat(one.full[:, j])
+        og = flat(og_full[:, j])
         gate, up = mm(x, wg[...]), mm(x, wu[...])
         hg = mm(og, wd[...], NT)
         sig = jax.nn.sigmoid(gate)
@@ -852,22 +1022,14 @@
         x = columns(one.full, g)
         grads[here, 0:units] = mm(x, all_rows(gg_all[...]), TN).astype(bf16)
         grads[here, units : 2 * units] = mm(x, all_rows(ug_all[...]), TN).astype(bf16)
-        half_steps = steps // 2
-        hidden = hidden_all[...]
-        total = None
-        for part, og in enumerate((og_low, og_high)):
-            cols = og[:, :, :, pl.ds(pl.multiple_of(g * group, group), group)]
-            cols = cols.reshape(length // 2, group)
-            rows = hidden[:, part * half_steps : (part + 1) * half_steps]
-            term = mm(cols, rows.reshape(length // 2, units), TN)
-            total = term if total is None else total + term
+        total = mm(columns(og_full, g), all_rows(hidden_all[...]), TN)
         grads[here, 2 * units : 3 * units] = total.astype(bf16)
         give(g).start()
 
     def give(g):
         here = pl.ds(pl.multiple_of(g * group, group), group)
         return pltpu.make_async_copy(
-            grads.at[here, 0 : 3 * units], grads_out.at[here, 0 : 3 * units], load.at[5 + g]
+            grads.at[here, 0 : 3 * units], grads_out.at[here, 0 : 3 * units], load.at[4 + g]
         )
 
     def given(g, _):
@@ -901,13 +1063,9 @@
         def _():
             fetch.wait()
 
-        @pl.when(jnp.logical_and(ready_one >= 0, ready_one < steps // 2))
-        def _():
-            middle(ready_one, flat(og_low[:, ready_one]))
-
-        @pl.when(jnp.logical_and(ready_one >= steps // 2, ready_one < steps))
-        def _():
-            middle(ready_one, flat(og_high[:, ready_one - steps // 2]))
+        @pl.when(one.inside(ready_one))
+        def _():
+            middle(ready_one)
 
         ready_two = two.ready_step(i - lag)
 
@@ -926,7 +1084,7 @@
     lax.fori_loop(0, steps + lag + two.lag(), iteration, 0)
     lax.fori_loop(0, groups, mix_grads, 0)
     last = pltpu.make_async_copy(
-        grads.at[:, 3 * units :], grads_out.at[:, 3 * units :], load.at[5 + groups]
+        grads.at[:, 3 * units :], grads_out.at[:, 3 * units :], load.at[4 + groups]
     )
     last.start()
     lax.fori_loop(0, groups, given, 0)
@@ -1022,13 +1180,19 @@
 
         lax.fori_loop(low, self.open(stage) if high is None else high, one, 0)
 
+    def take(self, half, stage, e):
+        self.copy(half, stage, e).wait_recv()
+        place, part = self.block(half, stage, e, False), self.part(half)
+        got = self.got[self.slot(stage, e), part]
+        self.data[place, part] = self.data[place, part] + got
+
     def finish(self, stage):
         def one(e, _):
             for half in range(2):
                 self.copy(half, stage, e).wait_recv()
                 place, part = self.block(half, stage, e, False), self.part(half)
                 got = self.got[self.slot(stage, e), part]
-                self.data[place, part] = (self.data[place, part].astype(f32) + got.astype(f32)).astype(bf16)
+                self.data[place, part] = self.data[place, part] + got
             return 0
 
         lax.fori_loop(0, self.open(stage), one, 0)
@@ -1203,23 +1367,78 @@
     fetch.copies[1].wait()
     fetch.copies[2].wait()
 
-    def each_group(g, _):
-        embed_group(g)
-        return 0
-
-    lax.fori_loop(0, groups, each_group, 0)
-    lax.fori_loop(0, size, consume, 0)
     in_out[...] = ins.data[ins.me]
     hops = len(small.hops)
-    for turn in range(max(hops, emb.bits)):
+
+    def small_turn(turn):
         if turn < hops:
             small.finish(turn)
             if turn + 1 < hops:
                 small.start(turn + 1)
-        if turn < emb.bits:
-            emb.finish(turn)
-            if turn + 1 < emb.bits:
-                emb.start(turn + 1)
+
+    if emb.bits == 3:
+        mid, top = emb.bit(1), emb.bit(2)
+        far_mid, far_top = 1 - mid, 1 - top
+
+        def each_turn(t, _):
+            g_mid = mid + (1 - t // 2) * (far_mid - mid)
+            g_top = top + (1 - lax.rem(t, 2)) * (far_top - top)
+            embed_group(g_mid + 2 * g_top)
+
+            @pl.when(t == 1)
+            def _():
+                for half in range(2):
+                    emb.take(half, 0, far_mid + 2 * far_top)
+                emb.copy(0, 1, far_top).start()
+                emb.copy(1, 1, far_mid).start()
+
+            @pl.when(t == 2)
+            def _():
+                for half in range(2):
+                    emb.take(half, 0, far_mid + 2 * top)
+                emb.copy(0, 1, top).start()
+
+            @pl.when(t == 3)
+            def _():
+                for half in range(2):
+                    emb.take(half, 0, mid + 2 * far_top)
+                emb.copy(1, 1, mid).start()
+
+            return 0
+
+        lax.fori_loop(0, groups, each_turn, 0)
+        small_turn(0)
+        for half in range(2):
+            emb.take(half, 0, mid + 2 * top)
+        lax.fori_loop(0, size // 2, consume, 0)
+        small_turn(1)
+        emb.take(0, 1, far_top)
+        emb.copy(0, 2, 0).start()
+        emb.take(1, 1, far_mid)
+        emb.copy(1, 2, 0).start()
+        lax.fori_loop(size // 2, size, consume, 0)
+        small_turn(2)
+        emb.take(0, 1, top)
+        emb.take(1, 1, mid)
+        small_turn(3)
+        emb.take(0, 2, 0)
+        emb.take(1, 2, 0)
+        for turn in range(4, hops):
+            small_turn(turn)
+    else:
+
+        def each_group(g, _):
+            embed_group(g)
+            return 0
+
+        lax.fori_loop(0, groups, each_group, 0)
+        lax.fori_loop(0, size, consume, 0)
+        for turn in range(max(hops, emb.bits)):
+            small_turn(turn)
+            if turn < emb.bits:
+                emb.finish(turn)
+                if turn + 1 < emb.bits:
+                    emb.start(turn + 1)
     small_out[0:8] = small.parts[dp.bit_length() - 1, 0:8]
     small_out[8:16] = small.parts[hops, 8:16]
     embed_out[...] = emb.data[emb.me]
@@ -1325,9 +1544,6 @@
     )
     one_gain, two_gain = first_gain[None], second_gain[None]
     buffers = Line.scratch(size, STEPS, sub, width)
-    og_low, og_high = out_grad[: mine // 2], out_grad[mine // 2 :]
-    og_low = lax.all_gather(og_low, "tp", axis=0)
-
     resid_one, full_one, projected, step_raw = comm_call(
         functools.partial(embed_kernel, size),
         (
@@ -1347,17 +1563,17 @@
         *in_list,
         kept=(4, 5, 6, 7, 8, 9, 10),
     )
-    og_low, og_high, projected = lax.optimization_barrier((og_low, og_high, projected))
-    og_high = lax.all_gather(og_high, "tp", axis=0)
     projected = projected.reshape(length, PROJ)
     step_raw = step_raw.reshape(length, step_weight.shape[1])
-    mix_in, ssd, states, lse = mixer_fwd(size, projected, step_raw, seg_row, taps, *core_params)
+    own_grad = out_grad.reshape(STEPS, sub, width)
+    mix_in, ssd, states, lse, og_full = mixer_fwd(
+        size, projected, step_raw, seg_row, taps, *core_params, own_grad
+    )
     inner_width = mamba_output.shape[0]
     hidden_width = ffn_gate.shape[1]
     rows16 = sds((*shape, width), bf16)
     rows32 = sds((STEPS, sub, width), f32)
     mixed = mix_in.shape[1]
-    half_shape = (size, STEPS // 2, sub, width)
     resid_grad, ffn_part, resid_two, dmix, grads, second_gain_grad = comm_call(
         functools.partial(ffn_kernel, size),
         (
@@ -1369,10 +1585,9 @@
             pltpu.VMEM(ffn_gate.shape, bf16),
             pltpu.VMEM(ffn_up.shape, bf16),
             pltpu.VMEM(ffn_down.shape, bf16),
-            pltpu.VMEM(half_shape, bf16),
-            pltpu.VMEM(half_shape, bf16),
+            pltpu.VMEM((*shape, width), bf16),
             pltpu.VMEM((width, 3 * hidden_width + mixed), bf16),
-            pltpu.SemaphoreType.DMA((6 + width // 256,)),
+            pltpu.SemaphoreType.DMA((5 + width // 256,)),
         ]
         + buffers
         + buffers,
@@ -1385,19 +1600,20 @@
         ffn_gate,
         ffn_up,
         ffn_down,
-        og_low.reshape(half_shape),
-        og_high.reshape(half_shape),
-        out_grad.reshape(STEPS, sub, width),
-        kept=(5, 6, 7, 8, 9),
+        og_full,
+        own_grad,
+        kept=(5, 6, 7, 8),
         given=(4,),
     )
     ffn_sum = lax.psum_scatter(
         ffn_part.reshape(length, width), "tp", scatter_dimension=0, tiled=True
     )
-    mid_sum = lax.psum_scatter(grads, "dp", scatter_dimension=0, tiled=True)
-    proj_grad, step_grad, dtaps, dheads, dgain, dskip = mixer_bwd(
+    blocks = lax.axis_size("dp")
+    grads = grads.reshape(blocks, width // blocks, grads.shape[1])
+    proj_grad, step_grad, dtaps, dheads, dgain, dskip, mid_sum = mixer_bwd(
         size, projected, step_raw, seg_row, taps, *core_params, mix_in, ssd, states, lse,
         dmix.reshape(length, mixed),
+        grads,
     )
     dp = lax.axis_size("dp")
     block = width // dp

time: 434 us -> 426 us (0.982)
  waiting for transfers between devices: 4.81 us -> 0.04 us
    pallas_call x3, Pallas kernels: 335 us -> 299 us  [comm_call(): pl.pallas_call(body, out_shape=out_shape, in_specs=[pl.BlockSpec(memory_s...]
    pallas_call x1, Pallas kernels: 24.4 us -> 47.9 us  [mixer_fwd(): pl.pallas_call(functools.partial(fwd_kernel, count), out_shape=(jax.Shape...]
    pallas_call x1, Pallas kernels: 43.8 us -> 54.4 us  [mixer_bwd(): pl.pallas_call(functools.partial(bwd_kernel, count, dp), out_shape=(jax.S...]
    all_gather x2 -> x0, waiting for transfers between devices: 4.42 us -> none  [the longest x1 4.4 us: shards(): og_high = lax.all_gather(og_high, 'tp', axis=0)]
  transfers between devices with their start and end apart: 4 -> 1, of which waited for: 1 -> 0; matrix products, arithmetic and copies ran while one was open for 0% -> 0% of each run, Pallas kernels for 64% -> 37%
where the time goes in v4:
time: 426 us; the launch traced here: 425 us
  Pallas kernels  408 us (96%)
  between operations  14.1 us (3%)
    pallas_call x3, Pallas kernels, comm_call(): pl.pallas_call(body, out_shape=out_shape, in_specs=[pl.BlockSpec(memory_s...  299 us
    pallas_call x1, Pallas kernels, mixer_bwd(): pl.pallas_call(functools.partial(bwd_kernel, count, dp), out_shape=(jax.S...  54.4 us
    pallas_call x1, Pallas kernels, mixer_fwd(): pl.pallas_call(functools.partial(fwd_kernel, count), out_shape=(jax.Shape...  47.9 us
  transfers between devices with their start and end apart: 1, of which 0 were waited for; matrix products, arithmetic and copies ran while one was open for 0% of the time, Pallas kernels for 37%

profile of v4, /device:TPU:0, one launch (start us, length us, event | category | flops | bytes accessed | tf_op | source)
XLA Modules:
  0.0 425.5 jit_solution(10141592075662508197)
XLA Ops:
  7.2 0.0 reduce-scatter.2.cloned.1.call-start
  7.2 0.7 convert_element_type.7
  7.9 0.9 reshape.107.keep_rows
  8.8 1.3 convert_element_type.8.seg
  10.1 73.8 %shard_map.450 = (f32[8,32,1024]{2,1,0:T(8,128)}, bf16[4,8,32,1024]{3,2,1,0:T(8,128)(2,1)}, bf16[4,8,32,2048]{3,2,1,0:T(8,128)(2,1)}, f32[4,8,32,8]{3,2,1,0:T(8,128)}) custom-call(bf16[4,8,32,2048]{3,2,1,0:T(8,128)(2,1)} %bitcast.28, bf16[2048,1024]{1,0:T(8,128)(2,1)} %embed_in.1, f32[8,32,1]{2,1,0:T(8,128)} %reshape.107.keep_rows, f32[1,1024]{1,0:T(1,128)} %bitcast.47, ...), custom_call_target="tpu_custom_call" | custom-call | tf_op jit(solution)/shard_map/pallas_call | solution.py:1097
  83.9 47.9 %shard_map.451 = (bf16[1024,768]{1,0:T(8,128)(2,1)}, bf16[1024,512]{1,0:T(8,128)(2,1)}, bf16[4,128,512]{2,1,0:T(8,128)(2,1)}, f32[8,1024]{1,0:T(8,128)}, bf16[4,8,32,1024]{3,2,1,0:T(8,128)(2,1)}) custom-call(bf16[1024,2048]{1,0:T(8,128)(2,1)} %bitcast.30, f32[1024,8]{1,0:T(8,128)} %bitcast.40, f32[1,1024]{1,0:T(1,128)} %convert_element_type.8.seg, ...), custom_call_target="tpu_custom_call" | custom-call | tf_op jit(solution)/shard_map/pallas_call | solution.py:752
  131.8 121.7 %shard_map.452 = (f32[8,32,1024]{2,1,0:T(8,128)}, bf16[4,8,32,1024]{3,2,1,0:T(8,128)(2,1)}, f32[8,32,1024]{2,1,0:T(8,128)}, bf16[4,8,32,768]{3,2,1,0:T(8,128)(2,...) custom-call(bf16[4,8,32,768]{3,2,1,0:T(8,128)(2,1)} %bitcast.33, bf16[512,1024]{1,0:T(8,128)(2,1)} %wmo.1, ...), custom_call_target="tpu_custom_call" | custom-call | tf_op jit(solution)/shard_map/pallas_call | solution.py:1097
  253.5 0.0 reduce-scatter.2.cloned.1.call-update
  253.6 54.4 %shard_map.453 = (bf16[1024,2048]{1,0:T(8,128)(2,1)}, bf16[1024,8]{1,0:T(8,128)(2,1)}, f32[4,768]{1,0:T(4,128)}, f32[2,8]{1,0:T(2,128)}, f32[1,512]{1,0:T(1,128)...) custom-call(bf16[1024,2048]{1,0:T(8,128)(2,1)} %bitcast.31, f32[1024,8]{1,0:T(8,128)} %bitcast.41, ...), custom_call_target="tpu_custom_call" | custom-call | tf_op jit(solution)/shard_map/pallas_call | solution.py:465
  308.0 103.0 %shard_map.454 = (bf16[4,8,32,2048]{3,2,1,0:T(8,128)(2,1)}, bf16[128,2048]{1,0:T(8,128)(2,1)}, bf16[128,2176]{1,0:T(8,128)(2,1)}, f32[16,1024]{1,0:T(8,128)}) custom-call(bf16[4,8,32,2048]{3,2,1,0:T(8,128)(2,1)} %bitcast.34, bf16[4,8,32,8]{3,2,1,0:T(8,128)(2,1)} %bitcast.44, bf16[1024,512]{1,0:T(8,128)(2,1)} %wz.1, bf16[1024,512]{1,0:T(8,128)(2,1)} %wx.1, ...), custom_call_target="tpu_custom_call" | custom-call | tf_op jit(solution)/shard_map/pallas_call | solution.py:1097
  411.0 0.0 reduce-scatter.2.cloned.1.call-done.ffn
  411.1 7.5 %shard_map.455 = (bf16[1024,2048]{1,0:T(8,128)(2,1)}, bf16[256,1024]{1,0:T(8,128)(2,1)}, f32[2048,128]{1,0:T(8,128)}, f32[128,512]{1,0:T(8,128)}, f32[128,512]{1...) custom-call(bf16[1024,2048]{1,0:T(8,128)(2,1)} %bitcast.35, ...), custom_call_target="tpu_custom_call" | custom-call | tf_op jit(solution)/shard_map/pallas_call | solution.py:1665
Async XLA Ops:
  7.2 403.9 %reduce-scatter.2.cloned.1.call-start = ((), (), s32[]{:S(2)}) async-start(), calls=%async_computation.1 | async-start | bytes 2621440 | tf_op jit(solution)/shard_map/reduce_scatter | solution.py:1608
Sparse Core Ops, SparseCore 0:
  253.7 43.9 reduce-scatter.1

commit v5 on v4

--- a/solution.py
+++ b/solution.py
@@ -722,10 +722,9 @@
 
     def chunk(index, _):
         def hook(k):
-            place = index * (HOOKS + 1) + k
-            turn = place * ring.turns // hooks
-
-            @pl.when((place + 1) * ring.turns // hooks > turn)
+            turn = index * (HOOKS + 1) + k - (hooks - ring.turns)
+
+            @pl.when(turn >= 0)
             def _():
                 ring.move(turn)
 

time: 426 us -> 425 us (level)
  no operation moved by 1% of the time
where the time goes in v5:
time: 425 us; the launch traced here: 424 us
  Pallas kernels  407 us (96%)
  between operations  14.1 us (3%)
    pallas_call x3, Pallas kernels, comm_call(): pl.pallas_call(body, out_shape=out_shape, in_specs=[pl.BlockSpec(memory_s...  301 us
    pallas_call x1, Pallas kernels, mixer_bwd(): pl.pallas_call(functools.partial(bwd_kernel, count, dp), out_shape=(jax.S...  54.1 us
    pallas_call x1, Pallas kernels, mixer_fwd(): pl.pallas_call(functools.partial(fwd_kernel, count), out_shape=(jax.Shape...  44.6 us
  transfers between devices with their start and end apart: 1, of which 0 were waited for; matrix products, arithmetic and copies ran while one was open for 0% of the time, Pallas kernels for 37%

profile of v5, /device:TPU:0, one launch (start us, length us, event | category | flops | bytes accessed | tf_op | source)
XLA Modules:
  0.0 424.3 jit_solution(329171826019871810)
XLA Ops:
  7.2 0.0 reduce-scatter.2.cloned.1.call-start
  7.2 0.7 convert_element_type.7
  7.9 0.9 reshape.107.keep_rows
  8.8 1.3 convert_element_type.8.seg
  10.1 73.8 %shard_map.450 = (f32[8,32,1024]{2,1,0:T(8,128)}, bf16[4,8,32,1024]{3,2,1,0:T(8,128)(2,1)}, bf16[4,8,32,2048]{3,2,1,0:T(8,128)(2,1)}, f32[4,8,32,8]{3,2,1,0:T(8,128)}) custom-call(bf16[4,8,32,2048]{3,2,1,0:T(8,128)(2,1)} %bitcast.28, bf16[2048,1024]{1,0:T(8,128)(2,1)} %embed_in.1, f32[8,32,1]{2,1,0:T(8,128)} %reshape.107.keep_rows, f32[1,1024]{1,0:T(1,128)} %bitcast.47, ...), custom_call_target="tpu_custom_call" | custom-call | tf_op jit(solution)/shard_map/pallas_call | solution.py:1096
  83.9 44.6 %shard_map.451 = (bf16[1024,768]{1,0:T(8,128)(2,1)}, bf16[1024,512]{1,0:T(8,128)(2,1)}, bf16[4,128,512]{2,1,0:T(8,128)(2,1)}, f32[8,1024]{1,0:T(8,128)}, bf16[4,8,32,1024]{3,2,1,0:T(8,128)(2,1)}) custom-call(bf16[1024,2048]{1,0:T(8,128)(2,1)} %bitcast.30, f32[1024,8]{1,0:T(8,128)} %bitcast.40, f32[1,1024]{1,0:T(1,128)} %convert_element_type.8.seg, ...), custom_call_target="tpu_custom_call" | custom-call | tf_op jit(solution)/shard_map/pallas_call | solution.py:751
  128.6 124.1 %shard_map.452 = (f32[8,32,1024]{2,1,0:T(8,128)}, bf16[4,8,32,1024]{3,2,1,0:T(8,128)(2,1)}, f32[8,32,1024]{2,1,0:T(8,128)}, bf16[4,8,32,768]{3,2,1,0:T(8,128)(2,...) custom-call(bf16[4,8,32,768]{3,2,1,0:T(8,128)(2,1)} %bitcast.33, bf16[512,1024]{1,0:T(8,128)(2,1)} %wmo.1, ...), custom_call_target="tpu_custom_call" | custom-call | tf_op jit(solution)/shard_map/pallas_call | solution.py:1096
  252.6 0.0 reduce-scatter.2.cloned.1.call-update
  252.7 54.1 %shard_map.453 = (bf16[1024,2048]{1,0:T(8,128)(2,1)}, bf16[1024,8]{1,0:T(8,128)(2,1)}, f32[4,768]{1,0:T(4,128)}, f32[2,8]{1,0:T(2,128)}, f32[1,512]{1,0:T(1,128)...) custom-call(bf16[1024,2048]{1,0:T(8,128)(2,1)} %bitcast.31, f32[1024,8]{1,0:T(8,128)} %bitcast.41, ...), custom_call_target="tpu_custom_call" | custom-call | tf_op jit(solution)/shard_map/pallas_call | solution.py:465
  306.8 103.0 %shard_map.454 = (bf16[4,8,32,2048]{3,2,1,0:T(8,128)(2,1)}, bf16[128,2048]{1,0:T(8,128)(2,1)}, bf16[128,2176]{1,0:T(8,128)(2,1)}, f32[16,1024]{1,0:T(8,128)}) custom-call(bf16[4,8,32,2048]{3,2,1,0:T(8,128)(2,1)} %bitcast.34, bf16[4,8,32,8]{3,2,1,0:T(8,128)(2,1)} %bitcast.44, bf16[1024,512]{1,0:T(8,128)(2,1)} %wz.1, bf16[1024,512]{1,0:T(8,128)(2,1)} %wx.1, ...), custom_call_target="tpu_custom_call" | custom-call | tf_op jit(solution)/shard_map/pallas_call | solution.py:1096
  409.9 0.0 reduce-scatter.2.cloned.1.call-done.ffn
  409.9 7.5 %shard_map.455 = (bf16[1024,2048]{1,0:T(8,128)(2,1)}, bf16[256,1024]{1,0:T(8,128)(2,1)}, f32[2048,128]{1,0:T(8,128)}, f32[128,512]{1,0:T(8,128)}, f32[128,512]{1...) custom-call(bf16[1024,2048]{1,0:T(8,128)(2,1)} %bitcast.35, ...), custom_call_target="tpu_custom_call" | custom-call | tf_op jit(solution)/shard_map/pallas_call | solution.py:1664
Async XLA Ops:
  7.2 402.7 %reduce-scatter.2.cloned.1.call-start = ((), (), s32[]{:S(2)}) async-start(), calls=%async_computation.1 | async-start | bytes 2621440 | tf_op jit(solution)/shard_map/reduce_scatter | solution.py:1607
Sparse Core Ops, SparseCore 0:
  252.8 43.6 reduce-scatter.1
